TPU v7x, 32 devices: a whole 2x2x4 slice. The times are simulated.
32 devices in a mesh: dp: 8 (over z, x), mp: 4 (over y, core).
Axes of the slice: x: 2, y: 2, z: 4, core: 2. Of those that a mesh axis runs over, the one named last changes fastest.
Arguments:
- slow_input: float32 [192, 196, 1024], P('dp', None, 'mp')
- fast_input: float32 [768, 196, 128], P('dp')
- clip_starts: int32 [24], replicated, may hold values from 0 to 191, as said below
- fast_reduce: float32 [128, 32], replicated, may hold values from -0.5 to 0.5
- fast_reduce_gain: float32 [32], replicated, may hold values from 0.1 to 1.9
- fast_reduce_bias: float32 [32], replicated, may hold values from -1.5 to 1.5
- fast_temporal: float32 [3, 32, 32], replicated, may hold values from -0.625 to 0.625
- fast_temporal_gain: float32 [32], replicated, may hold values from 0.1 to 1.9
- fast_temporal_bias: float32 [32], replicated, may hold values from -1.5 to 1.5
- fast_expand: float32 [32, 128], replicated, may hold values from -1 to 1
- fast_expand_gain: float32 [128], replicated, may hold values from 0.1 to 1.9
- fast_expand_bias: float32 [128], replicated, may hold values from -1.5 to 1.5
- lateral_conv: float32 [5, 128, 256], P(None, None, 'mp'), may hold values from -0.25 to 0.25
- lateral_gain: float32 [256], P('mp'), may hold values from 0.1 to 1.9
- lateral_bias: float32 [256], P('mp'), may hold values from -1.5 to 1.5
- slow_reduce: float32 [1280, 256], P(None, 'mp'), may hold values from -0.15625 to 0.15625
- slow_reduce_gain: float32 [256], P('mp'), may hold values from 0.1 to 1.9
- slow_reduce_bias: float32 [256], P('mp'), may hold values from -1.5 to 1.5
- slow_temporal: float32 [3, 256, 256], P(None, None, 'mp'), may hold values from -0.21875 to 0.21875
- slow_temporal_gain: float32 [256], P('mp'), may hold values from 0.1 to 1.9
- slow_temporal_bias: float32 [256], P('mp'), may hold values from -1.5 to 1.5
- slow_expand: float32 [256, 1024], P('mp'), may hold values from -0.375 to 0.375
- slow_expand_gain: float32 [1024], P('mp'), may hold values from 0.1 to 1.9
- slow_expand_bias: float32 [1024], P('mp'), may hold values from -1.5 to 1.5
- shortcut_conv: float32 [1280, 1024], P(None, 'mp'), may hold values from -0.15625 to 0.15625
- shortcut_gain: float32 [1024], P('mp'), may hold values from 0.1 to 1.9
- shortcut_bias: float32 [1024], P('mp'), may hold values from -1.5 to 1.5
- slow_cotangent: float32 [192, 196, 1024], P('dp', None, 'mp')
- fast_cotangent: float32 [768, 196, 128], P('dp')
Outputs:
- slow_output: float32 [192, 196, 1024], P('dp', None, 'mp')
- fast_output: float32 [768, 196, 128], P('dp')
- slow_input_gradient: float32 [192, 196, 1024], P('dp', None, 'mp')
- fast_input_gradient: float32 [768, 196, 128], P('dp')
- fast_reduce_gradient: float32 [128, 32], replicated
- fast_reduce_gain_gradient: float32 [32], replicated
- fast_reduce_bias_gradient: float32 [32], replicated
- fast_temporal_gradient: float32 [3, 32, 32], replicated
- fast_temporal_gain_gradient: float32 [32], replicated
- fast_temporal_bias_gradient: float32 [32], replicated
- fast_expand_gradient: float32 [32, 128], replicated
- fast_expand_gain_gradient: float32 [128], replicated
- fast_expand_bias_gradient: float32 [128], replicated
- lateral_conv_gradient: float32 [5, 128, 256], P(None, None, 'mp')
- lateral_gain_gradient: float32 [256], P('mp')
- lateral_bias_gradient: float32 [256], P('mp')
- slow_reduce_gradient: float32 [1280, 256], P(None, 'mp')
- slow_reduce_gain_gradient: float32 [256], P('mp')
- slow_reduce_bias_gradient: float32 [256], P('mp')
- slow_temporal_gradient: float32 [3, 256, 256], P(None, None, 'mp')
- slow_temporal_gain_gradient: float32 [256], P('mp')
- slow_temporal_bias_gradient: float32 [256], P('mp')
- slow_expand_gradient: float32 [256, 1024], P('mp')
- slow_expand_gain_gradient: float32 [1024], P('mp')
- slow_expand_bias_gradient: float32 [1024], P('mp')
- shortcut_conv_gradient: float32 [1280, 1024], P(None, 'mp')
- shortcut_gain_gradient: float32 [1024], P('mp')
- shortcut_bias_gradient: float32 [1024], P('mp')
Inputs may be any that keep to these rules, and one draw needn't show every extreme that they name: clip_starts[0] is 0; clip k from 1 to 22 starts at frame 8 * k plus 1 to 7; the last clip starts at 191; a clip runs up to the next start, the last one to the last frame.
All inputs are finite; a program needn't handle non-finite values.
Results may differ from a plain program's by a relative error of at most 0.0003.
Values sent between devices are 32-bit elements; how exact they have to be, the bound alone decides.
A program may use at most 384 MiB of HBM per device.

v0:
```python
import jax
import jax.numpy as jnp
from jax import lax
from jax.sharding import PartitionSpec as P

EPSILON = 1e-05
PRECISE = lax.Precision.HIGHEST


def with_halo(cells, sides, width):
    for axis, dim in sides:
        count = lax.axis_size(axis)
        ends = count - 1
        head = lax.slice_in_dim(cells, 0, width, axis=dim)
        tail = lax.slice_in_dim(cells, cells.shape[dim] - width, cells.shape[dim], axis=dim)
        cells = jnp.concatenate(
            [
                lax.ppermute(tail, axis, [(i, (i + 1) % count) for i in range(ends)]),
                cells,
                lax.ppermute(head, axis, [((i + 1) % count, i) for i in range(ends)]),
            ],
            axis=dim,
        )
    return cells


def passed_along(array, axis, by):
    count = lax.axis_size(axis)
    pairs = [(i, i + by) for i in range(count) if 0 <= i + by < count]
    return lax.ppermute(array, axis, pairs)


def product(former, latter):
    return jnp.dot(former, latter, precision=PRECISE, preferred_element_type=jnp.float32)


def contract(former, latter):
    return jnp.einsum(
        "fpc,fpo->co", former, latter, precision=PRECISE, preferred_element_type=jnp.float32
    )


def slope(before):
    sigmoid = jax.nn.sigmoid(before)
    return sigmoid * (1.0 + before * (1.0 - sigmoid))


def clip_ids(frame_at, starts):
    return jnp.sum((starts[None, :] <= frame_at[:, None]).astype(jnp.int32), axis=1) - 1


def tap_masks(frame_at, starts, offsets):
    own_clip = clip_ids(frame_at, starts)
    return jnp.stack(
        [
            (clip_ids(frame_at + offset, starts) == own_clip).astype(jnp.float32)
            for offset in offsets
        ],
        axis=1,
    )


def masked(mask_rows, column, tensor):
    return mask_rows[:, column][:, None, None] * tensor


def dp_sums(former, latter):
    return lax.psum((former, latter), "dp")


def norm_forward(tensor, gain_vector, bias_vector):
    number = tensor.shape[0] * tensor.shape[1] * lax.axis_size("dp")
    summed, squares = dp_sums(jnp.sum(tensor, axis=(0, 1)), jnp.sum(tensor * tensor, axis=(0, 1)))
    average = summed / number
    inverse = lax.rsqrt(squares / number - average * average + EPSILON)
    centred = (tensor - average) * inverse
    return (centred, inverse, centred * gain_vector + bias_vector)


def norm_backward(upstream, centred, inverse, gain_vector):
    number = upstream.shape[0] * upstream.shape[1] * lax.axis_size("dp")
    bias_change, gain_change = dp_sums(
        jnp.sum(upstream, axis=(0, 1)), jnp.sum(upstream * centred, axis=(0, 1))
    )
    adjusted = upstream - bias_change / number - centred * (gain_change / number)
    return (gain_vector * inverse * adjusted, gain_change, bias_change)


def pad_frames(tensor):
    return with_halo(tensor, (("dp", 0),), 1)


def pad_grads(tensor):
    return with_halo(tensor, (("dp", 0),), 1)


def widen_input(slow_local, side_local):
    return (
        lax.all_gather(slow_local, "mp", axis=2, tiled=True),
        lax.all_gather(side_local, "mp", axis=2, tiled=True),
    )


def widen_middle(tensor):
    return lax.all_gather(tensor, "mp", axis=2, tiled=True)


def narrow_middle(tensor):
    return lax.psum_scatter(tensor, "mp", scatter_dimension=2, tiled=True)


def temporal_forward(padded, weight, mask_rows):
    length = mask_rows.shape[0]
    summed = masked(mask_rows, 0, product(padded[0:length], weight[0]))
    for column in range(1, 3):
        summed = summed + masked(
            mask_rows, column, product(padded[column : column + length], weight[column])
        )
    return summed


def temporal_weight(padded, upstream, mask_rows):
    length = mask_rows.shape[0]
    return jnp.stack(
        [
            contract(padded[column : column + length], masked(mask_rows, column, upstream))
            for column in range(3)
        ],
        axis=0,
    )


def temporal_input(upstream_padded, weight, wide_masks, length):
    pieces = []
    for column in range(3):
        start_row = 2 - column
        weighted = masked(
            wide_masks[start_row : start_row + length],
            column,
            upstream_padded[start_row : start_row + length],
        )
        pieces.append(product(weighted, jnp.transpose(weight[column])))
    return pieces[0] + pieces[1] + pieces[2]


def lateral_taps(fast_local, rim_frames, speed_ratio):
    grid_shape = (fast_local.shape[0] // speed_ratio, speed_ratio) + fast_local.shape[1:]
    grouped = fast_local.reshape(grid_shape)
    earlier = jnp.concatenate([rim_frames, fast_local[:-2]], axis=0).reshape(grid_shape)
    return [earlier[:, 0], earlier[:, 1], grouped[:, 0], grouped[:, 1], grouped[:, 2]]


def lateral_untaps(tap_grads, speed_ratio):
    slow_count, pixels, channels = tap_grads[0].shape
    zero_block = jnp.zeros_like(tap_grads[0])
    grouped = jnp.stack(
        [tap_grads[2], tap_grads[3], tap_grads[4]] + [zero_block] * (speed_ratio - 3), axis=1
    )
    grouped = grouped.reshape(slow_count * speed_ratio, pixels, channels)
    earlier = jnp.stack([tap_grads[0], tap_grads[1]] + [zero_block] * (speed_ratio - 2), axis=1)
    earlier = earlier.reshape(slow_count * speed_ratio, pixels, channels)
    local_part = grouped + jnp.concatenate(
        [earlier[2:], jnp.zeros((2, pixels, channels), jnp.float32)], axis=0
    )
    return (local_part, earlier[:2])


def local(
    slow_input,
    fast_input,
    clip_starts,
    fast_reduce,
    fast_reduce_gain,
    fast_reduce_bias,
    fast_temporal,
    fast_temporal_gain,
    fast_temporal_bias,
    fast_expand,
    fast_expand_gain,
    fast_expand_bias,
    lateral_conv,
    lateral_gain,
    lateral_bias,
    slow_reduce,
    slow_reduce_gain,
    slow_reduce_bias,
    slow_temporal,
    slow_temporal_gain,
    slow_temporal_bias,
    slow_expand,
    slow_expand_gain,
    slow_expand_bias,
    shortcut_conv,
    shortcut_gain,
    shortcut_bias,
    slow_cotangent,
    fast_cotangent,
):
    slow_frames = slow_input.shape[0]
    fast_frames = fast_input.shape[0]
    speed_ratio = fast_frames // slow_frames
    device = lax.axis_index("dp")
    fast_starts = clip_starts * speed_ratio
    slow_masks = tap_masks(
        device * slow_frames + jnp.arange(-1, slow_frames + 1, dtype=jnp.int32),
        clip_starts,
        (-1, 0, 1),
    )
    fast_masks = tap_masks(
        device * fast_frames + jnp.arange(-1, fast_frames + 1, dtype=jnp.int32),
        fast_starts,
        (-1, 0, 1),
    )
    side_masks = tap_masks(
        (device * slow_frames + jnp.arange(slow_frames, dtype=jnp.int32)) * speed_ratio,
        fast_starts,
        (-2, -1, 0, 1, 2),
    )
    fast_first_linear = product(fast_input, fast_reduce)
    fast_first_centred, fast_first_inverse, fast_first_normed = norm_forward(
        fast_first_linear, fast_reduce_gain, fast_reduce_bias
    )
    fast_first_padded = pad_frames(jax.nn.silu(fast_first_normed))
    fast_middle_linear = temporal_forward(fast_first_padded, fast_temporal, fast_masks[1:-1])
    fast_middle_centred, fast_middle_inverse, fast_middle_normed = norm_forward(
        fast_middle_linear, fast_temporal_gain, fast_temporal_bias
    )
    fast_middle_active = jax.nn.silu(fast_middle_normed)
    fast_last_linear = product(fast_middle_active, fast_expand)
    fast_last_centred, fast_last_inverse, fast_last_normed = norm_forward(
        fast_last_linear, fast_expand_gain, fast_expand_bias
    )
    fast_joined = fast_last_normed + fast_input
    fast_output = jax.nn.silu(fast_joined)
    rim_frames = passed_along(fast_input[fast_frames - 2 :], "dp", 1)
    tap_inputs = lateral_taps(fast_input, rim_frames, speed_ratio)
    side_linear = masked(side_masks, 0, product(tap_inputs[0], lateral_conv[0]))
    for column in range(1, 5):
        side_linear = side_linear + masked(
            side_masks, column, product(tap_inputs[column], lateral_conv[column])
        )
    side_centred, side_inverse, side_normed = norm_forward(side_linear, lateral_gain, lateral_bias)
    side_active = jax.nn.silu(side_normed)
    slow_full, side_full = widen_input(slow_input, side_active)
    split_at = slow_full.shape[2]
    slow_first_linear = product(slow_full, slow_reduce[:split_at]) + product(
        side_full, slow_reduce[split_at:]
    )
    slow_first_centred, slow_first_inverse, slow_first_normed = norm_forward(
        slow_first_linear, slow_reduce_gain, slow_reduce_bias
    )
    slow_first_active = jax.nn.silu(slow_first_normed)
    slow_first_padded = pad_frames(widen_middle(slow_first_active))
    slow_middle_linear = temporal_forward(slow_first_padded, slow_temporal, slow_masks[1:-1])
    slow_middle_centred, slow_middle_inverse, slow_middle_normed = norm_forward(
        slow_middle_linear, slow_temporal_gain, slow_temporal_bias
    )
    slow_middle_active = jax.nn.silu(slow_middle_normed)
    slow_last_linear = lax.psum_scatter(
        product(slow_middle_active, slow_expand), "mp", scatter_dimension=2, tiled=True
    )
    slow_last_centred, slow_last_inverse, slow_last_normed = norm_forward(
        slow_last_linear, slow_expand_gain, slow_expand_bias
    )
    short_linear = product(slow_full, shortcut_conv[:split_at]) + product(
        side_full, shortcut_conv[split_at:]
    )
    short_centred, short_inverse, short_normed = norm_forward(
        short_linear, shortcut_gain, shortcut_bias
    )
    slow_joined = slow_last_normed + short_normed
    slow_output = jax.nn.silu(slow_joined)
    slow_upstream = slow_cotangent * slope(slow_joined)
    slow_last_grad, slow_expand_gain_gradient, slow_expand_bias_gradient = norm_backward(
        slow_upstream, slow_last_centred, slow_last_inverse, slow_expand_gain
    )
    short_grad, shortcut_gain_gradient, shortcut_bias_gradient = norm_backward(
        slow_upstream, short_centred, short_inverse, shortcut_gain
    )
    shortcut_change = jnp.concatenate(
        [contract(slow_full, short_grad), contract(side_full, short_grad)], axis=0
    )
    expand_upstream = lax.all_gather(slow_last_grad, "mp", axis=2, tiled=True)
    expand_change = contract(slow_middle_active, expand_upstream)
    middle_upstream = product(expand_upstream, jnp.transpose(slow_expand))
    slow_middle_grad, slow_temporal_gain_gradient, slow_temporal_bias_gradient = norm_backward(
        middle_upstream * slope(slow_middle_normed),
        slow_middle_centred,
        slow_middle_inverse,
        slow_temporal_gain,
    )
    temporal_change = temporal_weight(slow_first_padded, slow_middle_grad, slow_masks[1:-1])
    first_upstream = narrow_middle(
        temporal_input(pad_grads(slow_middle_grad), slow_temporal, slow_masks, slow_frames)
    )
    slow_first_grad, slow_reduce_gain_gradient, slow_reduce_bias_gradient = norm_backward(
        first_upstream * slope(slow_first_normed),
        slow_first_centred,
        slow_first_inverse,
        slow_reduce_gain,
    )
    reduce_change = jnp.concatenate(
        [contract(slow_full, slow_first_grad), contract(side_full, slow_first_grad)], axis=0
    )
    joined_slow = product(slow_first_grad, jnp.transpose(slow_reduce[:split_at])) + product(
        short_grad, jnp.transpose(shortcut_conv[:split_at])
    )
    joined_side = product(slow_first_grad, jnp.transpose(slow_reduce[split_at:])) + product(
        short_grad, jnp.transpose(shortcut_conv[split_at:])
    )
    slow_input_gradient, side_upstream = (
        lax.psum_scatter(joined_slow, "mp", scatter_dimension=2, tiled=True),
        lax.psum_scatter(joined_side, "mp", scatter_dimension=2, tiled=True),
    )
    side_grad, lateral_gain_gradient, lateral_bias_gradient = norm_backward(
        side_upstream * slope(side_normed), side_centred, side_inverse, lateral_gain
    )
    side_weighted = [masked(side_masks, column, side_grad) for column in range(5)]
    lateral_change = jnp.stack(
        [contract(tap_inputs[column], side_weighted[column]) for column in range(5)], axis=0
    )
    tap_grads = [
        product(side_weighted[column], jnp.transpose(lateral_conv[column])) for column in range(5)
    ]
    local_part, rim_part = lateral_untaps(tap_grads, speed_ratio)
    received = passed_along(rim_part, "dp", -1)
    zero_fill = jnp.zeros((fast_frames - 2,) + received.shape[1:], jnp.float32)
    side_fast = local_part + jnp.concatenate([zero_fill, received], axis=0)
    side_fast = lax.psum(side_fast, "mp")
    fast_upstream = fast_cotangent * slope(fast_joined)
    fast_last_grad, fast_expand_gain_gradient, fast_expand_bias_gradient = norm_backward(
        fast_upstream, fast_last_centred, fast_last_inverse, fast_expand_gain
    )
    fast_expand_change = contract(fast_middle_active, fast_last_grad)
    fast_middle_grad, fast_temporal_gain_gradient, fast_temporal_bias_gradient = norm_backward(
        product(fast_last_grad, jnp.transpose(fast_expand)) * slope(fast_middle_normed),
        fast_middle_centred,
        fast_middle_inverse,
        fast_temporal_gain,
    )
    fast_temporal_change = temporal_weight(fast_first_padded, fast_middle_grad, fast_masks[1:-1])
    fast_first_upstream = temporal_input(
        pad_grads(fast_middle_grad), fast_temporal, fast_masks, fast_frames
    )
    fast_first_grad, fast_reduce_gain_gradient, fast_reduce_bias_gradient = norm_backward(
        fast_first_upstream * slope(fast_first_normed),
        fast_first_centred,
        fast_first_inverse,
        fast_reduce_gain,
    )
    fast_reduce_change = contract(fast_input, fast_first_grad)
    fast_input_gradient = (
        fast_upstream + product(fast_first_grad, jnp.transpose(fast_reduce)) + side_fast
    )
    (
        fast_reduce_gradient,
        fast_temporal_gradient,
        fast_expand_gradient,
        lateral_conv_gradient,
        slow_reduce_gradient,
        slow_temporal_gradient,
        slow_expand_gradient,
        shortcut_conv_gradient,
    ) = lax.psum(
        (
            fast_reduce_change,
            fast_temporal_change,
            fast_expand_change,
            lateral_change,
            reduce_change,
            temporal_change,
            expand_change,
            shortcut_change,
        ),
        "dp",
    )
    return (
        slow_output,
        fast_output,
        slow_input_gradient,
        fast_input_gradient,
        fast_reduce_gradient,
        fast_reduce_gain_gradient,
        fast_reduce_bias_gradient,
        fast_temporal_gradient,
        fast_temporal_gain_gradient,
        fast_temporal_bias_gradient,
        fast_expand_gradient,
        fast_expand_gain_gradient,
        fast_expand_bias_gradient,
        lateral_conv_gradient,
        lateral_gain_gradient,
        lateral_bias_gradient,
        slow_reduce_gradient,
        slow_reduce_gain_gradient,
        slow_reduce_bias_gradient,
        slow_temporal_gradient,
        slow_temporal_gain_gradient,
        slow_temporal_bias_gradient,
        slow_expand_gradient,
        slow_expand_gain_gradient,
        slow_expand_bias_gradient,
        shortcut_conv_gradient,
        shortcut_gain_gradient,
        shortcut_bias_gradient,
    )


def solution(mesh):
    return jax.shard_map(
        local,
        mesh=mesh,
        in_specs=(
            P("dp", None, "mp"),
            P("dp", None, None),
            P(),
            P(),
            P(),
            P(),
            P(),
            P(),
            P(),
            P(),
            P(),
            P(),
            P(None, None, "mp"),
            P("mp"),
            P("mp"),
            P(None, "mp"),
            P("mp"),
            P("mp"),
            P(None, None, "mp"),
            P("mp"),
            P("mp"),
            P("mp", None),
            P("mp"),
            P("mp"),
            P(None, "mp"),
            P("mp"),
            P("mp"),
            P("dp", None, "mp"),
            P("dp", None, None),
        ),
        out_specs=(
            P("dp", None, "mp"),
            P("dp", None, None),
            P("dp", None, "mp"),
            P("dp", None, None),
            P(),
            P(),
            P(),
            P(),
            P(),
            P(),
            P(),
            P(),
            P(),
            P(None, None, "mp"),
            P("mp"),
            P("mp"),
            P(None, "mp"),
            P("mp"),
            P("mp"),
            P(None, None, "mp"),
            P("mp"),
            P("mp"),
            P("mp", None),
            P("mp"),
            P("mp"),
            P(None, "mp"),
            P("mp"),
            P("mp"),
        ),
        check_vma=False,
    )
```

profile of v0, /device:TPU:0, one launch (start us, length us, event | category | flops | bytes accessed | tf_op | source)
XLA Modules:
  0.0 1518.2 jit_solution(11619909862545429411)
XLA Ops:
  7.3 6.2 copy.294
  13.6 9.4 copy.295
  33.7 6.7 fusion.26
  40.4 6.4 fusion.24
  46.9 6.6 fusion.28
  53.7 9.0 pad_maximum_fusion
  62.7 9.7 copy.297
  77.2 5.9 fusion.225
  83.1 19.9 %all-reduce.9 = (f32[64]{0:T(128)S(1)}, f32[64]{0:T(128)S(1)}) all-reduce(f32[64]{0:T(128)S(1)} %get-tuple-element.226, f32[64]{0:T(128)S(1)} %get-tuple-element.225), channel_id=1, replica_groups=mesh['dp'=8,'mp'=4] {'dp'}, use_global_device_ids=true, to_apply=%region_10.0 | all-reduce | flops 128 | bytes 1024 | tf_op jit(solution)/shard_map/psum | solution.py:68
  106.1 23.5 %fusion.216 = (f32[32]{0:T(128)S(1)}, f32[32]{0:T(128)S(1)}, f32[96,196,32]{0,2,1:T(8,128)}) fusion(f32[96,196,128]{2,0,1:T(8,128)} %param.30, f32[128,32]{0,1:T(8,128)S(1)} %copy-done.40), kind=kOutput, calls=%fused_computation.341 | convolution fusion | flops 926650304 | bytes 12058880 | tf_op jit(solution)/shard_map/dot_general | solution.py:34
  129.6 11.1 all-gather.5.cloned.1.call-done
  140.7 22.9 %fusion.125 = f32[24,196,64]{1,2,0:T(8,128)S(1)} fusion(f32[24,196,1024]{2,1,0:T(8,128)} %all-gather.5.cloned.1.call-done, f32[1280,64]{0,1:T(8,128)} %param.44), kind=kOutput, calls=%fused_computation.185 | convolution fusion | flops 3699376128 | bytes 21127168 | tf_op jit(solution)/shard_map/dot_general | solution.py:34
  163.6 25.6 %all-gather.7.cloned.1.call-done = f32[24,196,256]{1,2,0:T(8,128)} async-done(((f32[24,196,64]{1,2,0:T(8,128)}), f32[24,196,256]{1,2,0:T(8,128)}) %all-gather.7.cloned.1.call-update) | async-done | bytes 4816912 | tf_op jit(solution)/shard_map/all_gather | solution.py:100
  189.3 6.8 fusion.224
  196.1 21.4 %all-reduce.8 = (f32[64]{0:T(128)S(1)}, f32[64]{0:T(128)S(1)}, f32[32]{0:T(128)S(1)}, f32[32]{0:T(128)S(1)}) all-reduce(f32[64]{0:T(128)S(1)} %get-tuple-element.224, f32[64]{0:T(128)S(1)} %get-tuple-element.223, f32[32]{0:T(128)S(1)} %get-tuple-element.208, f32[32]{0:T(128)S(1)} %get-tuple-element.207), channel_id=1, replica_groups=mesh['dp'=8,'mp'=4] {'dp'}, use_global_device_ids=true, to_apply=%region_14.0 | all-reduce | flops 192 | bytes 1536 | tf_op jit(solution)/shard_map/psum | solution.py:68
  247.9 14.7 all-gather.9.cloned.1.call-done
  269.8 6.2 fusion.135
  284.3 6.2 fusion.138
  290.6 5.7 fusion.223
  296.3 20.2 %all-reduce.7 = (f32[64]{0:T(128)S(1)}, f32[64]{0:T(128)S(1)}, f32[32]{0:T(128)}, f32[32]{0:T(128)}) all-reduce(f32[64]{0:T(128)S(1)} %get-tuple-element.222, f32[64]{0:T(128)S(1)} %get-tuple-element.221, f32[32]{0:T(128)S(1)} %get-tuple-element.214, f32[32]{0:T(128)S(1)} %get-tuple-element.213), channel_id=1, replica_groups=mesh['dp'=8,'mp'=4] {'dp'}, use_global_device_ids=true, to_apply=%region_19.20 | all-reduce | flops 192 | bytes 1536 | tf_op jit(solution)/shard_map/psum | solution.py:68
  317.0 20.1 %fusion.122 = f32[24,196,1024]{2,1,0:T(8,128)} fusion(f32[64,1024]{1,0:T(8,128)S(1)} %copy-done, f32[24,196,64]{1,2,0:T(8,128)} %get-tuple-element.336, f32[64]{0:T(128)S(1)} %copy-done.43, f32[64]{0:T(128)S(1)} %copy-done.42, f32[64]{0:T(128)S(1)} %get-tuple-element.307, f32[64]{0:T(128)S(1)} %get-tuple-element.323), kind=kOutput, calls=%fused_computation.182 | convolution fusion | flops 3701784576 | bytes 20734976 | tf_op jit(solution)/shard_map/dot_general | solution.py:34
  337.2 20.5 %fusion.102 = f32[24,196,256]{2,1,0:T(8,128)S(1)} fusion(f32[24,196,1024]{2,1,0:T(8,128)} %all-gather.5.cloned.1.call-done, f32[1280,256]{1,0:T(8,128)} %param.53), kind=kOutput, calls=%fused_computation.161 | convolution fusion | flops 14797504512 | bytes 25526272 | tf_op jit(solution)/shard_map/dot_general | solution.py:34
  357.7 16.2 %fusion.215 = (f32[256]{0:T(256)S(1)}, f32[256]{0:T(256)S(1)}, f32[24,196,256]{2,1,0:T(8,128)}) fusion(f32[24,196,256]{2,1,0:T(8,128)S(1)} %fusion.102, f32[24,196,256]{1,2,0:T(8,128)} %all-gather.7.cloned.1.call-done, f32[1280,256]{1,0:T(8,128)} %param.53), kind=kOutput, calls=%fused_computation.340 | convolution fusion | flops 3704192512 | bytes 16189440 | tf_op jit(solution)/shard_map/dot_general | solution.py:34
  374.5 18.9 %fusion.213 = (f32[128]{0:T(128)}, f32[128]{0:T(128)}, f32[96,196,128]{2,1,0:T(8,128)}) fusion(f32[32,128]{1,0:T(8,128)S(1)} %copy-done.106, f32[96,196,32]{1,2,0:T(8,128)S(1)} %copy-done.22, f32[32]{0:T(128)S(1)} %copy-done.107, f32[32]{0:T(128)S(1)} %copy-done.100, f32[32]{0:T(128)S(1)} %get-tuple-element.305, f32[32]{0:T(128)S(1)} %get-tuple-element.318), kind=kOutput, calls=%fused_computation.338 | convolution fusion | flops 936886016 | bytes 12060160 | tf_op jit(solution)/shard_map/dot_general | solution.py:34
  393.4 84.7 %reduce-scatter.5.cloned.1.call-done = f32[24,196,256]{2,1,0:T(8,128)} async-done(((f32[24,196,1024]{2,1,0:T(8,128)}), f32[24,196,256]{2,1,0:T(8,128)}) %reduce-scatter.5.cloned.1.call-update) | async-done | bytes 4816912 | tf_op jit(solution)/shard_map/reduce_scatter | solution.py:259
  481.2 22.5 %all-reduce.6 = (f32[256]{0:T(256)}, f32[256]{0:T(256)}, f32[256]{0:T(256)}, f32[256]{0:T(256)}, f32[128]{0:T(128)}, /*index=5*/f32[128]{0:T(128)}) all-reduce(f32[256]{0:T(256)S(1)} %get-tuple-element.206, f32[256]{0:T(256)S(1)} %get-tuple-element.205, f32[256]{0:T(256)S(1)} %get-tuple-element.204, ...), channel_id=1, replica_groups=mesh['dp'=8,'mp'=4] {'dp'}, use_global_device_ids=true, to_apply=%region_28.29 | all-reduce | flops 1280 | bytes 10240 | tf_op jit(solution)/shard_map/psum | solution.py:68
  507.6 26.2 %fusion.212 = (f32[128]{0:T(128)}, f32[128]{0:T(128)}, f32[96,196,128]{2,1,0:T(8,128)}, f32[96,196,128]{2,1,0:T(8,128)}) fusion(f32[128]{0:T(128)S(1)} %get-tuple-element.309, f32[96,196,128]{2,1,0:T(8,128)} %get-tuple-element.339, f32[128]{0:T(128)S(1)} %get-tuple-element.324, f32[96,196,128]{2,0,1:T(8,128)} %param.30, f32[128]{0:T(128)} %param.40, ...), kind=kLoop, calls=%fused_computation.337 | loop fusion | flops 40943360 | bytes 48172032 | tf_op jit(solution)/shard_map/reduce_sum | solution.py:83
  533.9 7.2 multiply_reduce_fusion.3
  541.0 17.8 %all-reduce.5 = (f32[256]{0:T(256)}, f32[256]{0:T(256)}, f32[128]{0:T(128)}, f32[128]{0:T(128)}) all-reduce(f32[256]{0:T(256)} %get-tuple-element.202, f32[256]{0:T(256)S(1)} %get-tuple-element.200, f32[128]{0:T(128)} %get-tuple-element.197, f32[128]{0:T(128)} %get-tuple-element.196), channel_id=1, replica_groups=mesh['dp'=8,'mp'=4] {'dp'}, use_global_device_ids=true, to_apply=%region_45.46 | all-reduce | flops 768 | bytes 6144 | tf_op jit(solution)/shard_map/psum | solution.py:68
  560.2 7.0 subtract_multiply_fusion.3
  569.2 28.8 %fusion.218 = (f32[32]{0:T(128)}, f32[32]{0:T(128)}, f32[96,196,32]{1,2,0:T(8,128)}) fusion(f32[32]{0:T(128)S(1)} %copy-done.83, f32[96,196,32]{1,2,0:T(8,128)} %get-tuple-element.337, f32[32]{0:T(128)S(1)} %copy-done.86, f32[32]{0:T(128)} %param.37, f32[32]{0:T(128)} %param.36, f32[32,128]{1,0:T(8,128)} %param.38, ...), kind=kOutput, calls=%fused_computation.343 | convolution fusion | flops 948326336 | bytes 24104192 | tf_op jit(solution)/shard_map/dot_general | solution.py:34
  598.0 91.5 %all-gather.11.cloned.1.call-done = f32[24,196,1024]{2,1,0:T(8,128)} async-done(((f32[24,196,256]{2,1,0:T(8,128)}), f32[24,196,1024]{2,1,0:T(8,128)}) %all-gather.11.cloned.1.call-update) | async-done | bytes 19267600 | tf_op jit(solution)/shard_map/all_gather | solution.py:283
  689.5 25.4 %fusion.222 = (f32[64]{0:T(128)S(1)}, f32[64]{0:T(128)S(1)}, f32[24,196,64]{1,2,0:T(8,128)}) fusion(f32[64]{0:T(128)S(1)} %get-tuple-element.307, f32[24,196,64]{1,2,0:T(8,128)} %get-tuple-element.336, f32[64]{0:T(128)S(1)} %get-tuple-element.323, f32[64]{0:T(128)S(1)} %copy-done.43, f32[64]{0:T(128)S(1)} %copy-done.42, ...), kind=kOutput, calls=%fused_computation.347 | convolution fusion | flops 3703891968 | bytes 21939712 | tf_op jit(solution)/shard_map/dot_general | solution.py:34
  715.0 22.0 %all-reduce.4 = (f32[64]{0:T(128)S(1)}, f32[64]{0:T(128)S(1)}, f32[32]{0:T(128)}, f32[32]{0:T(128)}) all-reduce(f32[64]{0:T(128)S(1)} %get-tuple-element.220, f32[64]{0:T(128)S(1)} %get-tuple-element.219, f32[32]{0:T(128)} %get-tuple-element.212, f32[32]{0:T(128)} %get-tuple-element.211), channel_id=1, replica_groups=mesh['dp'=8,'mp'=4] {'dp'}, use_global_device_ids=true, to_apply=%region_51.52 | all-reduce | flops 192 | bytes 1536 | tf_op jit(solution)/shard_map/psum | solution.py:68
  756.4 7.9 add_add_fusion.2
  782.7 6.6 fusion.217
  789.4 29.8 %reduce-scatter.7.cloned.1.call-done = f32[24,196,64]{1,2,0:T(8,128)} async-done(((f32[24,196,256]{1,2,0:T(8,128)}), f32[24,196,64]{1,2,0:T(8,128)}) %reduce-scatter.7.cloned.1.call-update) | async-done | bytes 1204240 | tf_op jit(solution)/shard_map/reduce_scatter | solution.py:109
  823.3 21.5 %all-reduce.3 = (f32[256]{0:T(256)S(1)}, f32[64]{0:T(128)S(1)}, f32[64]{0:T(128)S(1)}, f32[32]{0:T(128)S(1)}, f32[32]{0:T(128)S(1)}) all-reduce(f32[256]{0:T(256)S(1)} %copy-done.64, f32[64]{0:T(128)S(1)} %get-tuple-element.218, f32[64]{0:T(128)S(1)} %get-tuple-element.217, ...), channel_id=1, replica_groups=mesh['dp'=8,'mp'=4] {'dp'}, use_global_device_ids=true, to_apply=%region_58.59 | all-reduce | flops 448 | bytes 3584 | tf_op jit(solution)/shard_map/psum | solution.py:68
  849.9 7.2 fusion.118
  858.7 8.1 convolution_add_fusion.1
  867.6 15.7 %fusion.93 = f32[32,128]{1,0:T(8,128)S(1)} fusion(f32[96,196,128]{2,1,0:T(8,128)} %get-tuple-element.279, f32[96,196,128]{2,1,0:T(8,128)} %get-tuple-element.339, f32[128]{0:T(128)S(1)} %copy-done.120, f32[128]{0:T(128)S(1)} %copy-done.122, f32[128]{0:T(128)S(1)} %copy-done.103, f32[128]{0:T(128)S(1)} %copy-done.90, f32[128]{0:T(128)S(1)} %copy-done.92, ...), kind=kOutput, calls=%fused_computation.154 | convolution fusion | flops 944111616 | bytes 21695488 | tf_op jit(solution)/shard_map/fpc,fpo->co/dot_general | solution.py:38
  892.2 6.0 convolution_bitcast_fusion.9
  898.2 5.9 fusion.61
  904.1 5.9 fusion.64
  910.7 18.8 %convolution_bitcast_fusion.7 = f32[64,1024]{1,0:T(8,128)} fusion(f32[24,196,1024]{2,1,0:T(8,128)} %all-gather.11.cloned.1.call-done, f32[24,196,64]{1,2,0:T(8,128)S(1)} %copy-done.10, f32[64]{0:T(128)S(1)} %copy-done.43, f32[64]{0:T(128)S(1)} %copy-done.42, f32[64]{0:T(128)S(1)} %get-tuple-element.307, f32[64]{0:T(128)S(1)} %get-tuple-element.323), kind=kOutput, calls=%fused_computation.138 | convolution fusion | flops 3701784576 | bytes 20734976 | tf_op jit(solution)/shard_map/fpc,fpo->co/dot_general | solution.py:38
  929.5 8.0 convolution_bitcast_fusion.10
  937.6 13.7 convolution_bitcast_fusion.8
  952.1 15.5 %convolution_bitcast_fusion.6 = f32[256,256]{0,1:T(8,128)S(1)} fusion(f32[24,196,256]{1,2,0:T(8,128)} %all-gather.7.cloned.1.call-done, f32[24,196,256]{2,1,0:T(8,128)} %copy-done.2), kind=kOutput, calls=%fused_computation.137 | convolution fusion | flops 3699376128 | bytes 9895936 | tf_op jit(solution)/shard_map/fpc,fpo->co/dot_general | solution.py:38
  967.6 18.1 %convolution_bitcast_fusion.5 = f32[1024,256]{0,1:T(8,128)S(1)} fusion(f32[24,196,256]{2,1,0:T(8,128)S(1)} %bitcast.319, f32[24,196,1024]{2,1,0:T(8,128)S(1)} %bitcast.316), kind=kOutput, calls=%fused_computation.135 | convolution fusion | flops 14797504512 | bytes 25133056 | tf_op jit(solution)/shard_map/fpc,fpo->co/dot_general | solution.py:38
  986.9 14.8 convolution_bitcast_fusion.12
  1006.0 34.5 %all-reduce.2 = (f32[64]{0:T(128)S(1)}, f32[64]{0:T(128)S(1)}, f32[128,32]{0,1:T(8,128)}, f32[3,32,32]{2,1,0:T(8,128)}, f32[32,128]{1,0:T(8,128)}) all-reduce(f32[64]{0:T(128)S(1)} %get-tuple-element.216, f32[64]{0:T(128)S(1)} %get-tuple-element.215, ...), channel_id=1, replica_groups=mesh['dp'=8,'mp'=4] {'dp'}, use_global_device_ids=true, to_apply=%region_76.77 | all-reduce | flops 11392 | bytes 91136 | tf_op jit(solution)/shard_map/psum | solution.py:68
  1042.4 5.6 fusion.88
  1090.1 6.3 maximum_maximum_fusion
  1105.9 9.4 fusion
  1116.6 18.9 %fusion.100 = f32[24,196,1024]{2,1,0:T(8,128)S(1)} fusion(f32[24,196,256]{2,1,0:T(8,128)} %copy-done.2, f32[1280,256]{1,0:T(8,128)S(1)} %copy-done.26), kind=kOutput, calls=%fused_computation.159 | convolution fusion | flops 14797504512 | bytes 25133056 | tf_op jit(solution)/shard_map/dot_general | solution.py:34
  1135.6 19.5 %convolution_add_fusion = f32[24,196,1024]{2,1,0:T(8,128)} fusion(f32[24,196,1024]{2,1,0:T(8,128)S(1)} %fusion.100, f32[24,196,64]{1,2,0:T(8,128)S(1)} %copy-done.16, f32[1280,64]{0,1:T(8,128)S(1)} %copy-done.27), kind=kOutput, calls=%fused_computation.14 | convolution fusion | flops 3704193024 | bytes 40763392 | tf_op jit(solution)/shard_map/dot_general | solution.py:34
  1155.1 6.2 copy.323
  1161.3 9.6 copy.324
  1171.0 18.4 %fusion.181 = f32[96,196,128]{2,1,0:T(8,128)} fusion(f32[128,32]{0,1:T(8,128)S(1)} %copy-done.41, f32[96,196,32]{1,2,0:T(8,128)S(1)} %copy-done.23, f32[96,196,32]{1,2,0:T(8,128)S(1)} %copy-done.13, f32[32]{0:T(128)S(1)} %broadcast_multiply_fusion.8, f32[32]{0:T(128)S(1)} %broadcast_multiply_fusion.9, f32[32]{0:T(128)S(1)} %copy-done.56, ...), kind=kOutput, calls=%fused_computation.247 | convolution fusion | flops 928456704 | bytes 14467712 | tf_op jit(solution)/shard_map/dot_general | solution.py:34
  1192.2 161.7 %all-reduce.14.cloned.1.call-done = f32[96,196,128]{2,1,0:T(8,128)} async-done(((f32[96,196,128]{2,1,0:T(8,128)}), f32[96,196,128]{2,1,0:T(8,128)}) %all-reduce.14.cloned.1.call-update) | async-done | bytes 9633808 | tf_op jit(solution)/shard_map/psum | solution.py:329
  1353.9 11.0 add_add_fusion
  1364.9 7.6 copy.326
  1372.5 128.8 %reduce-scatter.9.cloned.1.call-done = f32[24,196,256]{2,1,0:T(8,128)} async-done(((f32[24,196,1024]{2,1,0:T(8,128)}), f32[24,196,256]{2,1,0:T(8,128)}) %reduce-scatter.9.cloned.1.call-update) | async-done | bytes 4816912 | tf_op jit(solution)/shard_map/reduce_scatter | solution.py:312
  1501.4 6.2 copy.325
  (439 shorter events, 201.1 us)
Async XLA Ops:
  7.2 309.8 %copy-start = (f32[64,1024]{1,0:T(8,128)S(1)}, f32[64,1024]{1,0:T(8,128)}, u32[]{:S(2)}) copy-start(f32[64,1024]{1,0:T(8,128)} %param.50) | copy-start | bytes 786436
  7.2 133.5 %all-gather.5.cloned.1.call-start = ((), (), s32[]{:S(2)}) async-start(), calls=%async_computation.4 | async-start | bytes 24576000 | tf_op jit(solution)/shard_map/all_gather | solution.py:99
  13.5 175.8 %all-gather.7.cloned.1.call-start = ((), (), s32[]{:S(2)}) async-start(), calls=%async_computation.5 | async-start | bytes 7864320 | tf_op jit(solution)/shard_map/all_gather | solution.py:100
  28.4 25.2 %collective-permute-start = (f32[2,196,128]{2,1,0:T(8,128)S(1)}, f32[2,196,128]{2,1,0:T(8,128)S(1)}, u32[]{:S(2)}, u32[]{:S(2)}) collective-permute-start(f32[2,196,128]{2,1,0:T(8,128)S(1)} %slice.267), channel_id=1, source_target_pairs={{0,4},{4,8},{8,12},{12,16},{16,20},{20,24},{24,28},{1,5},{5,9},{9,... | collective-permute-start | bytes 602120 | tf_op jit(solution)/shard_map/ppermute | solution.py:30
  53.6 23.6 %copy-start.44 = (f32[24]{0:T(128)}, f32[24]{0:T(128)S(1)}, u32[]{:S(2)}) copy-start(f32[24]{0:T(128)S(1)} %get-tuple-element.331) | copy-start | bytes 292
  53.6 23.6 %copy-start.46 = (f32[24]{0:T(128)}, f32[24]{0:T(128)S(1)}, u32[]{:S(2)}) copy-start(f32[24]{0:T(128)S(1)} %get-tuple-element.332) | copy-start | bytes 292
  53.6 23.6 %copy-start.48 = (f32[24]{0:T(128)}, f32[24]{0:T(128)S(1)}, u32[]{:S(2)}) copy-start(f32[24]{0:T(128)S(1)} %get-tuple-element.329) | copy-start | bytes 292
  77.2 25.8 %copy-start.58 = (f32[64]{0:T(128)S(1)}, f32[64]{0:T(128)}, u32[]{:S(2)}) copy-start(f32[64]{0:T(128)} %param.42) | copy-start | bytes 772
  77.2 26.9 %copy-start.80 = (f32[64]{0:T(128)S(1)}, f32[64]{0:T(128)}, u32[]{:S(2)}) copy-start(f32[64]{0:T(128)} %param.43) | copy-start | bytes 772
  83.1 46.5 %copy-start.20 = (f32[24,196,64]{1,2,0:T(8,128)}, f32[24,196,64]{1,2,0:T(8,128)S(1)}, u32[]{:S(2)}) copy-start(f32[24,196,64]{1,2,0:T(8,128)S(1)} %get-tuple-element.333) | copy-start | bytes 3612676
  105.9 156.7 %all-gather.9.cloned.1.call-start = ((), (), s32[]{:S(2)}) async-start(), calls=%async_computation.6 | async-start | bytes 7864320 | tf_op jit(solution)/shard_map/all_gather | solution.py:105
  163.6 53.8 %copy-start.57 = (f32[64]{0:T(128)S(1)}, f32[64]{0:T(128)}, u32[]{:S(2)}) copy-start(f32[64]{0:T(128)} %param.45) | copy-start | bytes 772
  163.6 54.4 %copy-start.78 = (f32[64]{0:T(128)S(1)}, f32[64]{0:T(128)}, u32[]{:S(2)}) copy-start(f32[64]{0:T(128)} %param.46) | copy-start | bytes 772
  196.1 28.8 %copy-start.18 = (f32[24,196,64]{1,2,0:T(8,128)}, f32[24,196,64]{1,2,0:T(8,128)S(1)}, u32[]{:S(2)}) copy-start(f32[24,196,64]{1,2,0:T(8,128)S(1)} %get-tuple-element.334) | copy-start | bytes 3612676
  219.7 258.5 %reduce-scatter.5.cloned.1.call-start = ((), (), s32[]{:S(2)}) async-start(), calls=%async_computation.7 | async-start | bytes 24576000 | tf_op jit(solution)/shard_map/reduce_scatter | solution.py:259
  230.8 11.6 collective-permute-start.4
  232.1 7.4 collective-permute-start.3
  263.6 26.9 %collective-permute-start.2 = (f32[1,196,256]{1,2,0:T(8,128)S(1)}, f32[1,196,256]{1,2,0:T(8,128)S(1)}, u32[]{:S(2)}, u32[]{:S(2)}) collective-permute-start(f32[1,196,256]{1,2,0:T(8,128)S(1)} %get-tuple-element.283), channel_id=1, source_target_pairs={{4,0},{8,4},{12,8},{16,12},{20,16},{24,20},{28,24},{5,1},{9,5},{13... | collective-permute-start | bytes 602120 | tf_op jit(solution)/shard_map/ppermute | solution.py:20
  264.9 14.6 collective-permute-start.1
  290.5 25.9 %copy-start.42 = (f32[64]{0:T(128)S(1)}, f32[64]{0:T(128)}, u32[]{:S(2)}) copy-start(f32[64]{0:T(128)} %param.48) | copy-start | bytes 772
  290.6 26.4 %copy-start.43 = (f32[64]{0:T(128)S(1)}, f32[64]{0:T(128)}, u32[]{:S(2)}) copy-start(f32[64]{0:T(128)} %param.49) | copy-start | bytes 772
  337.1 352.4 %all-gather.11.cloned.1.call-start = ((), (), s32[]{:S(2)}) async-start(), calls=%async_computation.8 | async-start | bytes 24576000 | tf_op jit(solution)/shard_map/all_gather | solution.py:283
  393.4 110.3 %copy-start.66 = (f32[256]{0:T(256)S(1)}, f32[256]{0:T(256)}, u32[]{:S(2)}) copy-start(f32[256]{0:T(256)} %param.54) | copy-start | bytes 3076
  506.2 27.6 %copy-start.89 = (f32[128]{0:T(128)}, f32[128]{0:T(128)S(1)}, u32[]{:S(2)}) copy-start(f32[128]{0:T(128)S(1)} %get-tuple-element.309) | copy-start | bytes 1540
  506.2 27.6 %copy-start.91 = (f32[128]{0:T(128)}, f32[128]{0:T(128)S(1)}, u32[]{:S(2)}) copy-start(f32[128]{0:T(128)S(1)} %get-tuple-element.324) | copy-start | bytes 1540
  507.5 26.3 %slice-start.14 = ((s8[4915200]{0:T(1024)(128)(4,1)}), s8[4194304]{0:T(1024)(128)(4,1)S(1)}, s32[]{:S(2)}) async-start(s8[4915200]{0:T(1024)(128)(4,1)} %bitcast.332), calls=%async_computation.28 | async-start | bytes 8388608
  507.5 26.3 %slice-start.16 = ((s8[4915200]{0:T(1024)(128)(4,1)}), s8[4194304]{0:T(1024)(128)(4,1)S(1)}, s32[]{:S(2)}) async-start(s8[4915200]{0:T(1024)(128)(4,1)} %bitcast.334), calls=%async_computation.30 | async-start | bytes 8388608
  507.5 26.3 %slice-start.20 = ((s8[4816896]{0:T(1024)(128)(4,1)}), s8[4194304]{0:T(1024)(128)(4,1)S(1)}, s32[]{:S(2)}) async-start(s8[4816896]{0:T(1024)(128)(4,1)} %bitcast.344), calls=%async_computation.34 | async-start | bytes 8388608
  507.5 26.3 %slice-start.15 = ((s8[4915200]{0:T(1024)(128)(4,1)}), s8[720896]{0:T(1024)(128)(4,1)S(1)}, s32[]{:S(2)}) async-start(s8[4915200]{0:T(1024)(128)(4,1)} %bitcast.332), calls=%async_computation.29 | async-start | bytes 1441792
  507.5 26.3 %slice-start.17 = ((s8[4915200]{0:T(1024)(128)(4,1)}), s8[720896]{0:T(1024)(128)(4,1)S(1)}, s32[]{:S(2)}) async-start(s8[4915200]{0:T(1024)(128)(4,1)} %bitcast.334), calls=%async_computation.31 | async-start | bytes 1441792
  507.5 26.3 %slice-start.21 = ((s8[4816896]{0:T(1024)(128)(4,1)}), s8[622592]{0:T(1024)(128)(4,1)S(1)}, s32[]{:S(2)}) async-start(s8[4816896]{0:T(1024)(128)(4,1)} %bitcast.344), calls=%async_computation.35 | async-start | bytes 1245184
  507.5 26.3 %copy-start.65 = (f32[256]{0:T(256)S(1)}, f32[256]{0:T(256)}, u32[]{:S(2)}) copy-start(f32[256]{0:T(256)} %param.51) | copy-start | bytes 3076
  507.5 26.3 %copy-start.67 = (f32[256]{0:T(256)S(1)}, f32[256]{0:T(256)}, u32[]{:S(2)}) copy-start(f32[256]{0:T(256)} %param.54) | copy-start | bytes 3076
  507.5 26.3 %copy-start.93 = (f32[256]{0:T(256)S(1)}, f32[256]{0:T(256)}, u32[]{:S(2)}) copy-start(f32[256]{0:T(256)} %param.55) | copy-start | bytes 3076
  507.6 26.3 %copy-start.94 = (f32[256]{0:T(256)S(1)}, f32[256]{0:T(256)}, u32[]{:S(2)}) copy-start(f32[256]{0:T(256)} %param.52) | copy-start | bytes 3076
  567.2 252.0 %reduce-scatter.7.cloned.1.call-start = ((), (), s32[]{:S(2)}) async-start(), calls=%async_computation.9 | async-start | bytes 7864320 | tf_op jit(solution)/shard_map/reduce_scatter | solution.py:109
  714.9 26.0 %copy-start.29 = (f32[3,256,64]{1,2,0:T(8,128)S(1)}, f32[3,256,64]{1,2,0:T(8,128)}, u32[]{:S(2)}) copy-start(f32[3,256,64]{1,2,0:T(8,128)} %param.47) | copy-start | bytes 589828
  739.4 11.7 collective-permute-start.5
  746.3 10.1 collective-permute-start.6
  764.4 237.3 %reduce-scatter.11.cloned.1.call-start = ((), (), s32[]{:S(2)}) async-start(), calls=%async_computation.11 | async-start | bytes 7864320 | tf_op jit(solution)/shard_map/reduce_scatter | solution.py:313
  770.2 9.3 collective-permute-start.7
  774.9 7.7 collective-permute-start.8
  782.7 36.5 %copy-start.79 = (f32[64]{0:T(128)S(1)}, f32[64]{0:T(128)}, u32[]{:S(2)}) copy-start(f32[64]{0:T(128)} %param.46) | copy-start | bytes 772
  789.4 33.9 %copy-start.64 = (f32[256]{0:T(256)S(1)}, f32[256]{0:T(256)}, u32[]{:S(2)}) copy-start(f32[256]{0:T(256)} %get-tuple-element.201) | copy-start | bytes 3076
  789.4 55.6 %copy-start.68 = (f32[256]{0:T(256)S(1)}, f32[256]{0:T(256)}, u32[]{:S(2)}) copy-start(f32[256]{0:T(256)} %get-tuple-element.293) | copy-start | bytes 3076
  844.9 84.6 %copy-start.115 = (f32[32]{0:T(128)}, f32[32]{0:T(128)S(1)}, u32[]{:S(2)}) copy-start(f32[32]{0:T(128)S(1)} %get-tuple-element.414) | copy-start | bytes 388
  844.9 84.6 %copy-start.116 = (f32[32]{0:T(128)}, f32[32]{0:T(128)S(1)}, u32[]{:S(2)}) copy-start(f32[32]{0:T(128)S(1)} %get-tuple-element.415) | copy-start | bytes 388
  866.9 322.5 %all-reduce.16.cloned.1.call-start = ((), (), s32[]{:S(2)}) async-start(), calls=%async_computation.13 | async-start | bytes 4521984 | tf_op jit(solution)/shard_map/psum | solution.py:364
  904.1 33.4 %slice-start = ((s8[19660800]{0:T(1024)(128)(4,1)}), s8[4194304]{0:T(1024)(128)(4,1)S(1)}, s32[]{:S(2)}) async-start(s8[19660800]{0:T(1024)(128)(4,1)} %bitcast.315), calls=%async_computation.14 | async-start | bytes 8388608
  904.1 33.4 %slice-start.1 = ((s8[19660800]{0:T(1024)(128)(4,1)}), s8[4194304]{0:T(1024)(128)(4,1)S(1)}, s32[]{:S(2)}) async-start(s8[19660800]{0:T(1024)(128)(4,1)} %bitcast.315), calls=%async_computation.15 | async-start | bytes 8388608
  910.7 26.9 %slice-start.2 = ((s8[19660800]{0:T(1024)(128)(4,1)}), s8[4194304]{0:T(1024)(128)(4,1)S(1)}, s32[]{:S(2)}) async-start(s8[19660800]{0:T(1024)(128)(4,1)} %bitcast.315), calls=%async_computation.16 | async-start | bytes 8388608
  910.7 26.9 %slice-start.3 = ((s8[19660800]{0:T(1024)(128)(4,1)}), s8[4194304]{0:T(1024)(128)(4,1)S(1)}, s32[]{:S(2)}) async-start(s8[19660800]{0:T(1024)(128)(4,1)} %bitcast.315), calls=%async_computation.17 | async-start | bytes 8388608
  1001.7 38.8 %copy-start.21 = (f32[24,196,64]{1,2,0:T(8,128)S(1)}, f32[24,196,64]{1,2,0:T(8,128)}, u32[]{:S(2)}) copy-start(f32[24,196,64]{1,2,0:T(8,128)} %copy-done.20) | copy-start | bytes 3612676
  1001.7 38.8 %copy-start.72 = (f32[64]{0:T(128)S(1)}, f32[64]{0:T(128)}, u32[]{:S(2)}) copy-start(f32[64]{0:T(128)} %get-tuple-element.297) | copy-start | bytes 772
  1001.8 46.3 %copy-start.51 = (f32[24]{0:T(128)S(1)}, f32[24]{0:T(128)}, u32[]{:S(2)}) copy-start(f32[24]{0:T(128)} %copy-done.50) | copy-start | bytes 292
  1006.0 36.5 %copy-start.49 = (f32[24]{0:T(128)S(1)}, f32[24]{0:T(128)}, u32[]{:S(2)}) copy-start(f32[24]{0:T(128)} %copy-done.48) | copy-start | bytes 292
  1068.9 285.0 %all-reduce.14.cloned.1.call-start = ((), (), s32[]{:S(2)}) async-start(), calls=%async_computation.12 | async-start | bytes 19660800 | tf_op jit(solution)/shard_map/psum | solution.py:329
  1074.4 31.5 %collective-permute-start.9 = (f32[2,196,128]{2,1,0:T(8,128)S(1)}, f32[2,196,128]{2,1,0:T(8,128)S(1)}, u32[]{:S(2)}, u32[]{:S(2)}) collective-permute-start(f32[2,196,128]{2,1,0:T(8,128)S(1)} %slice.282), channel_id=1, source_target_pairs={{4,0},{8,4},{12,8},{16,12},{20,16},{24,20},{28,24},{5,1},{9,5},{13... | collective-permute-start | bytes 602120 | tf_op jit(solution)/shard_map/ppermute | solution.py:30
  1115.3 386.0 %reduce-scatter.9.cloned.1.call-start = ((), (), s32[]{:S(2)}) async-start(), calls=%async_computation.10 | async-start | bytes 24576000 | tf_op jit(solution)/shard_map/reduce_scatter | solution.py:312
  1372.5 135.1 %copy-start.69 = (f32[256]{0:T(256)S(1)}, f32[256]{0:T(256)}, u32[]{:S(2)}) copy-start(f32[256]{0:T(256)} %get-tuple-element.433) | copy-start | bytes 3076
  1372.5 135.6 %copy-start.36 = (f32[5,128,64]{1,2,0:T(8,128)S(1)}, f32[5,128,64]{1,2,0:T(8,128)}, u32[]{:S(2)}) copy-start(f32[5,128,64]{1,2,0:T(8,128)} %get-tuple-element.422) | copy-start | bytes 491524
  1372.5 136.3 %copy-start.32 = (f32[1280,64]{0,1:T(8,128)S(1)}, f32[1280,64]{0,1:T(8,128)}, u32[]{:S(2)}) copy-start(f32[1280,64]{0,1:T(8,128)} %get-tuple-element.425) | copy-start | bytes 983044
  1372.5 137.0 %copy-start.35 = (f32[3,256,64]{1,2,0:T(8,128)S(1)}, f32[3,256,64]{1,2,0:T(8,128)}, u32[]{:S(2)}) copy-start(f32[3,256,64]{1,2,0:T(8,128)} %get-tuple-element.428) | copy-start | bytes 589828
  1372.5 137.7 %copy-start.33 = (f32[64,1024]{1,0:T(8,128)S(1)}, f32[64,1024]{1,0:T(8,128)}, u32[]{:S(2)}) copy-start(f32[64,1024]{1,0:T(8,128)} %get-tuple-element.431) | copy-start | bytes 786436
  (101 other events, 944.8 us)
Sparse Core Ops, SparseCore 0:
  13.6 127.0 all-gather.4
  142.8 46.3 all-gather.6
  219.8 42.6 all-gather.8
  337.2 140.8 reduce-scatter.4
  567.4 122.1 all-gather.10
  764.5 54.6 reduce-scatter.6
  867.0 54.6 reduce-scatter.10
  1069.0 107.2 all-reduce.15
  1178.8 175.0 all-reduce.13
  1356.6 144.7 reduce-scatter.8
where the time goes:
time: 1530 us; the launch traced here: 1520 us
  waiting for transfers between devices  552 us (36%)
  matrix products  521 us (34%)
  blocking collectives  180 us (12%)
  other arithmetic  121 us (8%)
  local copies, waits for them, and re-layouts  96 us (6%)
  starting transfers between devices  32.1 us (2%)
  between operations  16.9 us (1%)
    dot_general x36, matrix products, product(): jnp.dot(former, latter, precision=PRECISE, preferred_element_type=jnp.flo...  370 us
    psum x8, blocking collectives, dp_sums(): return lax.psum((former, latter), 'dp')  180 us
    psum x1, waiting for transfers between devices, local(): side_fast = lax.psum(side_fast, 'mp')  162 us
    dot_general x18, matrix products, contract(): jnp.einsum('fpc,fpo->co', former, latter, precision=PRECISE, preferred_el...  151 us
    reduce_scatter x1, waiting for transfers between devices, local(): lax.psum_scatter(joined_slow, 'mp', scatter_dimension=2, tiled=True)  129 us
    all_gather x1, waiting for transfers between devices, local(): expand_upstream = lax.all_gather(slow_last_grad, 'mp', axis=2, tiled=True)  91.5 us
    reduce_scatter x1, waiting for transfers between devices, local(): lax.psum_scatter(product(slow_middle_active, slow_expand), 'mp', scatter_...  84.7 us
    unnamed x304, local copies, waits for them, and re-layouts  67.1 us
  transfers between devices with their start and end apart: 20, of which 9 were waited for; matrix products, arithmetic and copies ran while one was open for 35% of the time, Pallas kernels for 0%

commit v1 on v0

v1 whole, which is shorter than its diff:
```python
import functools

import jax
import jax.numpy as jnp
from jax import lax
from jax.experimental import pallas as pl
from jax.experimental.pallas import tpu as pltpu
from jax.sharding import Mesh, PartitionSpec as P

EPSILON = 1e-05
F32 = jnp.float32
BF16 = jnp.bfloat16
MESH = pl.DeviceIdType.MESH
LIMIT = 58 * 1024 * 1024
ROLE = ("yy", "hh")
ALL = ("dp", "yy", "hh")


def split(v):
    high = v.astype(BF16)
    return high, (v - high.astype(F32)).astype(BF16)


def dot(a, b, ca, cb):
    return lax.dot_general(a, b, (((ca,), (cb,)), ((), ())), preferred_element_type=F32)


def dot3(a, b, ca=1, cb=0):
    (ah, al), (bh, bl) = a, b
    return dot(ah, bh, ca, cb) + dot(ah, bl, ca, cb) + dot(al, bh, ca, cb)


def sigmoid(v):
    return 0.5 * jnp.tanh(0.5 * v) + 0.5


def silu(v):
    return v * sigmoid(v)


def slope(v):
    s = sigmoid(v)
    return s * (1.0 + v * (1.0 - s))


def colsum(v):
    return jnp.sum(v, axis=0, keepdims=True)


def moments(total, squares, number):
    mean = total * (1.0 / number)
    return mean, lax.rsqrt(squares * (1.0 / number) - mean * mean + EPSILON)


def back_terms(gain, mean, inverse, up, upz, number):
    alpha = gain * inverse
    beta = -alpha * inverse * (upz * inverse) * (1.0 / number)
    return alpha, beta, -alpha * up * (1.0 / number) - beta * mean


def fold32(v):
    return v + pltpu.roll(v, 32, 1) + pltpu.roll(v, 64, 1) + pltpu.roll(v, 96, 1)


def fold128(v):
    return v[:, 0:128] + v[:, 128:256] + v[:, 256:384] + v[:, 384:512]


def four(v):
    return jnp.concatenate([v, v, v, v], axis=1)


def rows_of(ref, g):
    pixels, count, lanes = ref.shape
    return ref[:, pl.ds(g, count // 4, stride=4), :].reshape(pixels * (count // 4), lanes)


def frames_of(ref):
    return jnp.concatenate([rows_of(ref, g) for g in range(4)], axis=1)


def masked(v, mask):
    frames = mask.shape[0]
    lanes = v.shape[1] // mask.shape[1]
    wide = mask[...] if lanes == 1 else jnp.concatenate([mask[...]] * lanes, axis=1)
    return (v.reshape(-1, frames, v.shape[1]) * wide[None]).reshape(v.shape)


def edge(ref, v, at, frames):
    rows = v.shape[0]
    parts = []
    for k in range(v.shape[1] // 128):
        ref[k] = v[:, 128 * k : 128 * (k + 1)]
        parts.append(ref[k, pl.ds(at, rows // frames, stride=frames), :])
    return jnp.concatenate(parts, axis=1)


def edges(ref, v, frames):
    rows = v.shape[0]
    first, last = [], []
    for k in range(v.shape[1] // 128):
        ref[k] = v[:, 128 * k : 128 * (k + 1)]
        first.append(ref[k, pl.ds(0, rows // frames, stride=frames), :])
        last.append(ref[k, pl.ds(frames - 1, rows // frames, stride=frames), :])
    return jnp.concatenate(first, axis=1), jnp.concatenate(last, axis=1)


def shifted(ref, v, step, frames, beyond):
    rows = v.shape[0]
    at = 0 if step == 1 else frames - 1
    parts = []
    for k in range(v.shape[1] // 128):
        lanes = slice(128 * k, 128 * (k + 1))
        ref[k] = pltpu.roll(v[:, lanes], 1 if step == 1 else rows - 1, 0)
        ref[k, pl.ds(at, rows // frames, stride=frames), :] = beyond[:, lanes]
        parts.append(ref[k])
    return jnp.concatenate(parts, axis=1)


def add_rows(ref, *rows):
    @pl.when(pl.program_id(0) == 0)
    def _():
        ref[...] = jnp.zeros_like(ref)

    for k, row in enumerate(rows):
        ref[k : k + 1, :] += row


def add_whole(ref, value):
    @pl.when(pl.program_id(0) == 0)
    def _():
        ref[...] = jnp.zeros_like(ref)

    ref[...] += value


def vmem():
    return pl.BlockSpec(memory_space=pltpu.VMEM)


def shape(*dims, dtype=F32):
    return jax.ShapeDtypeStruct(dims, dtype)


def cost(flops, nbytes):
    return pl.CostEstimate(flops=int(2 * flops), bytes_accessed=int(2 * nbytes), transcendentals=0)


def whole(x):
    rank = len(x.shape)
    return pl.BlockSpec(tuple(x.shape), lambda i, *s: (0,) * rank)


def part(x, rows, at=None):
    tail = (0,) * (len(x.shape) - 1)
    where = at or (lambda i, *s: i)
    return pl.BlockSpec((rows,) + tuple(x.shape[1:]), lambda i, *s: (where(i, *s),) + tail)


def stepped(body, name, steps, scalars, ins, outs, scratch=(), est=None):
    return pl.pallas_call(
        body,
        name=name,
        out_shape=[o for o, _ in outs],
        grid_spec=pltpu.PrefetchScalarGridSpec(
            num_scalar_prefetch=len(scalars),
            grid=(steps,),
            in_specs=[s for _, s in ins],
            out_specs=[s for _, s in outs],
            scratch_shapes=list(scratch),
        ),
        compiler_params=pltpu.CompilerParams(vmem_limit_bytes=LIMIT),
        cost_estimate=est,
    )(*scalars, *[a for a, _ in ins])


def sum_kernel(sizes, axes, widths, edges, *refs):
    dps, ys, hs = sizes
    roles = ys * hs if axes == ROLE else hs
    parts = len(widths)
    xs, refs = refs[:parts], refs[parts:]
    edge_in, refs = refs[:edges], refs[edges:]
    outs, refs = refs[:parts], refs[parts:]
    edge_out, refs = refs[:edges], refs[edges:]
    one_src, two_src, b1, b2, s1, r1, s2, r2 = refs[:8]
    d = lax.axis_index("dp")
    y = lax.axis_index("yy")
    h = lax.axis_index("hh")
    m = y * hs + h

    def role(i):
        if axes != ROLE:
            return {"hh": lax.rem(h + i, hs)}
        p = lax.rem(m + i, roles)
        return {"yy": p // hs, "hh": lax.rem(p, hs)}

    def along(i):
        return {"dp": lax.rem(d + i, dps)}

    def send(src, dst, ssem, rsem, to):
        c = pltpu.make_async_remote_copy(
            src_ref=src, dst_ref=dst, send_sem=ssem, recv_sem=rsem, device_id=to, device_id_type=MESH
        )
        c.start()
        return c

    bar = pltpu.get_barrier_semaphore()
    for i in range(1, roles):
        pl.semaphore_signal(bar, inc=1, device_id=role(i), device_id_type=MESH)
    for i in range(1, dps):
        pl.semaphore_signal(bar, inc=1, device_id=along(i), device_id_type=MESH)
    one_src[...] = jnp.zeros_like(one_src)
    start = 0
    for x, width in zip(xs, widths):
        one_src[start : start + x.shape[0], 0:width] = x[...]
        start += x.shape[0]
    pl.semaphore_wait(bar, roles + dps - 2)
    one = [send(one_src, b1.at[i - 1], s1.at[i - 1], r1.at[i - 1], role(i)) for i in range(1, roles)]
    rim = []
    if edges:
        s3, r3 = refs[8:]
        rim = [
            send(edge_in[k], edge_out[k], s3.at[k], r3.at[k], along(1 if k == 0 else dps - 1))
            for k in range(edges)
        ]
    acc = one_src[...]
    for i, c in enumerate(one):
        c.wait_recv()
        acc = acc + b1[i]
    two_src[...] = acc
    two = [send(two_src, b2.at[i - 1], s2.at[i - 1], r2.at[i - 1], along(i)) for i in range(1, dps)]
    for i, c in enumerate(two):
        c.wait_recv()
        acc = acc + b2[i]
    start = 0
    for o, width in zip(outs, widths):
        o[...] = acc[start : start + o.shape[0], 0:width]
        start += o.shape[0]
    for c in rim:
        c.wait_recv()
    for c in one + rim + two:
        c.wait_send()


def total(xs, cid, sizes, axes, rims=()):
    dps, ys, hs = sizes
    roles = ys * hs if axes == ROLE else hs
    widths = [x.shape[1] for x in xs]
    packed = (sum(x.shape[0] for x in xs), max(widths))
    dma = pltpu.SemaphoreType.DMA
    return pl.pallas_call(
        functools.partial(sum_kernel, sizes, axes, widths, len(rims)),
        name="sum%d" % cid,
        out_shape=[shape(*x.shape) for x in xs] + [shape(*r.shape) for r in rims],
        in_specs=[vmem()] * (len(xs) + len(rims)),
        out_specs=[vmem()] * (len(xs) + len(rims)),
        scratch_shapes=[
            pltpu.VMEM(packed, F32),
            pltpu.VMEM(packed, F32),
            pltpu.VMEM((roles - 1,) + packed, F32),
            pltpu.VMEM((dps - 1,) + packed, F32),
            dma((roles - 1,)), dma((roles - 1,)), dma((dps - 1,)), dma((dps - 1,)),
        ] + ([dma((2,)), dma((2,))] if rims else []),
        compiler_params=pltpu.CompilerParams(collective_id=cid, has_side_effects=True),
    )(*xs, *rims)


def fast1_kernel(frames, idx, x_ref, rh, rl, p_ref, e0, e1, st, tmp):
    p = dot3(split(frames_of(x_ref)), (rh[...], rl[...]))
    p_ref[...] = p
    e0[0], e1[0] = edges(tmp, p, frames)
    add_rows(st, colsum(p), colsum(p * p))


def lateral_taps(frames, mask, x_ref, halo, bz):
    x = [rows_of(x_ref, g) for g in range(4)]
    beyond = jnp.concatenate([halo[:, 6, :], halo[:, 7, :]], axis=1)
    early = shifted(bz, jnp.concatenate([x[2], x[3]], axis=1), 1, frames, beyond)
    return jnp.concatenate([masked(early, mask), x[0], x[1], x[2]], axis=1)


def lateral_kernel(frames, idx, mask, x_ref, halo, wh, wl, s_ref, e0, st, bz):
    p = dot3(split(lateral_taps(frames, mask, x_ref, halo, bz)), (wh[...], wl[...]), 1, 1)
    s_ref[...] = p
    e0[0] = edge(bz, p, 0, frames)
    add_rows(st, colsum(p), colsum(p * p))


def fast_norm(tot, number):
    return moments(fold32(tot[0:1, :]), fold32(tot[1:2, :]), number)


def wide_norm(tot, number):
    return moments(fold128(tot[0:1, :]), fold128(tot[1:2, :]), number)


def rims_of(v, prev, nxt):
    lane = lax.broadcasted_iota(jnp.int32, v.shape, 1)
    return jnp.where(lane >= 96, prev, jnp.where(lane < 32, nxt, 0.0))


def fast2_kernel(
    number, frames, mp, mn, tot, gain, bias, p1, before, after, wh, wl, a_ref, z_ref, p2, st, zp, zn
):
    mean, inverse = fast_norm(tot, number)
    scale = gain[...] * inverse
    shift = bias[...] - mean * scale
    a = silu(p1[...] * scale + shift)
    a_ref[...] = a
    prev = shifted(zp, a, 1, frames, silu(before[0] * scale + shift))
    nxt = shifted(zn, a, -1, frames, silu(after[0] * scale + shift))
    z = rims_of(a, masked(prev, mp), masked(nxt, mn))
    z_ref[...] = z
    p = dot3(split(jnp.concatenate([a, z], axis=1)), (wh[...], wl[...]))
    p2[...] = p
    add_rows(st, colsum(p), colsum(p * p))


def fast3_kernel(number, tot, gain, bias, p2, eh, el, b_ref, st):
    mean, inverse = fast_norm(tot, number)
    scale = gain[...] * inverse
    b = silu(p2[...] * scale + (bias[...] - mean * scale))
    b_ref[...] = b
    p = dot3(split(b), (eh[...], el[...]))
    add_rows(st, colsum(p), colsum(p * p))


def put_frames(ref, v):
    pixels, count, lanes = ref.shape
    for g in range(4):
        ref[:, pl.ds(g, count // 4, stride=4), :] = v[:, lanes * g : lanes * (g + 1)].reshape(
            pixels, count // 4, lanes
        )


def fast4_kernel(number, share, idx, tot, gain, bias, x_ref, c_ref, b_ref, eh, el, o_ref, f_ref, u_ref, st):
    mean, inverse = wide_norm(tot, number)
    scale = gain[...] * inverse
    shift = bias[...] - mean * scale
    p = dot3(split(b_ref[...]), (eh[...], el[...]))
    j = p * four(scale) + four(shift) + frames_of(x_ref)
    s = sigmoid(j)
    out = j * s
    put_frames(o_ref, out)
    put_frames(f_ref, out)
    u = frames_of(c_ref) * (s * (1.0 + j * (1.0 - s)))
    u_ref[...] = u
    add_rows(st, share * colsum(u), share * colsum(u * (p - four(mean))))


def fast5_kernel(
    number, frames, tot, back, gain, tot2, gain2, bias2, u_ref, b_ref, p2, eh, el, u2, eg, e0, e1, st, tmp
):
    mean, inverse = wide_norm(tot, number)
    alpha, beta, gamma = back_terms(
        gain[...], mean, inverse, fold128(back[0:1, :]), fold128(back[1:2, :]), number
    )
    bs = split(b_ref[...])
    e = (eh[...], el[...])
    g = split(four(alpha) * u_ref[...] + four(beta) * dot3(bs, e) + four(gamma))
    add_whole(eg, dot3(bs, g, 0, 0))
    v = dot3(g, e, 1, 1)
    mean2, inverse2 = fast_norm(tot2, number)
    z = p2[...] - mean2
    u = v * slope(z * (inverse2 * gain2[...]) + bias2[...])
    u2[...] = u
    e0[0, 0], e1[0, 0] = edges(tmp, u, frames)
    e0[0, 1], e1[0, 1] = edges(tmp, p2[...], frames)
    add_rows(st, colsum(u), colsum(u * z))


def fast6_kernel(
    number, frames, mp, mn, tot2, back2, gain2, tot1, gain1, bias1, u2, p2, before, after, a, z, p1,
    wh, wl, u1, tg, st, zp, zn
):
    mean2, inverse2 = fast_norm(tot2, number)
    alpha, beta, gamma = back_terms(
        gain2[...], mean2, inverse2, fold32(back2[0:1, :]), fold32(back2[1:2, :]), number
    )
    g = alpha * u2[...] + beta * p2[...] + gamma
    prev = shifted(zp, g, 1, frames, alpha * before[0, 0] + beta * before[0, 1] + gamma)
    nxt = shifted(zn, g, -1, frames, alpha * after[0, 0] + beta * after[0, 1] + gamma)
    gz = rims_of(g, masked(prev, mp), masked(nxt, mn))
    add_whole(tg, dot3(split(jnp.concatenate([a[...], z[...]], axis=1)), split(g), 0, 0))
    v = dot3(split(jnp.concatenate([g, gz], axis=1)), (wh[...], wl[...]), 1, 1)
    mean1, inverse1 = fast_norm(tot1, number)
    c = p1[...] - mean1
    u = v * slope(c * (gain1[...] * inverse1) + bias1[...])
    u1[...] = u
    add_rows(st, colsum(u), colsum(u * c))


def fast7_kernel(number, idx, tot1, back1, gain1, x_ref, u1, p1, g1, rg):
    mean, inverse = fast_norm(tot1, number)
    alpha, beta, gamma = back_terms(
        gain1[...], mean, inverse, fold32(back1[0:1, :]), fold32(back1[1:2, :]), number
    )
    g = alpha * u1[...] + beta * p1[...] + gamma
    g1[...] = g
    add_whole(rg, dot3(split(frames_of(x_ref)), split(g), 0, 0))


def slow1_kernel(
    number, frames, idx, tot, gain, bias, x0, x1, x2, x3, side, rh, rl, sh, sl,
    first, short, jh, jl, e0, e1, st, wide, tmp
):
    lanes = x0.shape[1]
    for r, x in enumerate((x0, x1, x2, x3)):
        at = pl.multiple_of(idx[3 + r] * lanes, lanes)
        wide[:, pl.ds(at, lanes)] = x[...]
    mean, inverse = moments(tot[0:1, :], tot[1:2, :], number)
    scale = gain[...] * inverse
    top = sh.shape[0] * lanes
    wide[:, top:] = silu(side[...] * scale + (bias[...] - mean * scale))
    joined = split(wide[...])
    jh[0], jl[0] = joined
    p = dot3(joined, (rh[...], rl[...]), 1, 1)
    first[...] = p
    e0[0], e1[0] = edges(tmp, p, frames)
    sums = [colsum(p)]
    squares = [colsum(p * p)]
    for n in range(sh.shape[0]):
        p = dot3(joined, (sh[n], sl[n]))
        short[:, n * lanes : (n + 1) * lanes] = p
        sums.append(colsum(p))
        squares.append(colsum(p * p))
    add_rows(st, jnp.concatenate(sums, axis=1), jnp.concatenate(squares, axis=1))


def slow2_kernel(
    number, frames, mp, mn, tot, gain, bias, first, before, after, wh, wl, th, tl, pm, st, zp, zn
):
    width = gain.shape[1]
    mean, inverse = moments(tot[0:1, 0:width], tot[1:2, 0:width], number)
    scale = gain[...] * inverse
    shift = bias[...] - mean * scale
    a = silu(first[...] * scale + shift)
    prev = shifted(zp, a, 1, frames, silu(before[0] * scale + shift))
    nxt = shifted(zn, a, -1, frames, silu(after[0] * scale + shift))
    taps = split(jnp.concatenate([masked(prev, mp), a, masked(nxt, mn)], axis=1))
    th[0], tl[0] = taps
    p = dot3(taps, (wh[...], wl[...]), 1, 1)
    pm[...] = p
    add_rows(st, colsum(p), colsum(p * p))


def slow3_kernel(number, tot, gain, bias, pm, eh, el, bh, bl, st):
    mean, inverse = moments(tot[0:1, :], tot[1:2, :], number)
    scale = gain[...] * inverse
    b = split(silu(pm[...] * scale + (bias[...] - mean * scale)))
    bh[0], bl[0] = b
    p = dot3(b, (eh[...], el[...]))
    add_rows(st, colsum(p), colsum(p * p))


def slow4_kernel(
    number, idx, tot_l, tot_s, gain_l, bias_l, gain_s, bias_s, bh, bl, short, c0, c1, c2, c3, eh, el,
    o0, o1, o2, o3, u_ref, st, wide
):
    lanes = c0.shape[1]
    for r, c in enumerate((c0, c1, c2, c3)):
        at = pl.multiple_of(idx[3 + r] * lanes, lanes)
        wide[:, pl.ds(at, lanes)] = c[...]
    off = tot_s.shape[1] - short.shape[1]
    bs = (bh[0], bl[0])
    sums = []
    for n in range(short.shape[1] // lanes):
        at = slice(n * lanes, (n + 1) * lanes)
        mean_l, inv_l = moments(tot_l[0:1, at], tot_l[1:2, at], number)
        far = slice(off + n * lanes, off + (n + 1) * lanes)
        mean_s, inv_s = moments(tot_s[0:1, far], tot_s[1:2, far], number)
        zl = dot3(bs, (eh[:, at], el[:, at])) - mean_l
        zs = short[:, at] - mean_s
        j = zl * (inv_l * gain_l[:, at]) + zs * (inv_s * gain_s[:, at]) + (bias_l[:, at] + bias_s[:, at])
        s = sigmoid(j)
        u = wide[:, at] * (s * (1.0 + j * (1.0 - s)))
        u_ref[:, at] = u
        sums.append((colsum(u), colsum(u * zl), colsum(u * zs)))
        wide[:, at] = j * s
    for r, o in enumerate((o0, o1, o2, o3)):
        at = pl.multiple_of(idx[3 + r] * lanes, lanes)
        o[...] = wide[:, pl.ds(at, lanes)]
    add_rows(st, *[jnp.concatenate(rows, axis=1) for rows in zip(*sums)])


def slow5_kernel(
    number, frames, tot_l, back, gain_l, tot_m, gain_m, bias_m, u_ref, bh, bl, pm, eh, el,
    um, eg, e0, e1, st, tmp
):
    mean, inverse = moments(tot_l[0:1, :], tot_l[1:2, :], number)
    alpha, beta, gamma = back_terms(gain_l[...], mean, inverse, back[0:1, :], back[1:2, :], number)
    bs = (bh[0], bl[0])
    e = (eh[...], el[...])
    g = split(alpha * u_ref[...] + beta * dot3(bs, e) + gamma)
    add_whole(eg, dot3(bs, g, 0, 0))
    v = dot3(g, e, 1, 1)
    mean_m, inv_m = moments(tot_m[0:1, :], tot_m[1:2, :], number)
    z = pm[...] - mean_m
    u = v * slope(z * (inv_m * gain_m[...]) + bias_m[...])
    um[...] = u
    e0[0, 0], e1[0, 0] = edges(tmp, u, frames)
    e0[0, 1], e1[0, 1] = edges(tmp, pm[...], frames)
    add_rows(st, colsum(u), colsum(u * z))


def slow6_kernel(number, tot_s, back, gain_s, u_ref, short, jh, jl, sh, sl, dx, grads):
    off = tot_s.shape[1] - short.shape[1]
    mean, inverse = moments(tot_s[0:1, off:], tot_s[1:2, off:], number)
    alpha, beta, gamma = back_terms(gain_s[...], mean, inverse, back[0:1, :], back[2:3, :], number)
    lanes = sh.shape[2]
    joined = (jh[0], jl[0])

    @pl.when(pl.program_id(0) == 0)
    def _():
        grads[...] = jnp.zeros_like(grads)

    out = None
    for n in range(sh.shape[0]):
        at = slice(n * lanes, (n + 1) * lanes)
        g = split(alpha[:, at] * u_ref[:, at] + beta[:, at] * short[:, at] + gamma[:, at])
        grads[n] += dot3(joined, g, 0, 0)
        part = dot3(g, (sh[n], sl[n]), 1, 1)
        out = part if out is None else out + part
    dx[...] = out


def slow7_kernel(
    number, frames, mp, mn, tot_m, back, gain_m, tot_f, gain_f, bias_f, um, pm, before, after, th, tl,
    first, wh, wl, uf, tg, st, zp, zn
):
    mean, inverse = moments(tot_m[0:1, :], tot_m[1:2, :], number)
    alpha, beta, gamma = back_terms(gain_m[...], mean, inverse, back[0:1, :], back[1:2, :], number)
    g = alpha * um[...] + beta * pm[...] + gamma
    prev = shifted(zp, g, 1, frames, alpha * before[0, 0] + beta * before[0, 1] + gamma)
    nxt = shifted(zn, g, -1, frames, alpha * after[0, 0] + beta * after[0, 1] + gamma)
    gs = split(g)
    add_whole(tg, dot3(gs, (th[0], tl[0]), 0, 0))
    width = gain_f.shape[1]
    v = dot3(split(masked(nxt, mn)), (wh[:, 0:width], wl[:, 0:width]))
    v += dot3(gs, (wh[:, width : 2 * width], wl[:, width : 2 * width]))
    v += dot3(split(masked(prev, mp)), (wh[:, 2 * width :], wl[:, 2 * width :]))
    mean_f, inv_f = moments(tot_f[0:1, 0:width], tot_f[1:2, 0:width], number)
    z = first[...] - mean_f
    u = v * slope(z * (gain_f[...] * inv_f) + bias_f[...])
    uf[...] = u
    add_rows(st, colsum(u), colsum(u * z))


def slow8_kernel(
    number, frames, idx, tot_f, back, gain_f, tot_a, gain_a, bias_a, uf, first, jh, jl, dx, side,
    rh, rl, o0, o1, o2, o3, us, rg, e0, st, wide, tmp
):
    width = gain_f.shape[1]
    mean, inverse = moments(tot_f[0:1, 0:width], tot_f[1:2, 0:width], number)
    alpha, beta, gamma = back_terms(gain_f[...], mean, inverse, back[0:1, :], back[1:2, :], number)
    g = split(alpha * uf[...] + beta * first[...] + gamma)
    add_whole(rg, dot3(g, (jh[0], jl[0]), 0, 0))
    lanes = o0.shape[1]
    wide[...] = dx[...] + dot3(g, (rh[...], rl[...]))
    for r, o in enumerate((o0, o1, o2, o3)):
        at = pl.multiple_of(idx[3 + r] * lanes, lanes)
        o[...] = wide[:, pl.ds(at, lanes)]
    mean_a, inv_a = moments(tot_a[0:1, :], tot_a[1:2, :], number)
    z = side[...] - mean_a
    top = wide.shape[1] - width
    u = wide[:, top:] * slope(z * (inv_a * gain_a[...]) + bias_a[...])
    us[...] = u
    e0[0] = edge(tmp, u, 0, frames)
    add_rows(st, colsum(u), colsum(u * z))


def side_terms(number, tot_a, back, gain_a):
    mean, inverse = moments(tot_a[0:1, :], tot_a[1:2, :], number)
    return back_terms(gain_a[...], mean, inverse, back[0:1, :], back[1:2, :], number)


def slow9_kernel(number, frames, idx, mask, tot_a, back, gain_a, us, side, x_ref, halo, lg, bz):
    alpha, beta, gamma = side_terms(number, tot_a, back, gain_a)
    g = split(alpha * us[...] + beta * side[...] + gamma)
    add_whole(lg, dot3(g, split(lateral_taps(frames, mask, x_ref, halo, bz)), 0, 0))


def last_kernel(
    number, frames, idx, mask, tot_a, back, gain_a, us, side, us_edge, side_edge, u3, g1, wh, wl,
    rh, rl, o_ref, f_ref, zn
):
    alpha, beta, gamma = side_terms(number, tot_a, back, gain_a)
    here = alpha * us[...] + beta * side[...] + gamma
    after = shifted(zn, here, -1, frames, alpha * us_edge[0] + beta * side_edge[0] + gamma)
    base = u3[...] + dot3(split(g1[...]), (rh[...], rl[...]), 1, 1)
    near = dot3(split(here), (wh[:, 256:], wl[:, 256:]))
    far = dot3(split(masked(after, mask)), (wh[:, 0:256], wl[:, 0:256]))
    both = jnp.concatenate(
        [near[:, 0:256], near[:, 256:384] + far[:, 0:128], far[:, 128:256]], axis=1
    )
    out = base + both
    put_frames(o_ref, out)
    put_frames(f_ref, out)


def weight_split(w):
    high = lax.reduce_precision(w, 8, 7)
    return high.astype(BF16), (w - high).astype(BF16)


def row(v):
    return v.reshape(1, -1)


def tiled_row(v):
    return jnp.tile(v.reshape(1, -1), (1, 4))


def by_pixel(v):
    return v.transpose(1, 0, 2)


def after(value, *events):
    return lax.optimization_barrier((value,) + events)[0]


def local(sizes, *args):
    (
        slow_input, fast_input, clip_starts,
        fast_reduce, fast_reduce_gain, fast_reduce_bias,
        fast_temporal, fast_temporal_gain, fast_temporal_bias,
        fast_expand, fast_expand_gain, fast_expand_bias,
        lateral_conv, lateral_gain, lateral_bias,
        slow_reduce, slow_reduce_gain, slow_reduce_bias,
        slow_temporal, slow_temporal_gain, slow_temporal_bias,
        slow_expand, slow_expand_gain, slow_expand_bias,
        shortcut_conv, shortcut_gain, shortcut_bias,
        slow_cotangent, fast_cotangent,
    ) = args
    dps, ys, hs = sizes
    roles = ys * hs
    d, y, h = (lax.axis_index(a) for a in ALL)
    m = y * hs + h
    frames, pixels, lanes = slow_input.shape
    shard_rows = slow_reduce.shape[1]
    inner = shard_rows * roles
    joined_width = slow_reduce.shape[0]
    wide = lanes * roles
    number = frames * dps * pixels
    fast_number = number * 4
    half = pixels // hs
    own = pixels // roles
    steps = 7
    half_block, own_block = half // steps, own // steps
    fast_rows, slow_rows = half_block * frames, own_block * frames

    slow_x = by_pixel(slow_input).reshape(pixels * frames, lanes)
    slow_c = by_pixel(slow_cotangent).reshape(pixels * frames, lanes)
    fast_x = by_pixel(fast_input)
    fast_c = by_pixel(fast_cotangent)

    def block_of(p):
        return (p % hs) * ys + p // hs

    def role_xor(r):
        return (y ^ (r // hs)) * hs + (h ^ (r % hs))

    peers = [role_xor(r) for r in range(roles)]
    q = block_of(m)
    idx = jnp.stack([h, q, y] + peers).astype(jnp.int32)
    own_rows = own * frames
    row_at = [own_rows * block_of(p) for p in peers]

    times = d * frames + jnp.arange(0, frames + 1, dtype=jnp.int32)

    def clip_of(t):
        return jnp.sum((clip_starts[None, :] <= t[:, None]).astype(jnp.int32), axis=1) - 1

    same = jnp.logical_and(
        clip_of(times) == clip_of(times - 1), jnp.logical_and(times >= 1, times < frames * dps)
    ).astype(F32)
    mask_prev = jnp.broadcast_to(same[:frames, None], (frames, 128))
    mask_next = jnp.broadcast_to(same[1:, None], (frames, 128))

    def role_pairs(r):
        return [(i, i ^ r) for i in range(roles)]

    def placed(out, got):
        for r in range(1, roles):
            out = lax.dynamic_update_slice_in_dim(out, got[r - 1], row_at[r], axis=0)
        return by_pixel(out.reshape(pixels, frames, lanes))

    swap = [(0, 1), (1, 0)]
    half_rows = half * frames

    def from_core(array):
        return lax.ppermute(
            lax.dynamic_slice_in_dim(array, half_rows * (1 - h), half_rows, axis=0), "hh", swap
        )

    def for_partner(array, here):
        return [
            lax.dynamic_slice_in_dim(array, half_rows * h + own_rows * (1 - y), own_rows, axis=0),
            lax.dynamic_slice_in_dim(here, own_rows * (1 - y), own_rows, axis=0),
        ]

    sho_y = lax.ppermute(shortcut_conv, "yy", swap)
    in_core = from_core(slow_x)
    in_send = jnp.concatenate(for_partner(slow_x, in_core), axis=0)
    in_y = lax.ppermute(in_send, "yy", swap)
    sho_core = jnp.stack([shortcut_conv, sho_y])
    sho_other = lax.ppermute(sho_core, "hh", swap)
    sho_all = jnp.stack([sho_core[0], sho_other[0], sho_core[1], sho_other[1]])
    sho_h, sho_l = weight_split(
        jnp.stack([lax.dynamic_index_in_dim(sho_all, p, 0, keepdims=False) for p in peers])
    )

    vectors = [
        lateral_gain, lateral_bias, slow_reduce_gain, slow_reduce_bias, slow_temporal_gain,
        slow_temporal_bias, slow_expand_gain, slow_expand_bias, shortcut_gain, shortcut_bias,
    ]
    vector = jnp.concatenate(vectors)
    across = -(-vector.shape[0] // (shard_rows * 128)) * 128
    vector = jnp.pad(vector, (0, shard_rows * across - vector.shape[0])).reshape(shard_rows, across)
    piece = jnp.concatenate([lateral_conv.transpose(2, 0, 1).reshape(shard_rows, -1), vector], axis=1)
    column = jnp.stack([piece, lax.ppermute(piece, "yy", swap)])
    other = lax.ppermute(column, "hh", swap)
    table = jnp.stack([column[0], other[0], column[1], other[1]])
    table = jnp.stack([lax.dynamic_index_in_dim(table, p, 0, keepdims=False) for p in peers])
    taps = lateral_conv.shape[0] * lateral_conv.shape[1]
    lat_h, lat_l = weight_split(table[:, :, 0:taps].reshape(inner, taps))
    vector = table[:, :, taps:].reshape(roles, -1)
    share = shard_rows // dps
    piece = jnp.concatenate(
        [slow_reduce.T, slow_temporal.transpose(2, 0, 1).reshape(shard_rows, -1), slow_expand], axis=1
    )
    piece = lax.dynamic_slice_in_dim(piece, d * share, share, axis=0)
    got = lax.all_gather(piece, ALL, axis=0, tiled=False).reshape((dps, roles) + piece.shape)
    matrix = got.transpose(1, 0, 2, 3).reshape(inner, -1)
    bounds = [0, joined_width, joined_width + 3 * inner, joined_width + 3 * inner + wide]
    (red_h, red_l), (tem_h, tem_l), (exp_h, exp_l) = [
        weight_split(matrix[:, bounds[k] : bounds[k + 1]]) for k in range(3)
    ]
    full = []
    start = 0
    for v in vectors:
        full.append(vector[:, start : start + v.shape[0]].reshape(1, -1))
        start += v.shape[0]
    (
        lat_gain, lat_bias, red_gain, red_bias, tem_gain, tem_bias, exp_gain, exp_bias, sho_gain, sho_bias
    ) = full

    eye = jnp.eye(4, dtype=F32)
    up = jnp.eye(4, k=1, dtype=F32)
    down = jnp.eye(4, k=-1, dtype=F32)
    far_next = jnp.eye(4, k=3, dtype=F32)
    far_prev = jnp.eye(4, k=-3, dtype=F32)
    fr_h, fr_l = weight_split(after(jnp.kron(eye, fast_reduce), in_send))
    fe_h, fe_l = weight_split(jnp.kron(eye, fast_expand))
    centre = jnp.kron(eye, fast_temporal[1]) + jnp.kron(up, fast_temporal[0]) + jnp.kron(down, fast_temporal[2])
    outer = jnp.kron(far_next, fast_temporal[2]) + jnp.kron(far_prev, fast_temporal[0])
    ft_h, ft_l = weight_split(jnp.concatenate([centre, outer], axis=0))
    fb_h, fb_l = weight_split(jnp.concatenate([centre, outer], axis=1))
    fr_gain, fr_bias = tiled_row(fast_reduce_gain), tiled_row(fast_reduce_bias)
    ft_gain, ft_bias = tiled_row(fast_temporal_gain), tiled_row(fast_temporal_bias)
    fe_gain, fe_bias = row(fast_expand_gain), row(fast_expand_bias)

    forth = [(i, i + 1) for i in range(dps - 1)]
    backw = [(i + 1, i) for i in range(dps - 1)]
    halo = lax.dynamic_slice(fast_x, (half * h, frames * 4 - 8, 0), (half, 8, 128))
    halo = lax.ppermute(halo, "dp", forth)

    in_half = lambda i, s, *_: s[0] * steps + i
    in_own = lambda i, s, *_: s[1] * steps + i
    own_in_half = lambda i, s, *_: s[2] * steps + i

    def all_of(*arrays):
        return [(x, whole(x)) for x in arrays]

    def const(*dims):
        o = shape(*dims)
        return (o, whole(o))

    def by_block(x, at=None):
        return (x, part(x, x.shape[0] // steps, at))

    def out_rows(rows, width):
        return by_block(shape(rows * steps, width))

    def out_blocks(*dims, dtype=F32):
        return by_block(shape(steps, *dims, dtype=dtype))

    def tmp(*dims):
        return pltpu.VMEM(dims, F32)

    def cut(rows, width):
        return tmp(width // 128, rows, 128)

    other_y = lambda i, s, *_: (1 - s[2]) * steps + i

    fr, sr = fast_rows, slow_rows
    nf, ns = fr * steps, sr * steps
    fx = (fast_x, part(fast_x, half_block, in_half))
    fc = (fast_c, part(fast_c, half_block, in_half))
    masks = all_of(mask_prev, mask_next)
    core = ("hh",)

    p1, e0, e1, st = stepped(
        functools.partial(fast1_kernel, frames), "fast1", steps, [idx], [fx] + all_of(fr_h, fr_l),
        [out_rows(fr, 128), out_blocks(half_block, 128), out_blocks(half_block, 128), const(2, 128)],
        scratch=[cut(fr, 128)],
        est=cost(2 * 3 * nf * 512 * 256, nf * 640 * 4),
    )
    tot_f1, before, beyond = total([st], 1, sizes, core, (e1, e0))
    a1, z1, p2, st = stepped(
        functools.partial(fast2_kernel, fast_number, frames), "fast2", steps, [],
        masks + all_of(tot_f1, fr_gain, fr_bias)
        + [by_block(p1), by_block(before), by_block(beyond)] + all_of(ft_h, ft_l),
        [out_rows(fr, 128)] * 3 + [const(2, 128)],
        scratch=[cut(fr, 128)] * 2,
        est=cost(2 * 3 * nf * 256 * 256, 4 * nf * 128 * 4),
    )
    (tot_f2,) = total([st], 2, sizes, core)
    cot_core = from_core(after(slow_c, tot_f1))
    slow_cot = [cot_core] + [
        lax.all_gather(after(v, matrix), "yy", axis=0, tiled=True) for v in for_partner(slow_c, cot_core)
    ]
    side, side_edge, st_a = stepped(
        functools.partial(lateral_kernel, frames), "lateral", steps, [idx],
        all_of(mask_prev) + [fx, by_block(halo)] + all_of(after(lat_h, st), lat_l),
        [out_rows(fr, inner), out_blocks(half_block, inner), const(2, inner)],
        scratch=[cut(fr, 256)],
        est=cost(2 * 3 * nf * 768 * 256, nf * 768 * 4),
    )
    side_edge = lax.ppermute(side_edge, "dp", backw)
    b1, st = stepped(
        functools.partial(fast3_kernel, fast_number), "fast3", steps, [],
        all_of(tot_f2, ft_gain, ft_bias) + [by_block(p2)] + all_of(fe_h, fe_l),
        [out_rows(fr, 128), const(2, 512)],
        est=cost(2 * 3 * nf * 256 * 512, 2 * nf * 128 * 4),
    )
    tot_f3, tot_a = total([st, st_a], 3, sizes, core)
    half_out = shape(half, frames * 4, 128)
    full_out = shape(pixels, frames * 4, 128)
    fast_half, fast_full, u3, st_f4 = stepped(
        functools.partial(fast4_kernel, fast_number, 1.0 / ys), "fast4", steps, [idx],
        all_of(tot_f3, fe_gain, fe_bias) + [fx, fc, by_block(b1)] + all_of(fe_h, fe_l),
        [by_block(half_out), (full_out, part(full_out, half_block, in_half)), out_rows(fr, 512), const(2, 512)],
        est=cost(2 * 3 * nf * 256 * 512, nf * 5 * 512 * 4),
    )

    side_own = (side, part(side, slow_rows, own_in_half))
    sx = (slow_x, part(slow_x, slow_rows, in_own))
    sc = (slow_c, part(slow_c, slow_rows, in_own))
    bf_joined = out_blocks(sr, joined_width, dtype=BF16)
    first, short, jh, jl, e0, e1, st = stepped(
        functools.partial(slow1_kernel, number, frames), "slow1", steps, [idx],
        all_of(after(tot_a, st_f4), lat_gain, lat_bias) + [sx, (in_core, part(in_core, slow_rows, own_in_half))]
        + [(in_y, part(in_y, slow_rows, at)) for at in (lambda i, *s: i, lambda i, *s: steps + i)]
        + [side_own]
        + all_of(red_h, red_l, sho_h, sho_l),
        [
            out_rows(sr, inner), out_rows(sr, wide), bf_joined, bf_joined,
            out_blocks(own_block, inner), out_blocks(own_block, inner), const(2, inner + wide),
        ],
        scratch=[tmp(sr, joined_width), cut(sr, inner)],
        est=cost(2 * 3 * ns * 1280 * 1280, ns * 4 * 3840 + 7e6),
    )
    tot_s, back_f3, before, beyond = total([st, st_f4], 8, sizes, ROLE, (e1, e0))
    bf_taps = out_blocks(sr, 3 * inner, dtype=BF16)
    wide_masks = all_of(*[jnp.concatenate([v, v], axis=1) for v in (mask_prev, mask_next)])
    th, tl, pm, st = stepped(
        functools.partial(slow2_kernel, number, frames), "slow2", steps, [],
        wide_masks + all_of(tot_s, red_gain, red_bias) + [by_block(x) for x in (first, before, beyond)]
        + all_of(tem_h, tem_l),
        [bf_taps, bf_taps, out_rows(sr, inner), const(2, inner)],
        scratch=[cut(sr, inner)] * 2,
        est=cost(2 * 3 * ns * 768 * 256, ns * 4 * 1500),
    )
    (tot_m,) = total([st], 9, sizes, ROLE)
    bf_mid = out_blocks(sr, inner, dtype=BF16)
    bh, bl, st = stepped(
        functools.partial(slow3_kernel, number), "slow3", steps, [],
        all_of(tot_m, tem_gain, tem_bias) + [by_block(pm)] + all_of(exp_h, exp_l),
        [bf_mid, bf_mid, const(2, wide)],
        est=cost(2 * 3 * ns * 1024 * 256, ns * 4 * 512),
    )
    (tot_l,) = total([st], 10, sizes, ROLE)
    slow_full = shape(pixels * frames, lanes)
    own_out = (slow_full, part(slow_full, slow_rows, in_own))
    *outs, u, st = stepped(
        functools.partial(slow4_kernel, number), "slow4", steps, [idx],
        all_of(tot_l, tot_s, exp_gain, exp_bias, sho_gain, sho_bias)
        + [by_block(x) for x in (bh, bl, short)] + [sc]
        + [(slow_cot[0], part(slow_cot[0], slow_rows, own_in_half))]
        + [(x, part(x, slow_rows, other_y)) for x in slow_cot[1:]]
        + all_of(exp_h, exp_l),
        [own_out] + [out_rows(sr, lanes)] * (roles - 1) + [out_rows(sr, wide), const(4, wide)],
        scratch=[tmp(sr, wide)],
        est=cost(2 * 3 * ns * 1024 * 256, ns * 4 * 4352),
    )
    (back_ls,) = total([st], 11, sizes, ROLE)
    sent = [lax.ppermute(after(outs[r], back_ls), ROLE, role_pairs(r)) for r in range(1, roles)]

    dx, short_grads = stepped(
        functools.partial(slow6_kernel, number), "slow6", steps, [],
        all_of(tot_s, back_ls, sho_gain) + [by_block(x) for x in (u, short, jh, jl)] + all_of(sho_h, sho_l),
        [out_rows(sr, joined_width), const(roles, joined_width, lanes)],
        est=cost(2 * 6 * ns * 1280 * 1024, ns * 4 * 4600 + 12e6),
    )
    um, expand_grad, e0, e1, st = stepped(
        functools.partial(slow5_kernel, number, frames), "slow5", steps, [],
        all_of(tot_l, after(back_ls, dx), exp_gain, tot_m, tem_gain, tem_bias)
        + [by_block(x) for x in (u, bh, bl, pm)] + all_of(exp_h, exp_l),
        [
            out_rows(sr, inner), const(inner, wide), out_blocks(2, own_block, inner),
            out_blocks(2, own_block, inner), const(2, inner),
        ],
        scratch=[cut(sr, inner)],
        est=cost(2 * 9 * ns * 1024 * 256, ns * 4 * 1800),
    )
    slow_output = placed(outs[0], sent)
    back_m, before, beyond = total([after(st, *sent)], 12, sizes, ROLE, (e1, e0))
    def by_peer(g):
        rows = g.shape[0] // roles
        parts = [lax.dynamic_slice_in_dim(g, p * rows, rows, axis=0) for p in peers]
        return jnp.stack([parts[0], parts[2]]), jnp.stack([parts[1], parts[3]])

    def chip_sum(near, far):
        return near + lax.ppermute(far, "hh", swap)

    near, far = by_peer(short_grads.reshape(roles * joined_width, lanes))
    short_both = chip_sum(near, after(far, back_m))
    short_got = lax.all_gather(short_both[1], "yy", axis=0, tiled=False)
    uf, temporal_grad, st = stepped(
        functools.partial(slow7_kernel, number, frames), "slow7", steps, [],
        wide_masks + all_of(tot_m, back_m, tem_gain, tot_s, red_gain, red_bias)
        + [by_block(x) for x in (um, pm, before, beyond, th, tl, first)] + all_of(tem_h, tem_l),
        [out_rows(sr, inner), const(inner, 3 * inner), const(2, inner)],
        scratch=[cut(sr, inner)] * 2,
        est=cost(2 * 6 * ns * 768 * 256, ns * 4 * 1500),
    )
    (back_f,) = total([st], 13, sizes, ROLE)
    *outs, us, reduce_grad, us_edge, st = stepped(
        functools.partial(slow8_kernel, number, frames), "slow8", steps, [idx],
        all_of(tot_s, back_f, red_gain, tot_a, lat_gain, lat_bias)
        + [by_block(x) for x in (uf, first, jh, jl, dx)] + [side_own] + all_of(red_h, red_l),
        [own_out] + [out_rows(sr, lanes)] * (roles - 1)
        + [out_rows(sr, inner), const(inner, joined_width), out_blocks(own_block, inner), const(2, inner)],
        scratch=[tmp(sr, joined_width), cut(sr, inner)],
        est=cost(2 * 6 * ns * 1280 * 256, ns * 4 * 5000),
    )
    (back_a,) = total([after(st, short_got)], 14, sizes, ROLE)
    shortcut_sum = lax.psum(
        short_both[0] + lax.dynamic_index_in_dim(short_got, 1 - y, 0, keepdims=False), "dp"
    )
    us_sent = after(us, back_a)
    us_other = lax.ppermute(us_sent, "yy", swap)
    edge_sent = after(us_edge, back_a)
    edge_same = lax.ppermute(edge_sent, "dp", backw)
    edge_cross = lax.ppermute(
        edge_sent, ("dp", "yy"), [(i * ys + j, (i - 1) * ys + 1 - j) for i in range(1, dps) for j in range(ys)]
    )

    own_halo = (halo, part(halo, own_block, own_in_half))
    (lateral_grad,) = stepped(
        functools.partial(slow9_kernel, number, frames), "slow9", steps, [idx],
        all_of(mask_prev, tot_a, back_a, lat_gain)
        + [by_block(us), side_own, (fast_x, part(fast_x, own_block, in_own)), own_halo],
        [const(inner, 640)],
        scratch=[cut(sr, 256)],
        est=cost(2 * 3 * ns * 640 * 256, ns * 4 * 1500),
    )

    both = chip_sum(*by_peer(jnp.concatenate([reduce_grad, temporal_grad, expand_grad, lateral_grad], axis=1)))
    rest = both[0] + lax.ppermute(both[1], "yy", swap)
    grads_sent = [
        lax.ppermute(after(outs[r], back_a if r == 1 else both), ROLE, role_pairs(r))
        for r in range(1, roles)
    ]
    slow_input_gradient = placed(outs[0], grads_sent)

    u2, expand_packed, e0, e1, st = stepped(
        functools.partial(fast5_kernel, fast_number, frames), "fast5", steps, [],
        all_of(tot_f3, after(back_f3, back_a, lateral_grad), fe_gain, tot_f2, ft_gain, ft_bias)
        + [by_block(u3), by_block(b1), by_block(p2)] + all_of(fe_h, fe_l),
        [
            out_rows(fr, 128), const(128, 512), out_blocks(2, half_block, 128),
            out_blocks(2, half_block, 128), const(2, 128),
        ],
        scratch=[cut(fr, 128)],
        est=cost(2 * 9 * nf * 256 * 512, nf * 900 * 4),
    )
    back_f2, before, beyond = total([after(st, us_other)], 5, sizes, core, (e1, e0))
    u1, temporal_packed, st = stepped(
        functools.partial(fast6_kernel, fast_number, frames), "fast6", steps, [],
        masks + all_of(tot_f2, back_f2, ft_gain, tot_f1, fr_gain, fr_bias)
        + [by_block(x) for x in (u2, p2, before, beyond, a1, z1, p1)] + all_of(fb_h, fb_l),
        [out_rows(fr, 128), const(256, 128), const(2, 128)],
        scratch=[cut(fr, 128)] * 2,
        est=cost(2 * 6 * nf * 256 * 256, 6 * nf * 128 * 4),
    )
    (back_f1,) = total([st], 6, sizes, core)
    g1, reduce_packed = stepped(
        functools.partial(fast7_kernel, fast_number), "fast7", steps, [idx],
        all_of(tot_f1, back_f1, fr_gain) + [fx, by_block(u1), by_block(p1)],
        [out_rows(fr, 128), const(512, 128)],
        est=cost(2 * 3 * nf * 512 * 256, nf * 900 * 4),
    )

    def in_order(mine, other):
        return jnp.concatenate([jnp.where(y == 0, mine, other), jnp.where(y == 0, other, mine)], axis=0)

    us_half = in_order(us, us_other)
    rim = in_order(edge_same.reshape(own, inner), edge_cross.reshape(own, inner))
    grad_half, grad_full = stepped(
        functools.partial(last_kernel, number, frames), "last", steps, [idx],
        all_of(mask_next, tot_a, after(back_a, rest, grads_sent[1], shortcut_sum), lat_gain)
        + [by_block(x) for x in (us_half, side, rim.reshape(steps, half_block, inner), side_edge, u3, g1)]
        + all_of(lat_h, lat_l, fr_h, fr_l),
        [by_block(half_out), (full_out, part(full_out, half_block, in_half))],
        scratch=[cut(fr, inner)],
        est=cost(2 * 3 * nf * 1024 * 256, nf * 4 * 2000),
    )

    def fast_whole(mine, full):
        got = lax.ppermute(mine, "hh", swap)
        return by_pixel(lax.dynamic_update_slice_in_dim(full, got, half * (1 - h), axis=0))

    fast_output = fast_whole(fast_half, fast_full)
    fast_input_gradient = fast_whole(grad_half, grad_full)

    rest = lax.psum(after(rest, shortcut_sum), "dp")
    reduce_sum = rest[:, 0:joined_width].T
    expand_sum = rest[:, joined_width + 3 * inner : joined_width + 3 * inner + wide]
    lateral_sum = rest[:, joined_width + 3 * inner + wide :].reshape(shard_rows, -1, 128).transpose(1, 2, 0)
    temporal_sum = rest[:, joined_width : joined_width + 3 * inner].reshape(shard_rows, 3, inner).transpose(1, 2, 0)

    eb = expand_packed.reshape(4, 32, 4, 128)
    expand_small = eb[0, :, 0] + eb[1, :, 1] + eb[2, :, 2] + eb[3, :, 3]
    rb = reduce_packed.reshape(4, 128, 4, 32)
    reduce_small = rb[0, :, 0] + rb[1, :, 1] + rb[2, :, 2] + rb[3, :, 3]
    tb = temporal_packed.reshape(8, 32, 4, 32)
    tap0 = tb[0, :, 1] + tb[1, :, 2] + tb[2, :, 3] + tb[7, :, 0]
    tap1 = tb[0, :, 0] + tb[1, :, 1] + tb[2, :, 2] + tb[3, :, 3]
    tap2 = tb[1, :, 0] + tb[2, :, 1] + tb[3, :, 2] + tb[4, :, 3]
    small = jnp.concatenate(
        [expand_small, reduce_small.reshape(32, 128), jnp.stack([tap0, tap1, tap2]).reshape(24, 128)], axis=0
    )
    (small,) = total([small], 15, sizes, core)

    def fold(v):
        return jnp.sum(v.reshape(4, -1), axis=0)

    def zhat(back, tot, n, row_at=1, off=0):
        mean = tot[0, off:] / n
        return back[row_at] * lax.rsqrt(tot[1, off:] / n - mean * mean + EPSILON)

    def fast_pair(back, tot):
        sums = jnp.sum(tot.reshape(2, 4, -1), axis=1)
        bias = fold(back[0])
        mean = sums[0] / fast_number
        return fold(back[1]) * lax.rsqrt(sums[1] / fast_number - mean * mean + EPSILON), bias

    def shard(v):
        size = v.shape[0] // roles
        return lax.dynamic_slice_in_dim(v, m * size, size, axis=0)

    def slow_pair(back, tot, n=number, row_at=1, off=0, width=None):
        tot = tot[:, : width] if width else tot
        return shard(zhat(back, tot, n, row_at, off)), shard(back[0])

    fr_gg, fr_bg = fast_pair(back_f1, tot_f1)
    ft_gg, ft_bg = fast_pair(back_f2, tot_f2)
    fe_gg, fe_bg = fast_pair(back_f3, tot_f3)
    la_gg, la_bg = slow_pair(back_a, tot_a, number)
    re_gg, re_bg = slow_pair(back_f, tot_s, width=inner)
    te_gg, te_bg = slow_pair(back_m, tot_m)
    ex_gg, ex_bg = slow_pair(back_ls, tot_l)
    sh_gg, sh_bg = slow_pair(back_ls, tot_s, row_at=2, off=inner)
    return (
        slow_output, fast_output, slow_input_gradient, fast_input_gradient,
        small[32:64].reshape(128, 32), fr_gg, fr_bg,
        small[64:88].reshape(3, 32, 32), ft_gg, ft_bg,
        small[0:32], fe_gg, fe_bg,
        lateral_sum, la_gg, la_bg,
        reduce_sum, re_gg, re_bg,
        temporal_sum, te_gg, te_bg,
        expand_sum, ex_gg, ex_bg,
        shortcut_sum, sh_gg, sh_bg,
    )


def solution(mesh):
    dps, roles = mesh.shape["dp"], mesh.shape["mp"]
    sizes = (dps, roles // 2, 2)
    fine = Mesh(mesh.devices.reshape(sizes), ALL)
    mp = ROLE
    frames3 = P("dp", None, mp)
    fast3 = P("dp", None, None)
    none = P()
    in_specs = (
        (frames3, fast3) + (none,) * 10
        + (P(None, None, mp), P(mp), P(mp), P(None, mp), P(mp), P(mp), P(None, None, mp), P(mp), P(mp),
           P(mp, None), P(mp), P(mp), P(None, mp), P(mp), P(mp), frames3, fast3)
    )
    out_specs = (
        (frames3, fast3, frames3, fast3) + (none,) * 9
        + (P(None, None, mp), P(mp), P(mp), P(None, mp), P(mp), P(mp), P(None, None, mp), P(mp), P(mp),
           P(mp, None), P(mp), P(mp), P(None, mp), P(mp), P(mp))
    )
    return jax.shard_map(
        functools.partial(local, sizes), mesh=fine, in_specs=in_specs, out_specs=out_specs, check_vma=False
    )
```

time: 1530 us -> 662 us (0.43)
  matrix products: 521 us -> 0 us
  waiting for transfers between devices: 552 us -> 98.4 us
  Pallas kernels: 0 us -> 388 us
  blocking collectives: 180 us -> 0 us
  other arithmetic: 121 us -> 47.9 us
    dot_general x54 -> x0, matrix products: 521 us -> none  [the longest x36 370 us: product(): jnp.dot(former, latter, precision=PRECISE, preferred_element_type=jnp.flo...]
    pallas_call x0 -> x31, Pallas kernels: none -> 388 us  [the longest x18 249 us: stepped(): pl.pallas_call(body, name=name, out_shape=[o for o, _ in outs], grid_spec...]
    reduce_scatter x4 -> x0, waiting for transfers between devices: 243 us -> none  [the longest x1 129 us: local(): lax.psum_scatter(joined_slow, 'mp', scatter_dimension=2, tiled=True)]
    psum x8 -> x0, blocking collectives: 180 us -> none  [dp_sums(): return lax.psum((former, latter), 'dp')]
    all_gather x4, waiting for transfers between devices: 143 us -> 0.08 us  [the longest x2 0.04 us: local(): lax.all_gather(after(v, matrix), 'yy', axis=0, tiled=True)]
    psum x2, waiting for transfers between devices: 162 us -> 52.1 us  [the longest x1 52.1 us: local(): rest = lax.psum(after(rest, shortcut_sum), 'dp')]
    unnamed x304 -> x113, local copies, waits for them, and re-layouts: 67.1 us -> 8.35 us
    reduce_sum x8 -> x10, other arithmetic: 45.1 us -> 1.81 us  [the longest x6 1.66 us: fold(): return jnp.sum(v.reshape(4, -1), axis=0)]
  transfers between devices with their start and end apart: 20 -> 29, of which waited for: 9 -> 4; matrix products, arithmetic and copies ran while one was open for 35% -> 19% of each run, Pallas kernels for 0% -> 57%
where the time goes in v1:
time: 662 us; the launch traced here: 657 us
  Pallas kernels  388 us (59%)
  waiting for transfers between devices  98.4 us (15%)
  local copies, waits for them, and re-layouts  85.3 us (13%)
  other arithmetic  47.9 us (7%)
  starting transfers between devices  21.2 us (3%)
  between operations  15.6 us (2%)
    pallas_call x18, Pallas kernels, stepped(): pl.pallas_call(body, name=name, out_shape=[o for o, _ in outs], grid_spec...  249 us
    pallas_call x13, Pallas kernels, total(): pl.pallas_call(functools.partial(sum_kernel, sizes, axes, widths, len(rim...  139 us
    psum x1, waiting for transfers between devices, local(): rest = lax.psum(after(rest, shortcut_sum), 'dp')  52.1 us
    ppermute x3, waiting for transfers between devices, local(): lax.ppermute(after(outs[r], back_a if r == 1 else both), ROLE, role_pairs...  38 us
  transfers between devices with their start and end apart: 29, of which 4 were waited for; matrix products, arithmetic and copies ran while one was open for 19% of the time, Pallas kernels for 57%

profile of v1, /device:TPU:0, one launch (start us, length us, event | category | flops | bytes accessed | tf_op | source)
XLA Modules:
  0.0 656.8 jit_solution(11749005943651692970)
XLA Ops:
  11.5 3.0 collective-permute-start.2
  14.4 1.8 dynamic-slice_bitcast_fusion.8
  16.2 4.2 collective-permute-start.1
  20.9 3.3 constant_dynamic-slice_fusion.31
  30.5 1.7 fusion.8
  32.1 2.4 constant_dynamic-slice_fusion.32
  35.3 1.7 pad_maximum_fusion.10
  41.9 2.4 constant_dynamic-slice_fusion.19
  53.9 1.8 pad_maximum_fusion.3
  55.9 1.8 constant_dynamic-slice_fusion.30
  61.8 8.0 %fast1.1 = (f32[2352,128]{1,0:T(8,128)}, f32[7,14,128]{2,1,0:T(8,128)}, f32[7,14,128]{2,1,0:T(8,128)}, f32[2,128]{1,0:T(2,128)}) custom-call(s32[7]{0:T(128)} %stack.111.idx, f32[196,96,128]{2,1,0:T(8,128)} %bitcast.172, bf16[512,128]{1,0:T(8,128)(2,1)} %get-tuple-element.405.rh, bf16[512,128]{1,0:T(8,128)(2,1)} %get-tuple-element.404.rl), custom_call_target="tpu_custom_call" | custom-call | flops 3699376128 | bytes 12042240 | tf_op jit(solution)/shard_map/fast1/pallas_call | solution.py:161
  69.8 9.1 %sum1.1 = (f32[2,128]{1,0:T(2,128)}, f32[7,14,128]{2,1,0:T(8,128)}, f32[7,14,128]{2,1,0:T(8,128)}) custom-call(f32[2,128]{1,0:T(2,128)} %get-tuple-element.133.refs_0_, f32[7,14,128]{2,1,0:T(8,128)} %get-tuple-element.134.refs_1_, f32[7,14,128]{2,1,0:T(8,128)} %get-tuple-element.135.refs_2_), custom_call_target="tpu_custom_call" | custom-call | tf_op jit(solution)/shard_map/sum1/pallas_call | solution.py:251
  78.9 3.3 constant_dynamic-slice_fusion.20
  82.2 7.0 %fast2.1 = (f32[2352,128]{1,0:T(8,128)}, f32[2352,128]{1,0:T(8,128)}, f32[2352,128]{1,0:T(8,128)}, f32[2,128]{1,0:T(2,128)}) custom-call(f32[24,128]{1,0:T(8,128)} %copy-done.24, f32[24,128]{1,0:T(8,128)} %copy-done.28, f32[2,128]{1,0:T(2,128)} %get-tuple-element.136.tot.tot1, f32[1,128]{1,0:T(1,128)} %tile.33.gain.gain1, f32[1,128]{1,0:T(1,128)} %tile.35.bias.bias1, ...), custom_call_target="tpu_custom_call" | custom-call | flops 1849688064 | bytes 9633792 | tf_op jit(solution)/shard_map/fast2/pallas_call | solution.py:161
  89.1 8.5 %sum2.1.tot.tot2 = f32[2,128]{1,0:T(2,128)} custom-call(f32[2,128]{1,0:T(2,128)} %get-tuple-element.140.refs_0_), custom_call_target="tpu_custom_call" | custom-call | tf_op jit(solution)/shard_map/sum2/pallas_call | solution.py:251
  97.7 8.9 %lateral.1 = (f32[2352,256]{1,0:T(8,128)}, f32[7,14,256]{2,1,0:T(8,128)}, f32[2,256]{1,0:T(2,128)}) custom-call(s32[7]{0:T(128)} %stack.111.idx, f32[24,128]{1,0:T(8,128)} %copy-done.24, f32[196,96,128]{2,1,0:T(8,128)} %bitcast.173, f32[98,8,128]{2,1,0:T(8,128)} %collective-permute-done.1.halo, bf16[256,640]{1,0:T(8,128)(2,1)} %get-tuple-element.143.wh, ...), custom_call_target="tpu_custom_call" | custom-call | flops 5549064192 | bytes 14450688 | tf_op jit(solution)/shard_map/lateral/pallas_call | solution.py:161
  106.6 6.8 %fast3.1 = (f32[2352,128]{1,0:T(8,128)}, f32[2,512]{1,0:T(2,128)}) custom-call(f32[2,128]{1,0:T(2,128)} %sum2.1.tot.tot2, f32[1,128]{1,0:T(1,128)} %tile.37.gain.gain2, f32[1,128]{1,0:T(1,128)} %tile.39.bias.bias2, f32[2352,128]{1,0:T(8,128)} %get-tuple-element.141.p2, bf16[128,512]{1,0:T(8,128)(2,1)} %get-tuple-element.403.eh, ...), custom_call_target="tpu_custom_call" | custom-call | flops 3699376128 | bytes 4816896 | tf_op jit(solution)/shard_map/fast3/pallas_call | solution.py:161
  113.5 7.8 %sum3.1 = (f32[2,512]{1,0:T(2,128)}, f32[2,256]{1,0:T(2,128)}) custom-call(f32[2,512]{1,0:T(2,128)} %get-tuple-element.142.refs_0_, f32[2,256]{1,0:T(2,128)} %get-tuple-element.144.refs_1_), custom_call_target="tpu_custom_call" | custom-call | tf_op jit(solution)/shard_map/sum3/pallas_call | solution.py:251
  121.3 2.1 copy.140
  123.5 14.4 %fast4.1 = (f32[98,96,128]{2,1,0:T(8,128)}, f32[196,96,128]{2,1,0:T(8,128)}, f32[2352,512]{1,0:T(8,128)}, f32[2,512]{1,0:T(2,128)}) custom-call(s32[7]{0:T(128)} %stack.111.idx, f32[2,512]{1,0:T(2,128)} %get-tuple-element.146.tot, f32[1,128]{1,0:T(1,128)} %bitcast.232, f32[1,128]{1,0:T(1,128)} %bitcast.231, f32[196,96,128]{2,1,0:T(8,128)} %bitcast.174, ...), custom_call_target="tpu_custom_call" | custom-call | flops 3699376128 | bytes 48168960 | tf_op jit(solution)/shard_map/fast4/pallas_call | solution.py:161
  138.3 2.1 fusion.50
  141.1 2.8 fusion
  143.9 2.4 constant_dynamic-slice_fusion.18
  147.9 21.3 %slow1.1 = (f32[1176,256]{1,0:T(8,128)}, f32[1176,1024]{1,0:T(8,128)}, bf16[7,168,1280]{2,1,0:T(8,128)(2,1)}, bf16[7,168,1280]{2,1,0:T(8,128)(2,1)}, f32[7,7,256...) custom-call(s32[7]{0:T(128)} %stack.111.idx, f32[2,256]{1,0:T(2,128)} %get-tuple-element.149.tot.tot_a, ...), custom_call_target="tpu_custom_call" | custom-call | flops 23121100800 | bytes 50126720 | tf_op jit(solution)/shard_map/slow1/pallas_call | solution.py:161
  169.3 11.7 %sum8.1 = (f32[2,1280]{1,0:T(2,128)}, f32[2,512]{1,0:T(2,128)}, f32[7,7,256]{2,1,0:T(8,128)}, f32[7,7,256]{2,1,0:T(8,128)}) custom-call(f32[2,1280]{1,0:T(2,128)} %get-tuple-element.151.refs_0_, f32[2,512]{1,0:T(2,128)} %get-tuple-element.148.refs_1_, f32[7,7,256]{2,1,0:T(8,128)} %get-tuple-element.152.refs_2_, f32[7,7,256]{2,1,0:T(8,128)} %get-tuple-element.153.refs_3_), custom_call_target="tpu_custom_call" | custom-call | tf_op jit(solution)/shard_map/sum8/pallas_call | solution.py:251
  181.9 8.2 %slow2.1 = (bf16[7,168,768]{2,1,0:T(8,128)(2,1)}, bf16[7,168,768]{2,1,0:T(8,128)(2,1)}, f32[1176,256]{1,0:T(8,128)}, f32[2,256]{1,0:T(2,128)}) custom-call(f32[24,256]{1,0:T(8,128)} %pad_maximum_fusion.15.mp, f32[24,256]{1,0:T(8,128)} %pad_maximum_fusion.16.mn, f32[2,1280]{1,0:T(2,128)} %get-tuple-element.154.tot.tot_s.tot_f, ...), custom_call_target="tpu_custom_call" | custom-call | flops 2774532096 | bytes 14112000 | tf_op jit(solution)/shard_map/slow2/pallas_call | solution.py:161
  190.1 11.5 %sum9.1.tot.tot_m = f32[2,256]{1,0:T(2,128)} custom-call(f32[2,256]{1,0:T(2,128)} %get-tuple-element.158.refs_0_), custom_call_target="tpu_custom_call" | custom-call | tf_op jit(solution)/shard_map/sum9/pallas_call | solution.py:251
  202.8 6.9 %slow3.1 = (bf16[7,168,256]{2,1,0:T(8,128)(2,1)}, bf16[7,168,256]{2,1,0:T(8,128)(2,1)}, f32[2,1024]{1,0:T(2,128)}) custom-call(f32[2,256]{1,0:T(2,128)} %sum9.1.tot.tot_m, f32[1,256]{1,0:T(1,128)} %reshape.539.gain.gain_m, f32[1,256]{1,0:T(1,128)} %reshape.540.bias.bias_m, f32[1176,256]{1,0:T(8,128)} %get-tuple-element.159.pm, ...), custom_call_target="tpu_custom_call" | custom-call | flops 3699376128 | bytes 4816896 | tf_op jit(solution)/shard_map/slow3/pallas_call | solution.py:161
  209.7 10.9 %sum10.1.tot_l = f32[2,1024]{1,0:T(2,128)} custom-call(f32[2,1024]{1,0:T(2,128)} %get-tuple-element.160.refs_0_), custom_call_target="tpu_custom_call" | custom-call | tf_op jit(solution)/shard_map/sum10/pallas_call | solution.py:251
  220.6 13.5 %slow4.1 = (f32[4704,256]{1,0:T(8,128)}, f32[1176,256]{1,0:T(8,128)}, f32[1176,256]{1,0:T(8,128)}, f32[1176,256]{1,0:T(8,128)}, f32[1176,1024]{1,0:T(8,128)}, /*index=5*/f32[4,1024]{1,0:T(4,128)}) custom-call(s32[7]{0:T(128)} %stack.111.idx, f32[2,1024]{1,0:T(2,128)} %sum10.1.tot_l, f32[2,1280]{1,0:T(2,128)} %get-tuple-element.154.tot.tot_s.tot_f, ...), custom_call_target="tpu_custom_call" | custom-call | flops 3699376128 | bytes 40943616 | tf_op jit(solution)/shard_map/slow4/pallas_call | solution.py:161
  234.1 11.9 %sum11.1.back = f32[4,1024]{1,0:T(4,128)} custom-call(f32[4,1024]{1,0:T(4,128)} %get-tuple-element.169.refs_0_), custom_call_target="tpu_custom_call" | custom-call | tf_op jit(solution)/shard_map/sum11/pallas_call | solution.py:251
  248.0 38.2 %slow6.1 = (f32[1176,1280]{1,0:T(8,128)}, f32[4,1280,256]{2,1,0:T(8,128)}) custom-call(f32[2,1280]{1,0:T(2,128)} %get-tuple-element.154.tot.tot_s.tot_f, f32[4,1024]{1,0:T(4,128)} %sum11.1.back, f32[1,1024]{1,0:T(1,128)} %bitcast.223, f32[1176,1024]{1,0:T(8,128)} %get-tuple-element.177.u_ref, f32[1176,1024]{1,0:T(8,128)} %get-tuple-element.163.short, ...), custom_call_target="tpu_custom_call" | custom-call | flops 36993761280 | bytes 67276800 | tf_op jit(solution)/shard_map/slow6/pallas_call | solution.py:161
  286.2 4.3 dynamic-slice_bitcast_fusion.3
  290.8 29.7 %slow5.1 = (f32[1176,256]{1,0:T(8,128)}, f32[256,1024]{1,0:T(8,128)}, f32[7,2,7,256]{3,2,1,0:T(8,128)}, f32[7,2,7,256]{3,2,1,0:T(8,128)}, f32[2,256]{1,0:T(2,128)}) custom-call(f32[2,1024]{1,0:T(2,128)} %sum10.1.tot_l, f32[4,1024]{1,0:T(4,128)} %sum11.1.back, f32[1,1024]{1,0:T(1,128)} %bitcast.220, f32[2,256]{1,0:T(2,128)} %sum9.1.tot.tot_m, ...), custom_call_target="tpu_custom_call" | custom-call | flops 11098128384 | bytes 16934400 | tf_op jit(solution)/shard_map/slow5/pallas_call | solution.py:161
  320.5 12.8 %sum12.1 = (f32[2,256]{1,0:T(2,128)}, f32[7,2,7,256]{3,2,1,0:T(8,128)}, f32[7,2,7,256]{3,2,1,0:T(8,128)}) custom-call(f32[2,256]{1,0:T(2,128)} %get-tuple-element.183.refs_0_, f32[7,2,7,256]{3,2,1,0:T(8,128)} %get-tuple-element.184.refs_1_, f32[7,2,7,256]{3,2,1,0:T(8,128)} %get-tuple-element.185.refs_2_), custom_call_target="tpu_custom_call" | custom-call | tf_op jit(solution)/shard_map/sum12/pallas_call | solution.py:251
  337.5 5.1 constant_dynamic-update-slice_fusion.4
  343.8 2.1 maximum_add_fusion
  347.1 13.1 %slow7.1 = (f32[1176,256]{1,0:T(8,128)}, f32[256,768]{1,0:T(8,128)}, f32[2,256]{1,0:T(2,128)}) custom-call(f32[24,256]{1,0:T(8,128)} %pad_maximum_fusion.15.mp, f32[24,256]{1,0:T(8,128)} %pad_maximum_fusion.16.mn, f32[2,256]{1,0:T(2,128)} %sum9.1.tot.tot_m, f32[2,256]{1,0:T(2,128)} %get-tuple-element.186.back, f32[1,256]{1,0:T(1,128)} %reshape.539.gain.gain_m, ...), custom_call_target="tpu_custom_call" | custom-call | flops 5549064192 | bytes 14112000 | tf_op jit(solution)/shard_map/slow7/pallas_call | solution.py:161
  360.2 12.0 %sum13.1.back = f32[2,256]{1,0:T(2,128)} custom-call(f32[2,256]{1,0:T(2,128)} %get-tuple-element.192.refs_0_), custom_call_target="tpu_custom_call" | custom-call | tf_op jit(solution)/shard_map/sum13/pallas_call | solution.py:251
  375.3 2.4 constant_dynamic-update-slice_fusion.7
  377.7 2.4 constant_dynamic-update-slice_fusion.6
  380.1 19.7 %slow8.1 = (f32[4704,256]{1,0:T(8,128)}, f32[1176,256]{1,0:T(8,128)}, f32[1176,256]{1,0:T(8,128)}, f32[1176,256]{1,0:T(8,128)}, f32[1176,256]{1,0:T(8,128)}, /*i...) custom-call(s32[7]{0:T(128)} %stack.111.idx, f32[2,1280]{1,0:T(2,128)} %get-tuple-element.154.tot.tot_s.tot_f, ...), custom_call_target="tpu_custom_call" | custom-call | flops 9248440320 | bytes 47040000 | tf_op jit(solution)/shard_map/slow8/pallas_call | solution.py:161
  399.8 10.8 %sum14.1.back = f32[2,256]{1,0:T(2,128)} custom-call(f32[2,256]{1,0:T(2,128)} %get-tuple-element.199.refs_0_), custom_call_target="tpu_custom_call" | custom-call | tf_op jit(solution)/shard_map/sum14/pallas_call | solution.py:251
  413.2 2.6 fusion.2
  415.9 9.2 %slow9.1 = f32[256,640]{1,0:T(8,128)} custom-call(s32[7]{0:T(128)} %stack.111.idx, f32[24,128]{1,0:T(8,128)} %copy-done.24, f32[2,256]{1,0:T(2,128)} %get-tuple-element.149.tot.tot_a, f32[2,256]{1,0:T(2,128)} %sum14.1.back, f32[1,256]{1,0:T(1,128)} %reshape.532.gain.gain_a, f32[1176,256]{1,0:T(8,128)} %get-tuple-element.210.us, ...), custom_call_target="tpu_custom_call" | custom-call | flops 2312110080 | bytes 14112000 | tf_op jit(solution)/shard_map/slow9/pallas_call | solution.py:161
  429.9 13.2 %fast5.1 = (f32[2352,128]{1,0:T(8,128)}, f32[128,512]{1,0:T(8,128)}, f32[7,2,14,128]{3,2,1,0:T(8,128)}, f32[7,2,14,128]{3,2,1,0:T(8,128)}, f32[2,128]{1,0:T(2,128)}) custom-call(f32[2,512]{1,0:T(2,128)} %get-tuple-element.146.tot, f32[2,512]{1,0:T(2,128)} %get-tuple-element.216.back, f32[1,128]{1,0:T(1,128)} %bitcast.233, f32[2,128]{1,0:T(2,128)} %sum2.1.tot.tot2, ...), custom_call_target="tpu_custom_call" | custom-call | flops 11098128384 | bytes 16934400 | tf_op jit(solution)/shard_map/fast5/pallas_call | solution.py:161
  444.7 8.1 %collective-permute-done.18 = f32[1176,256]{1,0:T(8,128)} collective-permute-done((f32[1176,256]{1,0:T(8,128)S(1)}, f32[1176,256]{1,0:T(8,128)}, u32[]{:S(2)}, u32[]{:S(2)}) %collective-permute-start.18) | collective-permute-done | bytes 1204256 | tf_op jit(solution)/shard_map/ppermute | solution.py:953
  452.8 12.7 %sum5.1 = (f32[2,128]{1,0:T(2,128)}, f32[7,2,14,128]{3,2,1,0:T(8,128)}, f32[7,2,14,128]{3,2,1,0:T(8,128)}) custom-call(f32[2,128]{1,0:T(2,128)} %get-tuple-element.218.refs_0_, f32[7,2,14,128]{3,2,1,0:T(8,128)} %get-tuple-element.219.refs_1_, f32[7,2,14,128]{3,2,1,0:T(8,128)} %get-tuple-element.220.refs_2_), custom_call_target="tpu_custom_call" | custom-call | tf_op jit(solution)/shard_map/sum5/pallas_call | solution.py:251
  465.6 2.6 broadcast_select_fusion.1
  468.2 1.8 maximum_add_fusion.1
  471.8 9.4 %fast6.1 = (f32[2352,128]{1,0:T(8,128)}, f32[256,128]{1,0:T(8,128)}, f32[2,128]{1,0:T(2,128)}) custom-call(f32[24,128]{1,0:T(8,128)} %copy-done.24, f32[24,128]{1,0:T(8,128)} %copy-done.28, f32[2,128]{1,0:T(2,128)} %sum2.1.tot.tot2, f32[2,128]{1,0:T(2,128)} %get-tuple-element.221.back2, f32[1,128]{1,0:T(1,128)} %tile.37.gain.gain2, ...), custom_call_target="tpu_custom_call" | custom-call | flops 3699376128 | bytes 14450688 | tf_op jit(solution)/shard_map/fast6/pallas_call | solution.py:161
  481.2 7.7 %sum6.1.back1 = f32[2,128]{1,0:T(2,128)} custom-call(f32[2,128]{1,0:T(2,128)} %get-tuple-element.227.refs_0_), custom_call_target="tpu_custom_call" | custom-call | tf_op jit(solution)/shard_map/sum6/pallas_call | solution.py:251
  488.9 3.0 pad_maximum_fusion.6.us
  493.1 8.8 %fast7.1 = (f32[2352,128]{1,0:T(8,128)}, f32[512,128]{1,0:T(8,128)}) custom-call(s32[7]{0:T(128)} %stack.111.idx, f32[2,128]{1,0:T(2,128)} %get-tuple-element.136.tot.tot1, f32[2,128]{1,0:T(2,128)} %sum6.1.back1, f32[1,128]{1,0:T(1,128)} %tile.33.gain.gain1, f32[196,96,128]{2,1,0:T(8,128)} %bitcast.176, f32[2352,128]{1,0:T(8,128)} %get-tuple-element.228.u1, ...), custom_call_target="tpu_custom_call" | custom-call | flops 3699376128 | bytes 16934400 | tf_op jit(solution)/shard_map/fast7/pallas_call | solution.py:161
  502.0 2.3 fusion.4
  504.2 16.5 %collective-permute-done.15 = f32[1176,256]{1,0:T(8,128)S(1)} collective-permute-done((f32[1176,256]{1,0:T(8,128)}, f32[1176,256]{1,0:T(8,128)S(1)}, u32[]{:S(2)}, u32[]{:S(2)}) %collective-permute-start.15) | collective-permute-done | bytes 1204256 | tf_op jit(solution)/shard_map/ppermute | solution.py:973
  520.8 13.1 %last.1 = (f32[98,96,128]{2,1,0:T(8,128)}, f32[196,96,128]{2,1,0:T(8,128)}) custom-call(s32[7]{0:T(128)} %stack.111.idx, f32[24,128]{1,0:T(8,128)} %copy-done.28, f32[2,256]{1,0:T(2,128)} %get-tuple-element.149.tot.tot_a, f32[2,256]{1,0:T(2,128)} %sum14.1.back, f32[1,256]{1,0:T(1,128)} %reshape.532.gain.gain_a, f32[2352,256]{1,0:T(8,128)} %pad_maximum_fusion.6.us, ...), custom_call_target="tpu_custom_call" | custom-call | flops 7398752256 | bytes 37632000 | tf_op jit(solution)/shard_map/last/pallas_call | solution.py:161
  534.6 2.4 constant_dynamic-update-slice_fusion.5
  542.1 11.7 %sum15.1 = f32[88,128]{1,0:T(8,128)} custom-call(f32[88,128]{1,0:T(8,128)} %pad_maximum_fusion.14.refs_0_), custom_call_target="tpu_custom_call" | custom-call | tf_op jit(solution)/shard_map/sum15/pallas_call | solution.py:251
  555.2 1.7 collective-permute-start.16
  562.2 21.5 %collective-permute-done.16 = f32[1176,256]{1,0:T(8,128)} collective-permute-done((f32[1176,256]{1,0:T(8,128)}, f32[1176,256]{1,0:T(8,128)}, u32[]{:S(2)}, u32[]{:S(2)}) %collective-permute-start.16) | collective-permute-done | bytes 1204256 | tf_op jit(solution)/shard_map/ppermute | solution.py:973
  583.7 2.4 constant_dynamic-update-slice_fusion.1
  586.1 52.1 %all-reduce.6.cloned.1.call-done = f32[64,3712]{1,0:T(8,128)} async-done(((f32[64,3712]{1,0:T(8,128)}), f32[64,3712]{1,0:T(8,128)}) %all-reduce.6.cloned.1.call-update) | async-done | bytes 950288 | tf_op jit(solution)/shard_map/psum | solution.py:1028
  643.1 5.0 constant_dynamic-update-slice_fusion
  (311 shorter events, 78.1 us)
Async XLA Ops:
  7.2 13.1 %copy-start.2 = (f32[1280,256]{1,0:T(8,128)S(1)}, f32[1280,256]{1,0:T(8,128)}, u32[]{:S(2)}) copy-start(f32[1280,256]{1,0:T(8,128)} %param.53) | copy-start | bytes 3932164
  7.2 114.1 %all-gather.12.cloned.1.call-start = ((), (), s32[]{:S(2)}) async-start(), calls=%async_computation.5 | async-start | bytes 3244032 | tf_op jit(solution)/shard_map/all_gather | solution.py:733
  9.8 210.8 %all-gather.6.cloned.1.call-start = ((), (), s32[]{:S(2)}) async-start(), calls=%async_computation | async-start | bytes 3612672 | tf_op jit(solution)/shard_map/all_gather | solution.py:821
  11.5 23.8 %collective-permute-start.2 = (f32[64,768]{1,0:T(8,128)}, f32[64,768]{1,0:T(8,128)}, u32[]{:S(2)}, u32[]{:S(2)}) collective-permute-start(f32[64,768]{1,0:T(8,128)} %get-tuple-element.407), channel_id=1, source_target_pairs={{0,2},{2,0},{1,3},{3,1},{4,6},{6,4},{5,7},{7,5},{8,10},{10,8},{9,1... | collective-permute-start | bytes 589832 | tf_op jit(solution)/shard_map/ppermute | solution.py:721
  16.2 81.5 %collective-permute-start.1 = (f32[98,8,128]{2,1,0:T(8,128)}, f32[98,8,128]{2,1,0:T(8,128)}, u32[]{:S(2)}, u32[]{:S(2)}) collective-permute-start(f32[98,8,128]{2,1,0:T(8,128)} %dynamic-slice_bitcast_fusion.8), channel_id=1, source_target_pairs={{0,4},{4,8},{8,12},{12,16},{16,20},{20,24},{24,28},{1,5},{5,9},{9,... | collective-permute-start | bytes 1204232 | tf_op jit(solution)/shard_map/ppermute | solution.py:766
  20.4 33.5 %collective-permute-start.5 = (f32[1280,256]{1,0:T(8,128)S(1)}, f32[1280,256]{1,0:T(8,128)S(1)}, u32[]{:S(2)}, u32[]{:S(2)}) collective-permute-start(f32[1280,256]{1,0:T(8,128)S(1)} %copy-done.2), channel_id=1, source_target_pairs={{0,2},{2,0},{1,3},{3,1},{4,6},{6,4},{5,7},{7,5},{8,10},{10,8},{9,1... | collective-permute-start | bytes 3932168 | tf_op jit(solution)/shard_map/ppermute | solution.py:702
  24.2 6.2 copy-start.45
  24.2 31.7 %collective-permute-start = (f32[2352,256]{1,0:T(8,128)}, f32[2352,256]{1,0:T(8,128)}, u32[]{:S(2)}, u32[]{:S(2)}) collective-permute-start(f32[2352,256]{1,0:T(8,128)} %constant_dynamic-slice_fusion.31), channel_id=1, source_target_pairs={{0,1},{1,0},{2,3},{3,2},{4,5},{5,4},{6,7},{7,6},{8,9},{9,8},{10,11... | collective-permute-start | bytes 7225352 | tf_op jit(solution)/shard_map/ppermute | solution.py:692
  27.1 10.3 %copy-start.46 = (f32[32]{0:T(128)S(1)}, f32[32]{0:T(128)}, u32[]{:S(2)}) copy-start(f32[32]{0:T(128)} %param.33) | copy-start | bytes 388
  27.1 10.9 %copy-start.47 = (f32[32]{0:T(128)S(1)}, f32[32]{0:T(128)}, u32[]{:S(2)}) copy-start(f32[32]{0:T(128)} %param.34) | copy-start | bytes 388
  27.1 11.5 %copy-start.48 = (f32[32]{0:T(128)S(1)}, f32[32]{0:T(128)}, u32[]{:S(2)}) copy-start(f32[32]{0:T(128)} %param.36) | copy-start | bytes 388
  27.1 12.1 %copy-start.49 = (f32[32]{0:T(128)S(1)}, f32[32]{0:T(128)}, u32[]{:S(2)}) copy-start(f32[32]{0:T(128)} %param.37) | copy-start | bytes 388
  27.1 12.7 %copy-start.14 = (f32[4,128,4,32]{1,0,3,2:T(4,128)S(1)}, f32[4,128,4,32]{1,0,3,2:T(4,128)}, u32[]{:S(2)}) copy-start(f32[4,128,4,32]{1,0,3,2:T(4,128)} %broadcast_multiply_fusion.1) | copy-start | bytes 786436
  29.7 14.7 %copy-start.19 = (f32[128,256]{1,0:T(8,128)}, f32[128,256]{1,0:T(8,128)S(1)}, u32[]{:S(2)}) copy-start(f32[128,256]{1,0:T(8,128)S(1)} %get-tuple-element.424) | copy-start | bytes 393220
  34.7 11.7 %copy-start.24 = (f32[24,128]{1,0:T(8,128)}, f32[24,128]{1,0:T(8,128)S(1)}, u32[]{:S(2)}) copy-start(f32[24,128]{1,0:T(8,128)S(1)} %broadcast_in_dim.36.mp.mask) | copy-start | bytes 36868
  37.0 7.3 %collective-permute-start.3 = (f32[2,64,768]{2,1,0:T(8,128)}, f32[2,64,768]{2,1,0:T(8,128)}, u32[]{:S(2)}, u32[]{:S(2)}) collective-permute-start(f32[2,64,768]{2,1,0:T(8,128)} %pad_maximum_fusion.10), channel_id=1, source_target_pairs={{0,1},{1,0},{2,3},{3,2},{4,5},{5,4},{6,7},{7,6},{8,9},{9,8},{10,11... | collective-permute-start | bytes 1179656 | tf_op jit(solution)/shard_map/ppermute | solution.py:722
  41.3 5.2 copy-start.28
  55.8 82.5 %collective-permute-start.6 = (f32[2,1280,256]{2,1,0:T(8,128)}, f32[2,1280,256]{2,1,0:T(8,128)}, u32[]{:S(2)}, u32[]{:S(2)}) collective-permute-start(f32[2,1280,256]{2,1,0:T(8,128)} %pad_maximum_fusion.3), channel_id=1, source_target_pairs={{0,1},{1,0},{2,3},{3,2},{4,5},{5,4},{6,7},{7,6},{8,9},{9,8},{10,11... | collective-permute-start | bytes 7864328 | tf_op jit(solution)/shard_map/ppermute | solution.py:707
  59.5 88.5 %collective-permute-start.4 = (f32[2352,256]{1,0:T(8,128)}, f32[2352,256]{1,0:T(8,128)}, u32[]{:S(2)}, u32[]{:S(2)}) collective-permute-start(f32[2352,256]{1,0:T(8,128)} %pad_maximum_fusion.5), channel_id=1, source_target_pairs={{0,2},{2,0},{1,3},{3,1},{4,6},{6,4},{5,7},{7,5},{8,10},{10,8},{9,1... | collective-permute-start | bytes 7225352 | tf_op jit(solution)/shard_map/ppermute | solution.py:705
  82.2 61.8 %collective-permute-start.7 = (f32[2352,256]{1,0:T(8,128)}, f32[2352,256]{1,0:T(8,128)}, u32[]{:S(2)}, u32[]{:S(2)}) collective-permute-start(f32[2352,256]{1,0:T(8,128)} %constant_dynamic-slice_fusion.20), channel_id=1, source_target_pairs={{0,1},{1,0},{2,3},{3,2},{4,5},{5,4},{6,7},{7,6},{8,9},{9,8},{10,11... | collective-permute-start | bytes 7225352 | tf_op jit(solution)/shard_map/ppermute | solution.py:692
  123.5 97.2 %all-gather.8.cloned.1.call-start = ((), (), s32[]{:S(2)}) async-start(), calls=%async_computation.1 | async-start | bytes 3612672 | tf_op jit(solution)/shard_map/all_gather | solution.py:821
  137.9 199.6 %collective-permute-start.11 = (f32[98,96,128]{2,1,0:T(8,128)}, f32[98,96,128]{2,1,0:T(8,128)}, u32[]{:S(2)}, u32[]{:S(2)}) collective-permute-start(f32[98,96,128]{2,1,0:T(8,128)} %get-tuple-element.176), channel_id=1, source_target_pairs={{0,1},{1,0},{2,3},{3,2},{4,5},{5,4},{6,7},{7,6},{8,9},{9,8},{10,11... | collective-permute-start | bytes 14450696 | tf_op jit(solution)/shard_map/ppermute | solution.py:1022
  146.3 253.4 %all-gather.10.cloned.1.call-start = ((), (), s32[]{:S(2)}) async-start(), calls=%async_computation.2 | async-start | bytes 3932160 | tf_op jit(solution)/shard_map/all_gather | solution.py:929
  246.0 74.5 %collective-permute-start.8 = (f32[1176,256]{1,0:T(8,128)}, f32[1176,256]{1,0:T(8,128)}, u32[]{:S(2)}, u32[]{:S(2)}) collective-permute-start(f32[1176,256]{1,0:T(8,128)} %get-tuple-element.170), channel_id=1, source_target_pairs={{0,1},{1,0},{2,3},{3,2},{4,5},{5,4},{6,7},{7,6},{8,9},{9,8},{10,11... | collective-permute-start | bytes 3612680 | tf_op jit(solution)/shard_map/ppermute | solution.py:898
  246.1 74.4 %collective-permute-start.9 = (f32[1176,256]{1,0:T(8,128)}, f32[1176,256]{1,0:T(8,128)}, u32[]{:S(2)}, u32[]{:S(2)}) collective-permute-start(f32[1176,256]{1,0:T(8,128)} %get-tuple-element.172), channel_id=1, source_target_pairs={{0,2},{1,3},{2,0},{3,1},{4,6},{5,7},{6,4},{7,5},{8,10},{9,11},{10,... | collective-permute-start | bytes 3612680 | tf_op jit(solution)/shard_map/ppermute | solution.py:898
  246.8 73.8 %collective-permute-start.10 = (f32[1176,256]{1,0:T(8,128)}, f32[1176,256]{1,0:T(8,128)}, u32[]{:S(2)}, u32[]{:S(2)}) collective-permute-start(f32[1176,256]{1,0:T(8,128)} %get-tuple-element.174), channel_id=1, source_target_pairs={{0,3},{1,2},{2,1},{3,0},{4,7},{5,6},{6,5},{7,4},{8,11},{9,10},{10,... | collective-permute-start | bytes 3612680 | tf_op jit(solution)/shard_map/ppermute | solution.py:898
  290.7 42.9 %copy-start.20 = (f32[128,256]{1,0:T(8,128)S(1)}, f32[128,256]{1,0:T(8,128)}, u32[]{:S(2)}) copy-start(f32[128,256]{1,0:T(8,128)} %copy-done.19) | copy-start | bytes 393220
  290.7 43.6 %copy-start.43 = (f32[2,128]{1,0:T(2,128)S(1)}, f32[2,128]{1,0:T(2,128)}, u32[]{:S(2)}) copy-start(f32[2,128]{1,0:T(2,128)} %get-tuple-element.136.tot.tot1) | copy-start | bytes 3076
  290.7 43.6 %copy-start.36 = (f32[2,128]{1,0:T(2,128)S(1)}, f32[2,128]{1,0:T(2,128)}, u32[]{:S(2)}) copy-start(f32[2,128]{1,0:T(2,128)} %sum2.1.tot.tot2) | copy-start | bytes 3076
  290.7 43.7 %copy-start.33 = (f32[2,512]{1,0:T(2,128)S(1)}, f32[2,512]{1,0:T(2,128)}, u32[]{:S(2)}) copy-start(f32[2,512]{1,0:T(2,128)} %get-tuple-element.146.tot) | copy-start | bytes 12292
  290.7 45.1 %copy-start.34 = (f32[2,256]{1,0:T(2,128)S(1)}, f32[2,256]{1,0:T(2,128)}, u32[]{:S(2)}) copy-start(f32[2,256]{1,0:T(2,128)} %get-tuple-element.149.tot.tot_a) | copy-start | bytes 6148
  290.7 45.1 %copy-start.37 = (f32[2,512]{1,0:T(2,128)S(1)}, f32[2,512]{1,0:T(2,128)}, u32[]{:S(2)}) copy-start(f32[2,512]{1,0:T(2,128)} %get-tuple-element.216.back) | copy-start | bytes 12292
  290.7 46.2 %copy-start.29 = (f32[2,1280]{1,0:T(2,128)S(1)}, f32[2,1280]{1,0:T(2,128)}, u32[]{:S(2)}) copy-start(f32[2,1280]{1,0:T(2,128)} %get-tuple-element.154.tot.tot_s.tot_f) | copy-start | bytes 30724
  290.7 46.2 %copy-start.35 = (f32[2,256]{1,0:T(2,128)S(1)}, f32[2,256]{1,0:T(2,128)}, u32[]{:S(2)}) copy-start(f32[2,256]{1,0:T(2,128)} %sum9.1.tot.tot_m) | copy-start | bytes 6148
  290.8 46.7 %copy-start.25 = (f32[2,1024]{1,0:T(2,128)S(1)}, f32[2,1024]{1,0:T(2,128)}, u32[]{:S(2)}) copy-start(f32[2,1024]{1,0:T(2,128)} %sum10.1.tot_l) | copy-start | bytes 24580
  333.3 10.5 %collective-permute-start.12 = (f32[2,1280,256]{2,1,0:T(8,128)S(1)}, f32[2,1280,256]{2,1,0:T(8,128)}, u32[]{:S(2)}, u32[]{:S(2)}) collective-permute-start(f32[2,1280,256]{2,1,0:T(8,128)S(1)} %pad_maximum_fusion.4), channel_id=1, source_target_pairs={{0,1},{1,0},{2,3},{3,2},{4,5},{5,4},{6,7},{7,6},{8,9},{9,8},{10,11... | collective-permute-start | bytes 7864328 | tf_op jit(solution)/shard_map/ppermute | solution.py:925
  334.5 186.3 %collective-permute-start.21 = (f32[7,14,256]{2,1,0:T(8,128)}, f32[7,14,256]{2,1,0:T(8,128)}, u32[]{:S(2)}, u32[]{:S(2)}) collective-permute-start(f32[7,14,256]{2,1,0:T(8,128)} %get-tuple-element.213), channel_id=1, source_target_pairs={{4,0},{8,4},{12,8},{16,12},{20,16},{24,20},{28,24},{5,1},{9,5},{13... | collective-permute-start | bytes 301064 | tf_op jit(solution)/shard_map/ppermute | solution.py:830
  337.5 5.1 copy-start.26
  337.5 6.3 copy-start.6
  337.5 6.3 copy-start.7
  342.6 305.5 %copy-start.38 = (f32[1,256]{1,0:T(1,128)}, f32[1,256]{1,0:T(1,128)S(1)}, u32[]{:S(2)}) copy-start(f32[1,256]{1,0:T(1,128)S(1)} %constant_dynamic-slice_fusion.14) | copy-start | bytes 3076
  347.1 157.1 %all-reduce.4.cloned.1.call-start = ((), (), s32[]{:S(2)}) async-start(), calls=%async_computation.3 | async-start | bytes 2621440 | tf_op jit(solution)/shard_map/psum | solution.py:949
  347.1 26.5 %copy-start.42 = (f32[2,256]{1,0:T(2,128)S(1)}, f32[2,256]{1,0:T(2,128)}, u32[]{:S(2)}) copy-start(f32[2,256]{1,0:T(2,128)} %get-tuple-element.186.back) | copy-start | bytes 6148
  410.6 32.5 %collective-permute-start.20 = (f32[7,7,256]{2,1,0:T(8,128)}, f32[7,7,256]{2,1,0:T(8,128)S(1)}, u32[]{:S(2)}, u32[]{:S(2)}) collective-permute-start(f32[7,7,256]{2,1,0:T(8,128)} %get-tuple-element.212), channel_id=1, source_target_pairs={{4,2},{6,0},{8,6},{10,4},{12,10},{14,8},{16,14},{18,12},{20,18},{2... | collective-permute-start | bytes 150536 | tf_op jit(solution)/shard_map/ppermute | solution.py:956
  411.9 31.2 %collective-permute-start.19 = (f32[7,7,256]{2,1,0:T(8,128)}, f32[7,7,256]{2,1,0:T(8,128)}, u32[]{:S(2)}, u32[]{:S(2)}) collective-permute-start(f32[7,7,256]{2,1,0:T(8,128)} %get-tuple-element.212), channel_id=1, source_target_pairs={{4,0},{8,4},{12,8},{16,12},{20,16},{24,20},{28,24},{5,1},{9,5},{13... | collective-permute-start | bytes 150536 | tf_op jit(solution)/shard_map/ppermute | solution.py:955
  415.8 9.3 %copy-start.8 = (f32[1176,256]{1,0:T(8,128)S(1)}, f32[1176,256]{1,0:T(8,128)}, u32[]{:S(2)}) copy-start(f32[1176,256]{1,0:T(8,128)} %get-tuple-element.210.us) | copy-start | bytes 3612676
  415.8 9.8 %copy-start.13 = (f32[256,1280]{1,0:T(8,128)S(1)}, f32[256,1280]{1,0:T(8,128)}, u32[]{:S(2)}) copy-start(f32[256,1280]{1,0:T(8,128)} %get-tuple-element.202) | copy-start | bytes 3932164
  415.8 9.8 %copy-start.18 = (f32[256,768]{1,0:T(8,128)S(1)}, f32[256,768]{1,0:T(8,128)}, u32[]{:S(2)}) copy-start(f32[256,768]{1,0:T(8,128)} %get-tuple-element.203) | copy-start | bytes 2359300
  415.8 222.3 %all-reduce.6.cloned.1.call-start = ((), (), s32[]{:S(2)}) async-start(), calls=%async_computation.4 | async-start | bytes 1900544 | tf_op jit(solution)/shard_map/psum | solution.py:1028
  415.9 9.7 %copy-start.16 = (f32[256,1024]{1,0:T(8,128)S(1)}, f32[256,1024]{1,0:T(8,128)}, u32[]{:S(2)}) copy-start(f32[256,1024]{1,0:T(8,128)} %get-tuple-element.204) | copy-start | bytes 3145732
  425.1 27.7 %collective-permute-start.18 = (f32[1176,256]{1,0:T(8,128)S(1)}, f32[1176,256]{1,0:T(8,128)}, u32[]{:S(2)}, u32[]{:S(2)}) collective-permute-start(f32[1176,256]{1,0:T(8,128)S(1)} %copy-done.8), channel_id=1, source_target_pairs={{0,2},{2,0},{1,3},{3,1},{4,6},{6,4},{5,7},{7,5},{8,10},{10,8},{9,1... | collective-permute-start | bytes 3612680 | tf_op jit(solution)/shard_map/ppermute | solution.py:953
  429.9 38.3 %collective-permute-start.14 = (f32[2,64,3712]{2,1,0:T(8,128)}, f32[2,64,3712]{2,1,0:T(8,128)}, u32[]{:S(2)}, u32[]{:S(2)}) collective-permute-start(f32[2,64,3712]{2,1,0:T(8,128)} %pad_maximum_fusion.7), channel_id=1, source_target_pairs={{0,1},{1,0},{2,3},{3,2},{4,5},{5,4},{6,7},{7,6},{8,9},{9,8},{10,11... | collective-permute-start | bytes 5701640 | tf_op jit(solution)/shard_map/ppermute | solution.py:925
  471.0 30.9 %collective-permute-start.17 = (f32[64,3712]{1,0:T(8,128)}, f32[64,3712]{1,0:T(8,128)}, u32[]{:S(2)}, u32[]{:S(2)}) collective-permute-start(f32[64,3712]{1,0:T(8,128)} %slice_bitcast_fusion), channel_id=1, source_target_pairs={{0,2},{2,0},{1,3},{3,1},{4,6},{6,4},{5,7},{7,5},{8,10},{10,8},{9,1... | collective-permute-start | bytes 2850824 | tf_op jit(solution)/shard_map/ppermute | solution.py:971
  491.9 28.9 %collective-permute-start.15 = (f32[1176,256]{1,0:T(8,128)}, f32[1176,256]{1,0:T(8,128)S(1)}, u32[]{:S(2)}, u32[]{:S(2)}) collective-permute-start(f32[1176,256]{1,0:T(8,128)} %get-tuple-element.206), channel_id=1, source_target_pairs={{0,2},{1,3},{2,0},{3,1},{4,6},{5,7},{6,4},{7,5},{8,10},{9,11},{10,... | collective-permute-start | bytes 3612680 | tf_op jit(solution)/shard_map/ppermute | solution.py:973
  520.8 13.2 %copy-start.40 = (f32[1,256]{1,0:T(1,128)S(1)}, f32[1,256]{1,0:T(1,128)}, u32[]{:S(2)}) copy-start(f32[1,256]{1,0:T(1,128)} %get-tuple-element.449) | copy-start | bytes 3076
  520.8 13.2 %copy-start.41 = (f32[1,256]{1,0:T(1,128)S(1)}, f32[1,256]{1,0:T(1,128)}, u32[]{:S(2)}) copy-start(f32[1,256]{1,0:T(1,128)} %get-tuple-element.447) | copy-start | bytes 3076
  533.9 5.7 copy-start.22
  533.9 5.9 copy-start.23
  533.9 109.3 %collective-permute-start.22 = (f32[98,96,128]{2,1,0:T(8,128)}, f32[98,96,128]{2,1,0:T(8,128)}, u32[]{:S(2)}, u32[]{:S(2)}) collective-permute-start(f32[98,96,128]{2,1,0:T(8,128)} %get-tuple-element.231), channel_id=1, source_target_pairs={{0,1},{1,0},{2,3},{3,2},{4,5},{5,4},{6,7},{7,6},{8,9},{9,8},{10,11... | collective-permute-start | bytes 14450696 | tf_op jit(solution)/shard_map/ppermute | solution.py:1022
  534.6 5.7 copy-start.39
  537.1 23.0 %collective-permute-start.13 = (f32[1176,256]{1,0:T(8,128)}, f32[1176,256]{1,0:T(8,128)S(1)}, u32[]{:S(2)}, u32[]{:S(2)}) collective-permute-start(f32[1176,256]{1,0:T(8,128)} %get-tuple-element.200), channel_id=1, source_target_pairs={{0,1},{1,0},{2,3},{3,2},{4,5},{5,4},{6,7},{7,6},{8,9},{9,8},{10,11... | collective-permute-start | bytes 3612680 | tf_op jit(solution)/shard_map/ppermute | solution.py:973
  555.2 28.5 %collective-permute-start.16 = (f32[1176,256]{1,0:T(8,128)}, f32[1176,256]{1,0:T(8,128)}, u32[]{:S(2)}, u32[]{:S(2)}) collective-permute-start(f32[1176,256]{1,0:T(8,128)} %get-tuple-element.208), channel_id=1, source_target_pairs={{0,3},{1,2},{2,1},{3,0},{4,7},{5,6},{6,5},{7,4},{8,11},{9,10},{10,... | collective-permute-start | bytes 3612680 | tf_op jit(solution)/shard_map/ppermute | solution.py:973
  643.1 5.6 copy-start.12
  643.1 6.7 %copy-start.1 = (f32[5,128,64]{1,2,0:T(8,128)S(1)}, f32[5,128,64]{1,2,0:T(8,128)}, u32[]{:S(2)}) copy-start(f32[5,128,64]{1,2,0:T(8,128)} %param.41) | copy-start | bytes 491524
  (15 other events, 47.7 us)
Sparse Core Ops, SparseCore 0:
  11.0 63.6 all-gather.11
  123.6 35.2 all-gather.5
  161.0 37.5 all-gather.7
  347.2 39.5 all-gather.9
  415.9 85.6 all-reduce.3
  559.6 78.4 all-reduce.5

commit v2 on v1

--- a/solution.py
+++ b/solution.py
@@ -143,7 +143,7 @@
 
 
 def cost(flops, nbytes):
-    return pl.CostEstimate(flops=int(2 * flops), bytes_accessed=int(2 * nbytes), transcendentals=0)
+    return pl.CostEstimate(flops=int(flops / 2), bytes_accessed=int(nbytes / 2), transcendentals=0)
 
 
 def whole(x):
@@ -265,6 +265,75 @@
     )(*xs, *rims)
 
 
+def last_sum_kernel(sizes, x_ref, v_ref, o_ref, w_ref, two_src, b1, b2, vb, s1, r1, s2, r2, s3, r3, s4, r4):
+    dps, ys, hs = sizes
+    d = lax.axis_index("dp")
+    h = lax.axis_index("hh")
+
+    def along(i):
+        return lax.rem(d + i, dps)
+
+    def send(src, dst, ssem, rsem, to):
+        c = pltpu.make_async_remote_copy(
+            src_ref=src, dst_ref=dst, send_sem=ssem, recv_sem=rsem, device_id=to, device_id_type=MESH
+        )
+        c.start()
+        return c
+
+    bar = pltpu.get_barrier_semaphore()
+    other = {"hh": lax.rem(h + 1, hs)}
+    pl.semaphore_signal(bar, inc=1, device_id=other, device_id_type=MESH)
+    for i in range(1, dps):
+        pl.semaphore_signal(bar, inc=1, device_id={"dp": along(i)}, device_id_type=MESH)
+    pl.semaphore_wait(bar, dps)
+    one = send(x_ref, b1, s1, r1, other)
+    out = [
+        send(v_ref.at[along(i)], vb.at[i - 1], s3.at[i - 1], r3.at[i - 1], {"dp": along(i)})
+        for i in range(1, dps)
+    ]
+    one.wait_recv()
+    acc = x_ref[...] + b1[...]
+    two_src[...] = acc
+    two = [send(two_src, b2.at[i - 1], s2.at[i - 1], r2.at[i - 1], {"dp": along(i)}) for i in range(1, dps)]
+    piece = v_ref[d]
+    for i, c in enumerate(out):
+        c.wait_recv()
+        piece = piece + vb[i]
+    w_ref[d] = piece
+    back = [
+        send(w_ref.at[d], w_ref.at[d], s4.at[i - 1], r4.at[i - 1], {"dp": along(i)}) for i in range(1, dps)
+    ]
+    for i, c in enumerate(two):
+        c.wait_recv()
+        acc = acc + b2[i]
+    o_ref[...] = acc
+    for c in back:
+        c.wait_recv()
+    one.wait_send()
+    for c in out + two + back:
+        c.wait_send()
+
+
+def last_total(x, v, cid, sizes):
+    dps, ys, hs = sizes
+    dma = pltpu.SemaphoreType.DMA
+    return pl.pallas_call(
+        functools.partial(last_sum_kernel, sizes),
+        name="sum%d" % cid,
+        out_shape=[shape(*x.shape), shape(*v.shape)],
+        in_specs=[vmem()] * 2,
+        out_specs=[vmem()] * 2,
+        scratch_shapes=[
+            pltpu.VMEM(x.shape, F32),
+            pltpu.VMEM(x.shape, F32),
+            pltpu.VMEM((dps - 1,) + x.shape, F32),
+            pltpu.VMEM((dps - 1,) + v.shape[1:], F32),
+            dma, dma,
+        ] + [dma((dps - 1,))] * 6,
+        compiler_params=pltpu.CompilerParams(collective_id=cid, has_side_effects=True),
+    )(x, v)
+
+
 def fast1_kernel(frames, idx, x_ref, rh, rl, p_ref, e0, e1, st, tmp):
     p = dot3(split(frames_of(x_ref)), (rh[...], rl[...]))
     p_ref[...] = p
@@ -703,39 +772,34 @@
     in_core = from_core(slow_x)
     in_send = jnp.concatenate(for_partner(slow_x, in_core), axis=0)
     in_y = lax.ppermute(in_send, "yy", swap)
-    sho_core = jnp.stack([shortcut_conv, sho_y])
-    sho_other = lax.ppermute(sho_core, "hh", swap)
-    sho_all = jnp.stack([sho_core[0], sho_other[0], sho_core[1], sho_other[1]])
-    sho_h, sho_l = weight_split(
-        jnp.stack([lax.dynamic_index_in_dim(sho_all, p, 0, keepdims=False) for p in peers])
-    )
 
     vectors = [
         lateral_gain, lateral_bias, slow_reduce_gain, slow_reduce_bias, slow_temporal_gain,
         slow_temporal_bias, slow_expand_gain, slow_expand_bias, shortcut_gain, shortcut_bias,
     ]
     vector = jnp.concatenate(vectors)
-    across = -(-vector.shape[0] // (shard_rows * 128)) * 128
-    vector = jnp.pad(vector, (0, shard_rows * across - vector.shape[0])).reshape(shard_rows, across)
-    piece = jnp.concatenate([lateral_conv.transpose(2, 0, 1).reshape(shard_rows, -1), vector], axis=1)
-    column = jnp.stack([piece, lax.ppermute(piece, "yy", swap)])
-    other = lax.ppermute(column, "hh", swap)
-    table = jnp.stack([column[0], other[0], column[1], other[1]])
-    table = jnp.stack([lax.dynamic_index_in_dim(table, p, 0, keepdims=False) for p in peers])
+    share = shard_rows // dps
+    across = -(-vector.shape[0] // (share * 128)) * 128
+    vector = jnp.pad(vector, (0, share * across - vector.shape[0])).reshape(share, across)
+    piece = jnp.concatenate(
+        [
+            lateral_conv.transpose(2, 0, 1).reshape(shard_rows, -1),
+            slow_reduce.T,
+            slow_temporal.transpose(2, 0, 1).reshape(shard_rows, -1),
+            slow_expand,
+        ],
+        axis=1,
+    )
+    piece = jnp.concatenate([lax.dynamic_slice_in_dim(piece, d * share, share, axis=0), vector], axis=1)
+    got = lax.all_gather(piece, ALL, axis=0, tiled=False).reshape((dps, roles) + piece.shape)
+    matrix = got[:, :, :, : piece.shape[1] - across].transpose(1, 0, 2, 3).reshape(inner, -1)
     taps = lateral_conv.shape[0] * lateral_conv.shape[1]
-    lat_h, lat_l = weight_split(table[:, :, 0:taps].reshape(inner, taps))
-    vector = table[:, :, taps:].reshape(roles, -1)
-    share = shard_rows // dps
-    piece = jnp.concatenate(
-        [slow_reduce.T, slow_temporal.transpose(2, 0, 1).reshape(shard_rows, -1), slow_expand], axis=1
-    )
-    piece = lax.dynamic_slice_in_dim(piece, d * share, share, axis=0)
-    got = lax.all_gather(piece, ALL, axis=0, tiled=False).reshape((dps, roles) + piece.shape)
-    matrix = got.transpose(1, 0, 2, 3).reshape(inner, -1)
-    bounds = [0, joined_width, joined_width + 3 * inner, joined_width + 3 * inner + wide]
-    (red_h, red_l), (tem_h, tem_l), (exp_h, exp_l) = [
-        weight_split(matrix[:, bounds[k] : bounds[k + 1]]) for k in range(3)
+    bounds = [0, taps, taps + joined_width, taps + joined_width + 3 * inner]
+    bounds.append(bounds[-1] + wide)
+    (lat_h, lat_l), (red_h, red_l), (tem_h, tem_l), (exp_h, exp_l) = [
+        weight_split(matrix[:, bounds[k] : bounds[k + 1]]) for k in range(4)
     ]
+    vector = got[0, :, :, piece.shape[1] - across :].reshape(roles, -1)
     full = []
     start = 0
     for v in vectors:
@@ -806,6 +870,7 @@
         scratch=[cut(fr, 128)],
         est=cost(2 * 3 * nf * 512 * 256, nf * 640 * 4),
     )
+    st_f1 = st
     tot_f1, before, beyond = total([st], 1, sizes, core, (e1, e0))
     a1, z1, p2, st = stepped(
         functools.partial(fast2_kernel, fast_number, frames), "fast2", steps, [],
@@ -816,6 +881,14 @@
         est=cost(2 * 3 * nf * 256 * 256, 4 * nf * 128 * 4),
     )
     (tot_f2,) = total([st], 2, sizes, core)
+
+    def role_table(mine, from_y, event):
+        column = jnp.stack([after(mine, event), from_y])
+        other = lax.ppermute(column, "hh", swap)
+        table = jnp.stack([column[0], other[0], column[1], other[1]])
+        return jnp.stack([lax.dynamic_index_in_dim(table, p, 0, keepdims=False) for p in peers])
+
+    sho_h, sho_l = weight_split(role_table(shortcut_conv, sho_y, tot_f1))
     cot_core = from_core(after(slow_c, tot_f1))
     slow_cot = [cot_core] + [
         lax.all_gather(after(v, matrix), "yy", axis=0, tiled=True) for v in for_partner(slow_c, cot_core)
@@ -895,7 +968,9 @@
         est=cost(2 * 3 * ns * 1024 * 256, ns * 4 * 4352),
     )
     (back_ls,) = total([st], 11, sizes, ROLE)
-    sent = [lax.ppermute(after(outs[r], back_ls), ROLE, role_pairs(r)) for r in range(1, roles)]
+    near_rows = lax.ppermute(outs[1], "hh", swap)
+    far_rows = lax.ppermute(outs[3], "hh", swap)
+    from_y = [lax.all_gather(v, "yy", axis=0, tiled=False) for v in (outs[2], far_rows)]
 
     dx, short_grads = stepped(
         functools.partial(slow6_kernel, number), "slow6", steps, [],
@@ -914,8 +989,8 @@
         scratch=[cut(sr, inner)],
         est=cost(2 * 9 * ns * 1024 * 256, ns * 4 * 1800),
     )
-    slow_output = placed(outs[0], sent)
-    back_m, before, beyond = total([after(st, *sent)], 12, sizes, ROLE, (e1, e0))
+    slow_out = outs[0]
+    back_m, before, beyond = total([st], 12, sizes, ROLE, (e1, e0))
     def by_peer(g):
         rows = g.shape[0] // roles
         parts = [lax.dynamic_slice_in_dim(g, p * rows, rows, axis=0) for p in peers]
@@ -924,9 +999,10 @@
     def chip_sum(near, far):
         return near + lax.ppermute(far, "hh", swap)
 
-    near, far = by_peer(short_grads.reshape(roles * joined_width, lanes))
-    short_both = chip_sum(near, after(far, back_m))
-    short_got = lax.all_gather(short_both[1], "yy", axis=0, tiled=False)
+    expand_pair = lax.psum_scatter(
+        after(expand_grad, *from_y).reshape(roles, shard_rows, wide), ROLE, scatter_dimension=0, tiled=False
+    )
+    short_pair = lax.psum_scatter(after(short_grads, *from_y), ROLE, scatter_dimension=0, tiled=False)
     uf, temporal_grad, st = stepped(
         functools.partial(slow7_kernel, number, frames), "slow7", steps, [],
         wide_masks + all_of(tot_m, back_m, tem_gain, tot_s, red_gain, red_bias)
@@ -945,10 +1021,8 @@
         scratch=[tmp(sr, joined_width), cut(sr, inner)],
         est=cost(2 * 6 * ns * 1280 * 256, ns * 4 * 5000),
     )
-    (back_a,) = total([after(st, short_got)], 14, sizes, ROLE)
-    shortcut_sum = lax.psum(
-        short_both[0] + lax.dynamic_index_in_dim(short_got, 1 - y, 0, keepdims=False), "dp"
-    )
+    (back_a,) = total([st], 14, sizes, ROLE)
+    shortcut_sum, expand_sum = lax.psum((short_pair, expand_pair), "dp")
     us_sent = after(us, back_a)
     us_other = lax.ppermute(us_sent, "yy", swap)
     edge_sent = after(us_edge, back_a)
@@ -967,17 +1041,11 @@
         est=cost(2 * 3 * ns * 640 * 256, ns * 4 * 1500),
     )
 
-    both = chip_sum(*by_peer(jnp.concatenate([reduce_grad, temporal_grad, expand_grad, lateral_grad], axis=1)))
-    rest = both[0] + lax.ppermute(both[1], "yy", swap)
-    grads_sent = [
-        lax.ppermute(after(outs[r], back_a if r == 1 else both), ROLE, role_pairs(r))
-        for r in range(1, roles)
-    ]
-    slow_input_gradient = placed(outs[0], grads_sent)
-
+    both = chip_sum(*by_peer(jnp.concatenate([lateral_grad, reduce_grad, temporal_grad], axis=1)))
+    rest_y = lax.ppermute(both[1], "yy", swap)
     u2, expand_packed, e0, e1, st = stepped(
         functools.partial(fast5_kernel, fast_number, frames), "fast5", steps, [],
-        all_of(tot_f3, after(back_f3, back_a, lateral_grad), fe_gain, tot_f2, ft_gain, ft_bias)
+        all_of(tot_f3, after(back_f3, back_a, both, short_pair, expand_pair), fe_gain, tot_f2, ft_gain, ft_bias)
         + [by_block(u3), by_block(b1), by_block(p2)] + all_of(fe_h, fe_l),
         [
             out_rows(fr, 128), const(128, 512), out_blocks(2, half_block, 128),
@@ -986,10 +1054,17 @@
         scratch=[cut(fr, 128)],
         est=cost(2 * 9 * nf * 256 * 512, nf * 900 * 4),
     )
-    back_f2, before, beyond = total([after(st, us_other)], 5, sizes, core, (e1, e0))
+    rest = both[0] + after(rest_y, u2)
+    back_f2, before, beyond = total([st], 5, sizes, core, (e1, e0))
+    grads_sent = [
+        lax.ppermute(after(outs[r], back_a if r == 1 else rest), ROLE, role_pairs(r))
+        for r in range(1, roles)
+    ]
+    slow_input_gradient = placed(outs[0], grads_sent)
+
     u1, temporal_packed, st = stepped(
         functools.partial(fast6_kernel, fast_number, frames), "fast6", steps, [],
-        masks + all_of(tot_f2, back_f2, ft_gain, tot_f1, fr_gain, fr_bias)
+        masks + all_of(tot_f2, after(back_f2, rest), ft_gain, tot_f1, fr_gain, fr_bias)
         + [by_block(x) for x in (u2, p2, before, beyond, a1, z1, p1)] + all_of(fb_h, fb_l),
         [out_rows(fr, 128), const(256, 128), const(2, 128)],
         scratch=[cut(fr, 128)] * 2,
@@ -998,38 +1073,13 @@
     (back_f1,) = total([st], 6, sizes, core)
     g1, reduce_packed = stepped(
         functools.partial(fast7_kernel, fast_number), "fast7", steps, [idx],
-        all_of(tot_f1, back_f1, fr_gain) + [fx, by_block(u1), by_block(p1)],
+        all_of(tot_f1, after(back_f1, us_other), fr_gain) + [fx, by_block(u1), by_block(p1)],
         [out_rows(fr, 128), const(512, 128)],
         est=cost(2 * 3 * nf * 512 * 256, nf * 900 * 4),
     )
 
     def in_order(mine, other):
         return jnp.concatenate([jnp.where(y == 0, mine, other), jnp.where(y == 0, other, mine)], axis=0)
-
-    us_half = in_order(us, us_other)
-    rim = in_order(edge_same.reshape(own, inner), edge_cross.reshape(own, inner))
-    grad_half, grad_full = stepped(
-        functools.partial(last_kernel, number, frames), "last", steps, [idx],
-        all_of(mask_next, tot_a, after(back_a, rest, grads_sent[1], shortcut_sum), lat_gain)
-        + [by_block(x) for x in (us_half, side, rim.reshape(steps, half_block, inner), side_edge, u3, g1)]
-        + all_of(lat_h, lat_l, fr_h, fr_l),
-        [by_block(half_out), (full_out, part(full_out, half_block, in_half))],
-        scratch=[cut(fr, inner)],
-        est=cost(2 * 3 * nf * 1024 * 256, nf * 4 * 2000),
-    )
-
-    def fast_whole(mine, full):
-        got = lax.ppermute(mine, "hh", swap)
-        return by_pixel(lax.dynamic_update_slice_in_dim(full, got, half * (1 - h), axis=0))
-
-    fast_output = fast_whole(fast_half, fast_full)
-    fast_input_gradient = fast_whole(grad_half, grad_full)
-
-    rest = lax.psum(after(rest, shortcut_sum), "dp")
-    reduce_sum = rest[:, 0:joined_width].T
-    expand_sum = rest[:, joined_width + 3 * inner : joined_width + 3 * inner + wide]
-    lateral_sum = rest[:, joined_width + 3 * inner + wide :].reshape(shard_rows, -1, 128).transpose(1, 2, 0)
-    temporal_sum = rest[:, joined_width : joined_width + 3 * inner].reshape(shard_rows, 3, inner).transpose(1, 2, 0)
 
     eb = expand_packed.reshape(4, 32, 4, 128)
     expand_small = eb[0, :, 0] + eb[1, :, 1] + eb[2, :, 2] + eb[3, :, 3]
@@ -1042,7 +1092,31 @@
     small = jnp.concatenate(
         [expand_small, reduce_small.reshape(32, 128), jnp.stack([tap0, tap1, tap2]).reshape(24, 128)], axis=0
     )
-    (small,) = total([small], 15, sizes, core)
+    small, rest = last_total(small, rest.reshape(dps, -1, rest.shape[1]), 15, sizes)
+    rest = rest.reshape(shard_rows, -1)
+    lateral_sum = rest[:, 0:taps].reshape(shard_rows, -1, 128).transpose(1, 2, 0)
+    reduce_sum = rest[:, taps : taps + joined_width].T
+    temporal_sum = rest[:, taps + joined_width :].reshape(shard_rows, 3, inner).transpose(1, 2, 0)
+    us_half = in_order(us, after(us_other, g1))
+    rim = in_order(edge_same.reshape(own, inner), edge_cross.reshape(own, inner))
+    grad_half, grad_full = stepped(
+        functools.partial(last_kernel, number, frames), "last", steps, [idx],
+        all_of(mask_next, tot_a, after(back_a, grads_sent[1], grads_sent[2], shortcut_sum, small), lat_gain)
+        + [by_block(x) for x in (us_half, side, rim.reshape(steps, half_block, inner), side_edge, u3, g1)]
+        + all_of(lat_h, lat_l, fr_h, fr_l),
+        [by_block(half_out), (full_out, part(full_out, half_block, in_half))],
+        scratch=[cut(fr, inner)],
+        est=cost(2 * 3 * nf * 1024 * 256, nf * 4 * 2000),
+    )
+
+    def fast_whole(mine, full):
+        got = lax.ppermute(mine, "hh", swap)
+        return by_pixel(lax.dynamic_update_slice_in_dim(full, got, half * (1 - h), axis=0))
+
+    from_y = [lax.dynamic_index_in_dim(v, 1 - y, 0, keepdims=False) for v in from_y]
+    slow_output = placed(after(slow_out, small), [near_rows] + from_y)
+    fast_output = fast_whole(fast_half, after(fast_full, grad_half))
+    fast_input_gradient = fast_whole(grad_half, grad_full)
 
     def fold(v):
         return jnp.sum(v.reshape(4, -1), axis=0)

time: 662 us -> 594 us (0.90)
  waiting for transfers between devices: 98.4 us -> 12.8 us
  Pallas kernels: 388 us -> 430 us
  local copies, waits for them, and re-layouts: 85.3 us -> 74.2 us
  other arithmetic: 47.9 us -> 38.7 us
    pallas_call x0 -> x1, Pallas kernels: none -> 57.3 us  [last_total(): pl.pallas_call(functools.partial(last_sum_kernel, sizes), name='sum%d' %...]
    psum x2 -> x1, waiting for transfers between devices: 52.1 us -> 0.02 us  [local(): shortcut_sum, expand_sum = lax.psum((short_pair, expand_pair), 'dp')]
    ppermute x10 -> x7, waiting for transfers between devices: 38 us -> 4.92 us  [the longest x1 3.08 us: local(): far_rows = lax.ppermute(outs[3], 'hh', swap)]
    pallas_call x18, Pallas kernels: 249 us -> 239 us  [stepped(): pl.pallas_call(body, name=name, out_shape=[o for o, _ in outs], grid_spec...]
    ppermute x1, waiting for transfers between devices: 8.12 us -> 0.01 us  [local(): us_other = lax.ppermute(us_sent, 'yy', swap)]
    unnamed x113 -> x118, local copies, waits for them, and re-layouts: 8.35 us -> 16 us
    ppermute x10 -> x7, starting transfers between devices: 9.66 us -> 2.29 us  [the longest x3 1.77 us: local(): lax.ppermute(after(outs[r], back_a if r == 1 else rest), ROLE, role_pairs...]
    pallas_call x13 -> x12, Pallas kernels: 139 us -> 134 us  [total(): pl.pallas_call(functools.partial(sum_kernel, sizes, axes, widths, len(rim...]
  transfers between devices with their start and end apart: 29 -> 27, of which waited for: 4 -> 4; matrix products, arithmetic and copies ran while one was open for 19% -> 17% of each run, Pallas kernels for 57% -> 71%
where the time goes in v2:
time: 594 us; the launch traced here: 589 us
  Pallas kernels  430 us (72%)
  local copies, waits for them, and re-layouts  74.2 us (12%)
  other arithmetic  38.7 us (7%)
  starting transfers between devices  17.5 us (3%)
  between operations  15.4 us (3%)
  waiting for transfers between devices  12.8 us (2%)
    pallas_call x18, Pallas kernels, stepped(): pl.pallas_call(body, name=name, out_shape=[o for o, _ in outs], grid_spec...  239 us
    pallas_call x12, Pallas kernels, total(): pl.pallas_call(functools.partial(sum_kernel, sizes, axes, widths, len(rim...  134 us
    pallas_call x1, Pallas kernels, last_total(): pl.pallas_call(functools.partial(last_sum_kernel, sizes), name='sum%d' %...  57.3 us
    unnamed x118, local copies, waits for them, and re-layouts  16 us
    convert_element_type x9, other arithmetic, weight_split(): return (high.astype(BF16), (w - high).astype(BF16))  15.8 us
  transfers between devices with their start and end apart: 27, of which 4 were waited for; matrix products, arithmetic and copies ran while one was open for 17% of the time, Pallas kernels for 71%

profile of v2, /device:TPU:0, one launch (start us, length us, event | category | flops | bytes accessed | tf_op | source)
XLA Modules:
  0.0 588.7 jit_solution(7914735336297041540)
XLA Ops:
  10.7 3.4 constant_dynamic-slice_fusion.27
  14.6 1.8 dynamic-slice_bitcast_fusion.4
  16.3 4.4 collective-permute-start.1
  20.7 1.6 collective-permute-start.3
  25.4 1.4 constant_dynamic-slice_fusion.26
  26.8 1.6 pad_maximum_fusion.4
  29.2 1.7 fusion.6
  30.9 8.0 %fast1.1 = (f32[2352,128]{1,0:T(8,128)}, f32[7,14,128]{2,1,0:T(8,128)}, f32[7,14,128]{2,1,0:T(8,128)}, f32[2,128]{1,0:T(2,128)}) custom-call(s32[7]{0:T(128)} %stack.74.idx, f32[196,96,128]{2,1,0:T(8,128)} %bitcast.163, bf16[512,128]{1,0:T(8,128)(2,1)} %get-tuple-element.375.rh, bf16[512,128]{1,0:T(8,128)(2,1)} %get-tuple-element.374.rl), custom_call_target="tpu_custom_call" | custom-call | flops 924844032 | bytes 3010560 | tf_op jit(solution)/shard_map/fast1/pallas_call | solution.py:161
  38.9 9.9 %sum1.1 = (f32[2,128]{1,0:T(2,128)}, f32[7,14,128]{2,1,0:T(8,128)}, f32[7,14,128]{2,1,0:T(8,128)}) custom-call(f32[2,128]{1,0:T(2,128)} %get-tuple-element.136.refs_0_, f32[7,14,128]{2,1,0:T(8,128)} %get-tuple-element.137.refs_1_, f32[7,14,128]{2,1,0:T(8,128)} %get-tuple-element.138.refs_2_), custom_call_target="tpu_custom_call" | custom-call | tf_op jit(solution)/shard_map/sum1/pallas_call | solution.py:251
  48.8 5.7 collective-permute-done.3
  54.5 1.8 pad_maximum_fusion.3
  56.5 3.3 constant_dynamic-slice_fusion.20
  68.0 2.4 constant_dynamic-slice_fusion.19
  70.3 1.5 collective-permute-start.2
  71.8 7.0 %fast2.1 = (f32[2352,128]{1,0:T(8,128)}, f32[2352,128]{1,0:T(8,128)}, f32[2352,128]{1,0:T(8,128)}, f32[2,128]{1,0:T(2,128)}) custom-call(f32[24,128]{1,0:T(8,128)} %copy-done.18, f32[24,128]{1,0:T(8,128)} %copy-done.21, f32[2,128]{1,0:T(2,128)} %get-tuple-element.139.tot.tot1, f32[1,128]{1,0:T(1,128)} %tile.33.gain.gain1, f32[1,128]{1,0:T(1,128)} %tile.35.bias.bias1, ...), custom_call_target="tpu_custom_call" | custom-call | flops 462422016 | bytes 2408448 | tf_op jit(solution)/shard_map/fast2/pallas_call | solution.py:161
  78.9 8.1 %sum2.1.tot.tot2 = f32[2,128]{1,0:T(2,128)} custom-call(f32[2,128]{1,0:T(2,128)} %get-tuple-element.143.refs_0_), custom_call_target="tpu_custom_call" | custom-call | tf_op jit(solution)/shard_map/sum2/pallas_call | solution.py:251
  87.0 6.9 %fast3.1 = (f32[2352,128]{1,0:T(8,128)}, f32[2,512]{1,0:T(2,128)}) custom-call(f32[2,128]{1,0:T(2,128)} %sum2.1.tot.tot2, f32[1,128]{1,0:T(1,128)} %tile.37.gain.gain2, f32[1,128]{1,0:T(1,128)} %tile.39.bias.bias2, f32[2352,128]{1,0:T(8,128)} %get-tuple-element.144.p2, bf16[128,512]{1,0:T(8,128)(2,1)} %get-tuple-element.373.eh, ...), custom_call_target="tpu_custom_call" | custom-call | flops 924844032 | bytes 1204224 | tf_op jit(solution)/shard_map/fast3/pallas_call | solution.py:161
  95.1 2.4 slice.334
  97.5 2.1 copy.134
  99.7 2.0 fusion.49
  102.8 2.8 fusion
  105.6 2.1 fusion.5
  108.5 8.9 %lateral.1 = (f32[2352,256]{1,0:T(8,128)}, f32[7,14,256]{2,1,0:T(8,128)}, f32[2,256]{1,0:T(2,128)}) custom-call(s32[7]{0:T(128)} %stack.74.idx, f32[24,128]{1,0:T(8,128)} %copy-done.18, f32[196,96,128]{2,1,0:T(8,128)} %bitcast.164, f32[98,8,128]{2,1,0:T(8,128)} %copy-done.8, bf16[256,640]{1,0:T(8,128)(2,1)} %get-tuple-element.146.wh, ...), custom_call_target="tpu_custom_call" | custom-call | flops 1387266048 | bytes 3612672 | tf_op jit(solution)/shard_map/lateral/pallas_call | solution.py:161
  117.4 8.9 %sum3.1 = (f32[2,512]{1,0:T(2,128)}, f32[2,256]{1,0:T(2,128)}) custom-call(f32[2,512]{1,0:T(2,128)} %get-tuple-element.145.refs_0_, f32[2,256]{1,0:T(2,128)} %get-tuple-element.147.refs_1_), custom_call_target="tpu_custom_call" | custom-call | tf_op jit(solution)/shard_map/sum3/pallas_call | solution.py:251
  126.4 14.2 %fast4.1 = (f32[98,96,128]{2,1,0:T(8,128)}, f32[196,96,128]{2,1,0:T(8,128)}, f32[2352,512]{1,0:T(8,128)}, f32[2,512]{1,0:T(2,128)}) custom-call(s32[7]{0:T(128)} %stack.74.idx, f32[2,512]{1,0:T(2,128)} %get-tuple-element.149.tot, f32[1,128]{1,0:T(1,128)} %bitcast.233, f32[1,128]{1,0:T(1,128)} %bitcast.232, f32[196,96,128]{2,1,0:T(8,128)} %bitcast.165, ...), custom_call_target="tpu_custom_call" | custom-call | flops 924844032 | bytes 12042240 | tf_op jit(solution)/shard_map/fast4/pallas_call | solution.py:161
  144.3 2.5 fusion.1
  146.8 21.4 %slow1.1 = (f32[1176,256]{1,0:T(8,128)}, f32[1176,1024]{1,0:T(8,128)}, bf16[7,168,1280]{2,1,0:T(8,128)(2,1)}, bf16[7,168,1280]{2,1,0:T(8,128)(2,1)}, f32[7,7,256...) custom-call(s32[7]{0:T(128)} %stack.74.idx, f32[2,256]{1,0:T(2,128)} %get-tuple-element.152.tot.tot_a, ...), custom_call_target="tpu_custom_call" | custom-call | flops 5780275200 | bytes 12531680 | tf_op jit(solution)/shard_map/slow1/pallas_call | solution.py:161
  168.2 12.8 %sum8.1 = (f32[2,1280]{1,0:T(2,128)}, f32[2,512]{1,0:T(2,128)}, f32[7,7,256]{2,1,0:T(8,128)}, f32[7,7,256]{2,1,0:T(8,128)}) custom-call(f32[2,1280]{1,0:T(2,128)} %get-tuple-element.155.refs_0_, f32[2,512]{1,0:T(2,128)} %get-tuple-element.151.refs_1_, f32[7,7,256]{2,1,0:T(8,128)} %get-tuple-element.156.refs_2_, f32[7,7,256]{2,1,0:T(8,128)} %get-tuple-element.157.refs_3_), custom_call_target="tpu_custom_call" | custom-call | tf_op jit(solution)/shard_map/sum8/pallas_call | solution.py:251
  181.0 2.1 fusion.3
  183.2 8.2 %slow2.1 = (bf16[7,168,768]{2,1,0:T(8,128)(2,1)}, bf16[7,168,768]{2,1,0:T(8,128)(2,1)}, f32[1176,256]{1,0:T(8,128)}, f32[2,256]{1,0:T(2,128)}) custom-call(f32[24,256]{1,0:T(8,128)} %pad_maximum_fusion.11.mp, f32[24,256]{1,0:T(8,128)} %pad_maximum_fusion.12.mn, f32[2,1280]{1,0:T(2,128)} %get-tuple-element.158.tot.tot_s.tot_f, ...), custom_call_target="tpu_custom_call" | custom-call | flops 693633024 | bytes 3528000 | tf_op jit(solution)/shard_map/slow2/pallas_call | solution.py:161
  191.3 11.2 %sum9.1.tot.tot_m = f32[2,256]{1,0:T(2,128)} custom-call(f32[2,256]{1,0:T(2,128)} %get-tuple-element.162.refs_0_), custom_call_target="tpu_custom_call" | custom-call | tf_op jit(solution)/shard_map/sum9/pallas_call | solution.py:251
  203.8 2.4 fusion.2
  206.3 7.0 %slow3.1 = (bf16[7,168,256]{2,1,0:T(8,128)(2,1)}, bf16[7,168,256]{2,1,0:T(8,128)(2,1)}, f32[2,1024]{1,0:T(2,128)}) custom-call(f32[2,256]{1,0:T(2,128)} %sum9.1.tot.tot_m, f32[1,256]{1,0:T(1,128)} %reshape.536.gain.gain_m, f32[1,256]{1,0:T(1,128)} %reshape.537.bias.bias_m, f32[1176,256]{1,0:T(8,128)} %get-tuple-element.163.pm, ...), custom_call_target="tpu_custom_call" | custom-call | flops 924844032 | bytes 1204224 | tf_op jit(solution)/shard_map/slow3/pallas_call | solution.py:161
  213.2 10.6 %sum10.1.tot_l = f32[2,1024]{1,0:T(2,128)} custom-call(f32[2,1024]{1,0:T(2,128)} %get-tuple-element.164.refs_0_), custom_call_target="tpu_custom_call" | custom-call | tf_op jit(solution)/shard_map/sum10/pallas_call | solution.py:251
  226.3 13.4 %slow4.1 = (f32[4704,256]{1,0:T(8,128)}, f32[1176,256]{1,0:T(8,128)}, f32[1176,256]{1,0:T(8,128)}, f32[1176,256]{1,0:T(8,128)}, f32[1176,1024]{1,0:T(8,128)}, /*index=5*/f32[4,1024]{1,0:T(4,128)}) custom-call(s32[7]{0:T(128)} %stack.74.idx, f32[2,1024]{1,0:T(2,128)} %sum10.1.tot_l, f32[2,1280]{1,0:T(2,128)} %get-tuple-element.158.tot.tot_s.tot_f, ...), custom_call_target="tpu_custom_call" | custom-call | flops 924844032 | bytes 10235904 | tf_op jit(solution)/shard_map/slow4/pallas_call | solution.py:161
  239.9 3.1 collective-permute-done.7
  244.1 12.0 %sum11.1.back = f32[4,1024]{1,0:T(4,128)} custom-call(f32[4,1024]{1,0:T(4,128)} %get-tuple-element.173.refs_0_), custom_call_target="tpu_custom_call" | custom-call | tf_op jit(solution)/shard_map/sum11/pallas_call | solution.py:251
  256.1 38.2 %slow6.1 = (f32[1176,1280]{1,0:T(8,128)}, f32[4,1280,256]{2,1,0:T(8,128)}) custom-call(f32[2,1280]{1,0:T(2,128)} %get-tuple-element.158.tot.tot_s.tot_f, f32[4,1024]{1,0:T(4,128)} %sum11.1.back, f32[1,1024]{1,0:T(1,128)} %bitcast.223, f32[1176,1024]{1,0:T(8,128)} %get-tuple-element.174.u_ref, f32[1176,1024]{1,0:T(8,128)} %get-tuple-element.167.short, ...), custom_call_target="tpu_custom_call" | custom-call | flops 9248440320 | bytes 16819200 | tf_op jit(solution)/shard_map/slow6/pallas_call | solution.py:161
  294.3 19.2 %slow5.1 = (f32[1176,256]{1,0:T(8,128)}, f32[256,1024]{1,0:T(8,128)}, f32[7,2,7,256]{3,2,1,0:T(8,128)}, f32[7,2,7,256]{3,2,1,0:T(8,128)}, f32[2,256]{1,0:T(2,128)}) custom-call(f32[2,1024]{1,0:T(2,128)} %sum10.1.tot_l, f32[4,1024]{1,0:T(4,128)} %sum11.1.back, f32[1,1024]{1,0:T(1,128)} %bitcast.221, f32[2,256]{1,0:T(2,128)} %sum9.1.tot.tot_m, ...), custom_call_target="tpu_custom_call" | custom-call | flops 2774532096 | bytes 4233600 | tf_op jit(solution)/shard_map/slow5/pallas_call | solution.py:161
  316.8 1.5 collective-permute-start.15
  318.4 16.2 %sum12.1 = (f32[2,256]{1,0:T(2,128)}, f32[7,2,7,256]{3,2,1,0:T(8,128)}, f32[7,2,7,256]{3,2,1,0:T(8,128)}) custom-call(f32[2,256]{1,0:T(2,128)} %get-tuple-element.179.refs_0_, f32[7,2,7,256]{3,2,1,0:T(8,128)} %get-tuple-element.180.refs_1_, f32[7,2,7,256]{3,2,1,0:T(8,128)} %get-tuple-element.181.refs_2_), custom_call_target="tpu_custom_call" | custom-call | tf_op jit(solution)/shard_map/sum12/pallas_call | solution.py:251
  334.7 12.9 %slow7.1 = (f32[1176,256]{1,0:T(8,128)}, f32[256,768]{1,0:T(8,128)}, f32[2,256]{1,0:T(2,128)}) custom-call(f32[24,256]{1,0:T(8,128)} %pad_maximum_fusion.11.mp, f32[24,256]{1,0:T(8,128)} %pad_maximum_fusion.12.mn, f32[2,256]{1,0:T(2,128)} %sum9.1.tot.tot_m, f32[2,256]{1,0:T(2,128)} %get-tuple-element.182.back, f32[1,256]{1,0:T(1,128)} %reshape.536.gain.gain_m, ...), custom_call_target="tpu_custom_call" | custom-call | flops 1387266048 | bytes 3528000 | tf_op jit(solution)/shard_map/slow7/pallas_call | solution.py:161
  347.6 9.9 %sum13.1.back = f32[2,256]{1,0:T(2,128)} custom-call(f32[2,256]{1,0:T(2,128)} %get-tuple-element.188.refs_0_), custom_call_target="tpu_custom_call" | custom-call | tf_op jit(solution)/shard_map/sum13/pallas_call | solution.py:251
  357.5 20.2 %slow8.1 = (f32[4704,256]{1,0:T(8,128)}, f32[1176,256]{1,0:T(8,128)}, f32[1176,256]{1,0:T(8,128)}, f32[1176,256]{1,0:T(8,128)}, f32[1176,256]{1,0:T(8,128)}, /*i...) custom-call(s32[7]{0:T(128)} %stack.74.idx, f32[2,1280]{1,0:T(2,128)} %get-tuple-element.158.tot.tot_s.tot_f, ...), custom_call_target="tpu_custom_call" | custom-call | flops 2312110080 | bytes 11760000 | tf_op jit(solution)/shard_map/slow8/pallas_call | solution.py:161
  377.8 10.9 %sum14.1.back = f32[2,256]{1,0:T(2,128)} custom-call(f32[2,256]{1,0:T(2,128)} %get-tuple-element.190.refs_0_), custom_call_target="tpu_custom_call" | custom-call | tf_op jit(solution)/shard_map/sum14/pallas_call | solution.py:251
  388.7 8.8 %slow9.1 = f32[256,640]{1,0:T(8,128)} custom-call(s32[7]{0:T(128)} %stack.74.idx, f32[24,128]{1,0:T(8,128)} %copy-done.18, f32[2,256]{1,0:T(2,128)} %get-tuple-element.152.tot.tot_a, f32[2,256]{1,0:T(2,128)} %sum14.1.back, f32[1,256]{1,0:T(1,128)} %reshape.532.gain.gain_a, f32[1176,256]{1,0:T(8,128)} %get-tuple-element.215.us, ...), custom_call_target="tpu_custom_call" | custom-call | flops 578027520 | bytes 3528000 | tf_op jit(solution)/shard_map/slow9/pallas_call | solution.py:161
  405.9 1.8 maximum_add_fusion
  409.6 1.6 collective-permute-start.9
  412.0 13.2 %fast5.1 = (f32[2352,128]{1,0:T(8,128)}, f32[128,512]{1,0:T(8,128)}, f32[7,2,14,128]{3,2,1,0:T(8,128)}, f32[7,2,14,128]{3,2,1,0:T(8,128)}, f32[2,128]{1,0:T(2,128)}) custom-call(f32[2,512]{1,0:T(2,128)} %get-tuple-element.149.tot, f32[2,512]{1,0:T(2,128)} %get-tuple-element.200.back, f32[1,128]{1,0:T(1,128)} %bitcast.234, f32[2,128]{1,0:T(2,128)} %sum2.1.tot.tot2, ...), custom_call_target="tpu_custom_call" | custom-call | flops 2774532096 | bytes 4233600 | tf_op jit(solution)/shard_map/fast5/pallas_call | solution.py:161
  425.2 1.8 collective-permute-done.8
  427.0 15.2 %sum5.1 = (f32[2,128]{1,0:T(2,128)}, f32[7,2,14,128]{3,2,1,0:T(8,128)}, f32[7,2,14,128]{3,2,1,0:T(8,128)}) custom-call(f32[2,128]{1,0:T(2,128)} %get-tuple-element.203.refs_0_, f32[7,2,14,128]{3,2,1,0:T(8,128)} %get-tuple-element.204.refs_1_, f32[7,2,14,128]{3,2,1,0:T(8,128)} %get-tuple-element.205.refs_2_), custom_call_target="tpu_custom_call" | custom-call | tf_op jit(solution)/shard_map/sum5/pallas_call | solution.py:251
  443.2 9.4 %fast6.1 = (f32[2352,128]{1,0:T(8,128)}, f32[256,128]{1,0:T(8,128)}, f32[2,128]{1,0:T(2,128)}) custom-call(f32[24,128]{1,0:T(8,128)} %copy-done.18, f32[24,128]{1,0:T(8,128)} %copy-done.21, f32[2,128]{1,0:T(2,128)} %sum2.1.tot.tot2, f32[2,128]{1,0:T(2,128)} %get-tuple-element.209.back2, f32[1,128]{1,0:T(1,128)} %tile.37.gain.gain2, ...), custom_call_target="tpu_custom_call" | custom-call | flops 924844032 | bytes 3612672 | tf_op jit(solution)/shard_map/fast6/pallas_call | solution.py:161
  453.7 7.7 %sum6.1.back1 = f32[2,128]{1,0:T(2,128)} custom-call(f32[2,128]{1,0:T(2,128)} %get-tuple-element.214.refs_0_), custom_call_target="tpu_custom_call" | custom-call | tf_op jit(solution)/shard_map/sum6/pallas_call | solution.py:251
  461.6 9.0 %fast7.1 = (f32[2352,128]{1,0:T(8,128)}, f32[512,128]{1,0:T(8,128)}) custom-call(s32[7]{0:T(128)} %stack.74.idx, f32[2,128]{1,0:T(2,128)} %get-tuple-element.139.tot.tot1, f32[2,128]{1,0:T(2,128)} %sum6.1.back1, f32[1,128]{1,0:T(1,128)} %tile.33.gain.gain1, f32[196,96,128]{2,1,0:T(8,128)} %bitcast.167, f32[2352,128]{1,0:T(8,128)} %get-tuple-element.217.u1, ...), custom_call_target="tpu_custom_call" | custom-call | flops 924844032 | bytes 4233600 | tf_op jit(solution)/shard_map/fast7/pallas_call | solution.py:161
  472.1 1.6 collective-permute-start.11
  474.1 1.4 broadcast_select_fusion.1
  475.5 1.6 pad_maximum_fusion.5.us
  477.8 57.3 %sum15.1 = (f32[88,128]{1,0:T(8,128)}, f32[8,8,2688]{2,1,0:T(8,128)}) custom-call(f32[88,128]{1,0:T(8,128)} %pad_maximum_fusion.10.x_ref, f32[8,8,2688]{2,1,0:T(8,128)} %bitcast.182), custom_call_target="tpu_custom_call" | custom-call | tf_op jit(solution)/shard_map/sum15/pallas_call | solution.py:320
  535.3 13.1 %last.1 = (f32[98,96,128]{2,1,0:T(8,128)}, f32[196,96,128]{2,1,0:T(8,128)}) custom-call(s32[7]{0:T(128)} %stack.74.idx, f32[24,128]{1,0:T(8,128)} %copy-done.21, f32[2,256]{1,0:T(2,128)} %get-tuple-element.152.tot.tot_a, f32[2,256]{1,0:T(2,128)} %sum14.1.back, f32[1,256]{1,0:T(1,128)} %reshape.532.gain.gain_a, f32[2352,256]{1,0:T(8,128)} %pad_maximum_fusion.5.us, ...), custom_call_target="tpu_custom_call" | custom-call | flops 1849688064 | bytes 9408000 | tf_op jit(solution)/shard_map/last/pallas_call | solution.py:161
  560.4 2.5 constant_dynamic-update-slice_fusion.5
  567.0 2.4 constant_dynamic-update-slice_fusion.1
  569.4 5.0 constant_dynamic-update-slice_fusion.4
  574.5 3.0 constant_dynamic-update-slice_fusion
  579.4 1.7 copy.180
  (303 shorter events, 65.1 us)
Async XLA Ops:
  7.2 87.9 %all-gather.13.cloned.1.call-start = ((), (), s32[]{:S(2)}) async-start(), calls=%async_computation.6 | async-start | bytes 4190208 | tf_op jit(solution)/shard_map/all_gather | solution.py:794
  10.7 215.6 %all-gather.9.cloned.1.call-start = ((), (), s32[]{:S(2)}) async-start(), calls=%async_computation.2 | async-start | bytes 3612672 | tf_op jit(solution)/shard_map/all_gather | solution.py:894
  10.7 10.0 %copy-start.3 = (f32[1280,256]{1,0:T(8,128)S(1)}, f32[1280,256]{1,0:T(8,128)}, u32[]{:S(2)}) copy-start(f32[1280,256]{1,0:T(8,128)} %param.53) | copy-start | bytes 3932164
  10.7 11.7 %copy-start.25 = (f32[3,32,32]{2,1,0:T(8,128)S(1)}, f32[3,32,32]{2,1,0:T(8,128)}, u32[]{:S(2)}) copy-start(f32[3,32,32]{2,1,0:T(8,128)} %param.35) | copy-start | bytes 36868
  10.7 11.7 %copy-start.31 = (f32[128,32]{0,1:T(8,128)S(1)}, f32[128,32]{0,1:T(8,128)}, u32[]{:S(2)}) copy-start(f32[128,32]{0,1:T(8,128)} %param.32) | copy-start | bytes 49156
  14.1 11.3 %collective-permute-start = (f32[2352,256]{1,0:T(8,128)}, f32[2352,256]{1,0:T(8,128)}, u32[]{:S(2)}, u32[]{:S(2)}) collective-permute-start(f32[2352,256]{1,0:T(8,128)} %constant_dynamic-slice_fusion.27), channel_id=1, source_target_pairs={{0,1},{1,0},{2,3},{3,2},{4,5},{5,4},{6,7},{7,6},{8,9},{9,8},{10,11... | collective-permute-start | bytes 7225352 | tf_op jit(solution)/shard_map/ppermute | solution.py:761
  16.3 91.4 %collective-permute-start.1 = (f32[98,8,128]{2,1,0:T(8,128)}, f32[98,8,128]{2,1,0:T(8,128)S(1)}, u32[]{:S(2)}, u32[]{:S(2)}) collective-permute-start(f32[98,8,128]{2,1,0:T(8,128)} %dynamic-slice_bitcast_fusion.4), channel_id=1, source_target_pairs={{0,4},{4,8},{8,12},{12,16},{16,20},{20,24},{24,28},{1,5},{5,9},{9,... | collective-permute-start | bytes 1204232 | tf_op jit(solution)/shard_map/ppermute | solution.py:830
  20.7 33.7 %collective-permute-start.3 = (f32[1280,256]{1,0:T(8,128)S(1)}, f32[1280,256]{1,0:T(8,128)S(1)}, u32[]{:S(2)}, u32[]{:S(2)}) collective-permute-start(f32[1280,256]{1,0:T(8,128)S(1)} %copy-done.3), channel_id=1, source_target_pairs={{0,2},{2,0},{1,3},{3,1},{4,6},{6,4},{5,7},{7,5},{8,10},{10,8},{9,1... | collective-permute-start | bytes 3932168 | tf_op jit(solution)/shard_map/ppermute | solution.py:771
  56.4 43.3 %collective-permute-start.4 = (f32[2,1280,256]{2,1,0:T(8,128)}, f32[2,1280,256]{2,1,0:T(8,128)}, u32[]{:S(2)}, u32[]{:S(2)}) collective-permute-start(f32[2,1280,256]{2,1,0:T(8,128)} %pad_maximum_fusion.3), channel_id=1, source_target_pairs={{0,1},{1,0},{2,3},{3,2},{4,5},{5,4},{6,7},{7,6},{8,9},{9,8},{10,11... | collective-permute-start | bytes 7864328 | tf_op jit(solution)/shard_map/ppermute | solution.py:887
  56.4 4.8 copy-start.41
  56.4 5.4 copy-start.42
  56.4 7.2 %copy-start.43 = (f32[32]{0:T(128)S(1)}, f32[32]{0:T(128)}, u32[]{:S(2)}) copy-start(f32[32]{0:T(128)} %param.36) | copy-start | bytes 388
  56.4 7.9 %copy-start.44 = (f32[32]{0:T(128)S(1)}, f32[32]{0:T(128)}, u32[]{:S(2)}) copy-start(f32[32]{0:T(128)} %param.37) | copy-start | bytes 388
  56.4 8.4 %copy-start.45 = (s32[24]{0:T(128)S(1)}, s32[24]{0:T(128)}, u32[]{:S(2)}) copy-start(s32[24]{0:T(128)} %param.31) | copy-start | bytes 292
  56.5 10.7 %copy-start.32 = (f32[32,128]{1,0:T(8,128)S(1)}, f32[32,128]{1,0:T(8,128)}, u32[]{:S(2)}) copy-start(f32[32,128]{1,0:T(8,128)} %param.38) | copy-start | bytes 49156
  59.8 34.1 %collective-permute-start.5 = (f32[2352,256]{1,0:T(8,128)}, f32[2352,256]{1,0:T(8,128)S(1)}, u32[]{:S(2)}, u32[]{:S(2)}) collective-permute-start(f32[2352,256]{1,0:T(8,128)} %constant_dynamic-slice_fusion.20), channel_id=1, source_target_pairs={{0,1},{1,0},{2,3},{3,2},{4,5},{5,4},{6,7},{7,6},{8,9},{9,8},{10,11... | collective-permute-start | bytes 7225352 | tf_op jit(solution)/shard_map/ppermute | solution.py:761
  65.1 6.7 %copy-start.18 = (f32[24,128]{1,0:T(8,128)}, f32[24,128]{1,0:T(8,128)S(1)}, u32[]{:S(2)}) copy-start(f32[24,128]{1,0:T(8,128)S(1)} %broadcast_in_dim.36.mp.mask) | copy-start | bytes 36868
  65.8 6.0 %copy-start.21 = (f32[24,128]{1,0:T(8,128)}, f32[24,128]{1,0:T(8,128)S(1)}, u32[]{:S(2)}) copy-start(f32[24,128]{1,0:T(8,128)S(1)} %broadcast_in_dim.37.mn.mask) | copy-start | bytes 36868
  70.3 76.5 %collective-permute-start.2 = (f32[2352,256]{1,0:T(8,128)}, f32[2352,256]{1,0:T(8,128)}, u32[]{:S(2)}, u32[]{:S(2)}) collective-permute-start(f32[2352,256]{1,0:T(8,128)} %pad_maximum_fusion.4), channel_id=1, source_target_pairs={{0,2},{2,0},{1,3},{3,1},{4,6},{6,4},{5,7},{7,5},{8,10},{10,8},{9,1... | collective-permute-start | bytes 7225352 | tf_op jit(solution)/shard_map/ppermute | solution.py:774
  93.9 3.6 copy-start.2
  99.6 2.5 copy-start.6
  99.6 126.6 %all-gather.11.cloned.1.call-start = ((), (), s32[]{:S(2)}) async-start(), calls=%async_computation.3 | async-start | bytes 3612672 | tf_op jit(solution)/shard_map/all_gather | solution.py:894
  140.7 172.9 %all-gather.15.cloned.1.call-start = ((), (), s32[]{:S(2)}) async-start(), calls=%async_computation.7 | async-start | bytes 3612672 | tf_op jit(solution)/shard_map/all_gather | solution.py:973
  239.7 75.2 %all-gather.17.cloned.1.call-start = ((), (), s32[]{:S(2)}) async-start(), calls=%async_computation.8 | async-start | bytes 3612672 | tf_op jit(solution)/shard_map/all_gather | solution.py:973
  239.8 3.2 collective-permute-start.7
  244.0 167.9 %reduce-scatter.5.cloned.1.call-start = ((), (), s32[]{:S(2)}) async-start(), calls=%async_computation.5 | async-start | bytes 1310720 | tf_op jit(solution)/shard_map/reduce_scatter | solution.py:1002
  314.9 97.0 %reduce-scatter.3.cloned.1.call-start = ((), (), s32[]{:S(2)}) async-start(), calls=%async_computation.4 | async-start | bytes 6553600 | tf_op jit(solution)/shard_map/reduce_scatter | solution.py:1005
  315.0 3.4 copy-start.39
  315.7 219.5 %all-reduce.4.cloned.1.call-start = ((), (), s32[]{:S(2)}) async-start(), calls=%async_computation.9 | async-start | bytes 3145728 | tf_op jit(solution)/shard_map/psum | solution.py:1025
  316.8 218.5 %collective-permute-start.15 = (f32[7,14,256]{2,1,0:T(8,128)}, f32[7,14,256]{2,1,0:T(8,128)}, u32[]{:S(2)}, u32[]{:S(2)}) collective-permute-start(f32[7,14,256]{2,1,0:T(8,128)} %get-tuple-element.233), channel_id=1, source_target_pairs={{4,0},{8,4},{12,8},{16,12},{20,16},{24,20},{28,24},{5,1},{9,5},{13... | collective-permute-start | bytes 301064 | tf_op jit(solution)/shard_map/ppermute | solution.py:903
  318.3 251.1 %collective-permute-start.16 = (f32[98,96,128]{2,1,0:T(8,128)}, f32[98,96,128]{2,1,0:T(8,128)}, u32[]{:S(2)}, u32[]{:S(2)}) collective-permute-start(f32[98,96,128]{2,1,0:T(8,128)} %get-tuple-element.236), channel_id=1, source_target_pairs={{0,1},{1,0},{2,3},{3,2},{4,5},{5,4},{6,7},{7,6},{8,9},{9,8},{10,11... | collective-permute-start | bytes 14450696 | tf_op jit(solution)/shard_map/ppermute | solution.py:1113
  388.7 8.8 %copy-start.11 = (f32[256,1280]{1,0:T(8,128)S(1)}, f32[256,1280]{1,0:T(8,128)}, u32[]{:S(2)}) copy-start(f32[256,1280]{1,0:T(8,128)} %get-tuple-element.192) | copy-start | bytes 3932164
  388.7 8.8 %copy-start.14 = (f32[256,768]{1,0:T(8,128)S(1)}, f32[256,768]{1,0:T(8,128)}, u32[]{:S(2)}) copy-start(f32[256,768]{1,0:T(8,128)} %get-tuple-element.193) | copy-start | bytes 2359300
  399.8 2.3 copy-start.47
  399.8 4.9 copy-start.27
  401.0 3.8 collective-permute-start.6
  402.2 7.5 %collective-permute-start.13 = (f32[7,7,256]{2,1,0:T(8,128)S(1)}, f32[7,7,256]{2,1,0:T(8,128)S(1)}, u32[]{:S(2)}, u32[]{:S(2)}) collective-permute-start(f32[7,7,256]{2,1,0:T(8,128)S(1)} %copy-done.47), channel_id=1, source_target_pairs={{4,0},{8,4},{12,8},{16,12},{20,16},{24,20},{28,24},{5,1},{9,5},{13... | collective-permute-start | bytes 150536 | tf_op jit(solution)/shard_map/ppermute | solution.py:1029
  403.5 7.7 %collective-permute-start.14 = (f32[7,7,256]{2,1,0:T(8,128)S(1)}, f32[7,7,256]{2,1,0:T(8,128)S(1)}, u32[]{:S(2)}, u32[]{:S(2)}) collective-permute-start(f32[7,7,256]{2,1,0:T(8,128)S(1)} %copy-done.47), channel_id=1, source_target_pairs={{4,2},{6,0},{8,6},{10,4},{12,10},{14,8},{16,14},{18,12},{20,18},{2... | collective-permute-start | bytes 150536 | tf_op jit(solution)/shard_map/ppermute | solution.py:1030
  405.9 3.8 copy-start.7
  408.6 18.4 %collective-permute-start.8 = (f32[64,2688]{1,0:T(8,128)}, f32[64,2688]{1,0:T(8,128)S(1)}, u32[]{:S(2)}, u32[]{:S(2)}) collective-permute-start(f32[64,2688]{1,0:T(8,128)} %slice_bitcast_fusion), channel_id=1, source_target_pairs={{0,2},{2,0},{1,3},{3,1},{4,6},{6,4},{5,7},{7,5},{8,10},{10,8},{9,1... | collective-permute-start | bytes 2064392 | tf_op jit(solution)/shard_map/ppermute | solution.py:1045
  409.6 52.0 %collective-permute-start.9 = (f32[1176,256]{1,0:T(8,128)S(1)}, f32[1176,256]{1,0:T(8,128)}, u32[]{:S(2)}, u32[]{:S(2)}) collective-permute-start(f32[1176,256]{1,0:T(8,128)S(1)} %copy-done.7), channel_id=1, source_target_pairs={{0,2},{2,0},{1,3},{3,1},{4,6},{6,4},{5,7},{7,5},{8,10},{10,8},{9,1... | collective-permute-start | bytes 3612680 | tf_op jit(solution)/shard_map/ppermute | solution.py:1027
  411.2 149.2 %collective-permute-start.10 = (f32[1176,256]{1,0:T(8,128)}, f32[1176,256]{1,0:T(8,128)}, u32[]{:S(2)}, u32[]{:S(2)}) collective-permute-start(f32[1176,256]{1,0:T(8,128)} %get-tuple-element.222), channel_id=1, source_target_pairs={{0,1},{1,0},{2,3},{3,2},{4,5},{5,4},{6,7},{7,6},{8,9},{9,8},{10,11... | collective-permute-start | bytes 3612680 | tf_op jit(solution)/shard_map/ppermute | solution.py:971
  461.6 10.3 %copy-start.20 = (f32[128,512]{1,0:T(8,128)S(1)}, f32[128,512]{1,0:T(8,128)}, u32[]{:S(2)}) copy-start(f32[128,512]{1,0:T(8,128)} %get-tuple-element.202) | copy-start | bytes 786436
  472.1 63.0 %collective-permute-start.11 = (f32[1176,256]{1,0:T(8,128)}, f32[1176,256]{1,0:T(8,128)S(1)}, u32[]{:S(2)}, u32[]{:S(2)}) collective-permute-start(f32[1176,256]{1,0:T(8,128)} %get-tuple-element.225), channel_id=1, source_target_pairs={{0,2},{1,3},{2,0},{3,1},{4,6},{5,7},{6,4},{7,5},{8,10},{9,11},{10,... | collective-permute-start | bytes 3612680 | tf_op jit(solution)/shard_map/ppermute | solution.py:1060
  473.7 61.5 %collective-permute-start.12 = (f32[1176,256]{1,0:T(8,128)}, f32[1176,256]{1,0:T(8,128)}, u32[]{:S(2)}, u32[]{:S(2)}) collective-permute-start(f32[1176,256]{1,0:T(8,128)} %get-tuple-element.227), channel_id=1, source_target_pairs={{0,3},{1,2},{2,1},{3,0},{4,7},{5,6},{6,5},{7,4},{8,11},{9,10},{10,... | collective-permute-start | bytes 3612680 | tf_op jit(solution)/shard_map/ppermute | solution.py:1060
  535.1 18.0 %collective-permute-start.17 = (f32[1176,256]{1,0:T(8,128)}, f32[1176,256]{1,0:T(8,128)S(1)}, u32[]{:S(2)}, u32[]{:S(2)}) collective-permute-start(f32[1176,256]{1,0:T(8,128)} %get-tuple-element.239), channel_id=1, source_target_pairs={{0,1},{1,0},{2,3},{3,2},{4,5},{5,4},{6,7},{7,6},{8,9},{9,8},{10,11... | collective-permute-start | bytes 3612680 | tf_op jit(solution)/shard_map/ppermute | solution.py:1060
  535.2 13.7 %copy-start.30 = (f32[2,256]{1,0:T(2,128)S(1)}, f32[2,256]{1,0:T(2,128)}, u32[]{:S(2)}) copy-start(f32[2,256]{1,0:T(2,128)} %sum13.1.back) | copy-start | bytes 6148
  535.2 14.3 %copy-start.37 = (f32[2,256]{1,0:T(2,128)S(1)}, f32[2,256]{1,0:T(2,128)}, u32[]{:S(2)}) copy-start(f32[2,256]{1,0:T(2,128)} %get-tuple-element.182.back) | copy-start | bytes 6148
  535.2 16.1 %copy-start.24 = (f32[4,1024]{1,0:T(4,128)S(1)}, f32[4,1024]{1,0:T(4,128)}, u32[]{:S(2)}) copy-start(f32[4,1024]{1,0:T(4,128)} %sum11.1.back) | copy-start | bytes 49156
  548.4 5.8 copy-start.26
  548.4 5.8 copy-start.15
  548.4 7.2 %copy-start.36 = (f32[2,128]{1,0:T(2,128)S(1)}, f32[2,128]{1,0:T(2,128)}, u32[]{:S(2)}) copy-start(f32[2,128]{1,0:T(2,128)} %sum6.1.back1) | copy-start | bytes 3076
  548.4 8.7 %copy-start.38 = (f32[2,128]{1,0:T(2,128)S(1)}, f32[2,128]{1,0:T(2,128)}, u32[]{:S(2)}) copy-start(f32[2,128]{1,0:T(2,128)} %get-tuple-element.209.back2) | copy-start | bytes 3076
  548.4 26.0 %collective-permute-start.18 = (f32[98,96,128]{2,1,0:T(8,128)}, f32[98,96,128]{2,1,0:T(8,128)}, u32[]{:S(2)}, u32[]{:S(2)}) collective-permute-start(f32[98,96,128]{2,1,0:T(8,128)} %get-tuple-element.234), channel_id=1, source_target_pairs={{0,1},{1,0},{2,3},{3,2},{4,5},{5,4},{6,7},{7,6},{8,9},{9,8},{10,11... | collective-permute-start | bytes 14450696 | tf_op jit(solution)/shard_map/ppermute | solution.py:1113
  551.4 26.2 %copy-start.40 = (f32[1,256]{1,0:T(1,128)}, f32[1,256]{1,0:T(1,128)S(1)}, u32[]{:S(2)}) copy-start(f32[1,256]{1,0:T(1,128)S(1)} %constant_dynamic-slice_fusion.12) | copy-start | bytes 3076
  558.7 4.3 copy-start.16
  560.4 3.6 copy-start.17
  560.4 14.0 %slice-start = ((s8[9633792]{0:T(1024)(128)(4,1)}), s8[4194304]{0:T(1024)(128)(4,1)S(1)}, s32[]{:S(2)}) async-start(s8[9633792]{0:T(1024)(128)(4,1)} %bitcast.236), calls=%async_computation.10 | async-start | bytes 8388608
  565.2 9.2 %slice-start.1 = ((s8[9633792]{0:T(1024)(128)(4,1)}), s8[4194304]{0:T(1024)(128)(4,1)S(1)}, s32[]{:S(2)}) async-start(s8[9633792]{0:T(1024)(128)(4,1)} %bitcast.236), calls=%async_computation.11 | async-start | bytes 8388608
  569.4 5.0 slice-start.2
  574.4 3.7 copy-start.19
  574.5 4.9 copy-start.10
  574.5 7.4 %copy-start.1 = (f32[5,128,64]{1,2,0:T(8,128)S(1)}, f32[5,128,64]{1,2,0:T(8,128)}, u32[]{:S(2)}) copy-start(f32[5,128,64]{1,2,0:T(8,128)} %param.41) | copy-start | bytes 491524
  577.5 4.3 copy-start.46
  (14 other events, 23.5 us)
Sparse Core Ops, SparseCore 0:
  11.5 66.9 all-gather.12
  99.7 51.0 all-gather.8
  152.4 37.7 all-gather.10
  239.8 37.5 all-gather.14
  278.8 36.0 all-gather.16
  317.3 28.7 reduce-scatter.4
  348.8 51.4 reduce-scatter.2
  412.1 117.3 all-reduce.3

commit v3 on v2

--- a/solution.py
+++ b/solution.py
@@ -1023,8 +1023,6 @@
     )
     (back_a,) = total([st], 14, sizes, ROLE)
     shortcut_sum, expand_sum = lax.psum((short_pair, expand_pair), "dp")
-    us_sent = after(us, back_a)
-    us_other = lax.ppermute(us_sent, "yy", swap)
     edge_sent = after(us_edge, back_a)
     edge_same = lax.ppermute(edge_sent, "dp", backw)
     edge_cross = lax.ppermute(
@@ -1043,6 +1041,8 @@
 
     both = chip_sum(*by_peer(jnp.concatenate([lateral_grad, reduce_grad, temporal_grad], axis=1)))
     rest_y = lax.ppermute(both[1], "yy", swap)
+    us_other = lax.ppermute(after(us, both), "yy", swap)
+
     u2, expand_packed, e0, e1, st = stepped(
         functools.partial(fast5_kernel, fast_number, frames), "fast5", steps, [],
         all_of(tot_f3, after(back_f3, back_a, both, short_pair, expand_pair), fe_gain, tot_f2, ft_gain, ft_bias)
@@ -1115,7 +1115,7 @@
 
     from_y = [lax.dynamic_index_in_dim(v, 1 - y, 0, keepdims=False) for v in from_y]
     slow_output = placed(after(slow_out, small), [near_rows] + from_y)
-    fast_output = fast_whole(fast_half, after(fast_full, grad_half))
+    fast_output = fast_whole(after(fast_half, small), after(fast_full, small))
     fast_input_gradient = fast_whole(grad_half, grad_full)
 
     def fold(v):

time: 594 us -> 593 us (level)
  transfers between devices with their start and end apart: 27 -> 27, of which waited for: 4 -> 5; matrix products, arithmetic and copies ran while one was open for 17% -> 17% of each run, Pallas kernels for 71% -> 71%
where the time goes in v3:
time: 593 us; the launch traced here: 587 us
  Pallas kernels  428 us (72%)
  local copies, waits for them, and re-layouts  74.2 us (13%)
  other arithmetic  38.6 us (7%)
  starting transfers between devices  17.5 us (3%)
  between operations  15.4 us (3%)
  waiting for transfers between devices  13.3 us (2%)
    pallas_call x18, Pallas kernels, stepped(): pl.pallas_call(body, name=name, out_shape=[o for o, _ in outs], grid_spec...  239 us
    pallas_call x12, Pallas kernels, total(): pl.pallas_call(functools.partial(sum_kernel, sizes, axes, widths, len(rim...  131 us
    pallas_call x1, Pallas kernels, last_total(): pl.pallas_call(functools.partial(last_sum_kernel, sizes), name='sum%d' %...  57.5 us
    unnamed x118, local copies, waits for them, and re-layouts  16 us
    convert_element_type x9, other arithmetic, weight_split(): return (high.astype(BF16), (w - high).astype(BF16))  15.7 us
  transfers between devices with their start and end apart: 27, of which 5 were waited for; matrix products, arithmetic and copies ran while one was open for 17% of the time, Pallas kernels for 71%

profile of v3, /device:TPU:0, one launch (start us, length us, event | category | flops | bytes accessed | tf_op | source)
XLA Modules:
  0.0 586.7 jit_solution(17303966594206506960)
XLA Ops:
  10.7 3.4 constant_dynamic-slice_fusion.27
  14.6 1.8 dynamic-slice_bitcast_fusion.4
  16.3 4.4 collective-permute-start.1
  20.7 1.6 collective-permute-start.3
  24.1 1.4 constant_dynamic-slice_fusion.28
  25.4 1.4 constant_dynamic-slice_fusion.26
  26.8 1.6 pad_maximum_fusion.4
  29.2 1.7 fusion.6
  30.9 8.0 %fast1.1 = (f32[2352,128]{1,0:T(8,128)}, f32[7,14,128]{2,1,0:T(8,128)}, f32[7,14,128]{2,1,0:T(8,128)}, f32[2,128]{1,0:T(2,128)}) custom-call(s32[7]{0:T(128)} %stack.74.idx, f32[196,96,128]{2,1,0:T(8,128)} %bitcast.163, bf16[512,128]{1,0:T(8,128)(2,1)} %get-tuple-element.377.rh, bf16[512,128]{1,0:T(8,128)(2,1)} %get-tuple-element.376.rl), custom_call_target="tpu_custom_call" | custom-call | flops 924844032 | bytes 3010560 | tf_op jit(solution)/shard_map/fast1/pallas_call | solution.py:161
  38.9 9.9 %sum1.1 = (f32[2,128]{1,0:T(2,128)}, f32[7,14,128]{2,1,0:T(8,128)}, f32[7,14,128]{2,1,0:T(8,128)}) custom-call(f32[2,128]{1,0:T(2,128)} %get-tuple-element.137.refs_0_, f32[7,14,128]{2,1,0:T(8,128)} %get-tuple-element.138.refs_1_, f32[7,14,128]{2,1,0:T(8,128)} %get-tuple-element.139.refs_2_), custom_call_target="tpu_custom_call" | custom-call | tf_op jit(solution)/shard_map/sum1/pallas_call | solution.py:251
  48.8 5.7 collective-permute-done.3
  54.5 1.8 pad_maximum_fusion.3
  56.5 3.3 constant_dynamic-slice_fusion.20
  68.0 2.4 constant_dynamic-slice_fusion.19
  70.4 1.5 collective-permute-start.2
  71.9 7.1 %fast2.1 = (f32[2352,128]{1,0:T(8,128)}, f32[2352,128]{1,0:T(8,128)}, f32[2352,128]{1,0:T(8,128)}, f32[2,128]{1,0:T(2,128)}) custom-call(f32[24,128]{1,0:T(8,128)} %copy-done.18, f32[24,128]{1,0:T(8,128)} %copy-done.21, f32[2,128]{1,0:T(2,128)} %get-tuple-element.140.tot.tot1, f32[1,128]{1,0:T(1,128)} %tile.33.gain.gain1, f32[1,128]{1,0:T(1,128)} %tile.35.bias.bias1, ...), custom_call_target="tpu_custom_call" | custom-call | flops 462422016 | bytes 2408448 | tf_op jit(solution)/shard_map/fast2/pallas_call | solution.py:161
  78.9 8.1 %sum2.1.tot.tot2 = f32[2,128]{1,0:T(2,128)} custom-call(f32[2,128]{1,0:T(2,128)} %get-tuple-element.144.refs_0_), custom_call_target="tpu_custom_call" | custom-call | tf_op jit(solution)/shard_map/sum2/pallas_call | solution.py:251
  87.1 6.9 %fast3.1 = (f32[2352,128]{1,0:T(8,128)}, f32[2,512]{1,0:T(2,128)}) custom-call(f32[2,128]{1,0:T(2,128)} %sum2.1.tot.tot2, f32[1,128]{1,0:T(1,128)} %tile.37.gain.gain2, f32[1,128]{1,0:T(1,128)} %tile.39.bias.bias2, f32[2352,128]{1,0:T(8,128)} %get-tuple-element.145.p2, bf16[128,512]{1,0:T(8,128)(2,1)} %get-tuple-element.375.eh, ...), custom_call_target="tpu_custom_call" | custom-call | flops 924844032 | bytes 1204224 | tf_op jit(solution)/shard_map/fast3/pallas_call | solution.py:161
  95.2 2.3 slice.334
  97.5 2.1 copy.134
  99.8 2.0 fusion.49
  102.9 2.8 fusion
  105.7 2.1 fusion.5
  108.5 8.9 %lateral.1 = (f32[2352,256]{1,0:T(8,128)}, f32[7,14,256]{2,1,0:T(8,128)}, f32[2,256]{1,0:T(2,128)}) custom-call(s32[7]{0:T(128)} %stack.74.idx, f32[24,128]{1,0:T(8,128)} %copy-done.18, f32[196,96,128]{2,1,0:T(8,128)} %bitcast.164, f32[98,8,128]{2,1,0:T(8,128)} %copy-done.8, bf16[256,640]{1,0:T(8,128)(2,1)} %get-tuple-element.147.wh, ...), custom_call_target="tpu_custom_call" | custom-call | flops 1387266048 | bytes 3612672 | tf_op jit(solution)/shard_map/lateral/pallas_call | solution.py:161
  117.5 9.0 %sum3.1 = (f32[2,512]{1,0:T(2,128)}, f32[2,256]{1,0:T(2,128)}) custom-call(f32[2,512]{1,0:T(2,128)} %get-tuple-element.146.refs_0_, f32[2,256]{1,0:T(2,128)} %get-tuple-element.148.refs_1_), custom_call_target="tpu_custom_call" | custom-call | tf_op jit(solution)/shard_map/sum3/pallas_call | solution.py:251
  126.4 14.2 %fast4.1 = (f32[98,96,128]{2,1,0:T(8,128)}, f32[196,96,128]{2,1,0:T(8,128)}, f32[2352,512]{1,0:T(8,128)}, f32[2,512]{1,0:T(2,128)}) custom-call(s32[7]{0:T(128)} %stack.74.idx, f32[2,512]{1,0:T(2,128)} %get-tuple-element.150.tot, f32[1,128]{1,0:T(1,128)} %bitcast.233, f32[1,128]{1,0:T(1,128)} %bitcast.232, f32[196,96,128]{2,1,0:T(8,128)} %bitcast.165, ...), custom_call_target="tpu_custom_call" | custom-call | flops 924844032 | bytes 12042240 | tf_op jit(solution)/shard_map/fast4/pallas_call | solution.py:161
  144.4 2.5 fusion.1
  146.9 21.4 %slow1.1 = (f32[1176,256]{1,0:T(8,128)}, f32[1176,1024]{1,0:T(8,128)}, bf16[7,168,1280]{2,1,0:T(8,128)(2,1)}, bf16[7,168,1280]{2,1,0:T(8,128)(2,1)}, f32[7,7,256...) custom-call(s32[7]{0:T(128)} %stack.74.idx, f32[2,256]{1,0:T(2,128)} %get-tuple-element.153.tot.tot_a, ...), custom_call_target="tpu_custom_call" | custom-call | flops 5780275200 | bytes 12531680 | tf_op jit(solution)/shard_map/slow1/pallas_call | solution.py:161
  168.3 12.8 %sum8.1 = (f32[2,1280]{1,0:T(2,128)}, f32[2,512]{1,0:T(2,128)}, f32[7,7,256]{2,1,0:T(8,128)}, f32[7,7,256]{2,1,0:T(8,128)}) custom-call(f32[2,1280]{1,0:T(2,128)} %get-tuple-element.156.refs_0_, f32[2,512]{1,0:T(2,128)} %get-tuple-element.152.refs_1_, f32[7,7,256]{2,1,0:T(8,128)} %get-tuple-element.157.refs_2_, f32[7,7,256]{2,1,0:T(8,128)} %get-tuple-element.158.refs_3_), custom_call_target="tpu_custom_call" | custom-call | tf_op jit(solution)/shard_map/sum8/pallas_call | solution.py:251
  181.1 2.1 fusion.3
  183.2 8.2 %slow2.1 = (bf16[7,168,768]{2,1,0:T(8,128)(2,1)}, bf16[7,168,768]{2,1,0:T(8,128)(2,1)}, f32[1176,256]{1,0:T(8,128)}, f32[2,256]{1,0:T(2,128)}) custom-call(f32[24,256]{1,0:T(8,128)} %pad_maximum_fusion.11.mp, f32[24,256]{1,0:T(8,128)} %pad_maximum_fusion.12.mn, f32[2,1280]{1,0:T(2,128)} %get-tuple-element.159.tot.tot_s.tot_f, ...), custom_call_target="tpu_custom_call" | custom-call | flops 693633024 | bytes 3528000 | tf_op jit(solution)/shard_map/slow2/pallas_call | solution.py:161
  191.3 11.2 %sum9.1.tot.tot_m = f32[2,256]{1,0:T(2,128)} custom-call(f32[2,256]{1,0:T(2,128)} %get-tuple-element.163.refs_0_), custom_call_target="tpu_custom_call" | custom-call | tf_op jit(solution)/shard_map/sum9/pallas_call | solution.py:251
  203.8 2.4 fusion.2
  206.2 7.0 %slow3.1 = (bf16[7,168,256]{2,1,0:T(8,128)(2,1)}, bf16[7,168,256]{2,1,0:T(8,128)(2,1)}, f32[2,1024]{1,0:T(2,128)}) custom-call(f32[2,256]{1,0:T(2,128)} %sum9.1.tot.tot_m, f32[1,256]{1,0:T(1,128)} %reshape.536.gain.gain_m, f32[1,256]{1,0:T(1,128)} %reshape.537.bias.bias_m, f32[1176,256]{1,0:T(8,128)} %get-tuple-element.164.pm, ...), custom_call_target="tpu_custom_call" | custom-call | flops 924844032 | bytes 1204224 | tf_op jit(solution)/shard_map/slow3/pallas_call | solution.py:161
  213.2 10.6 %sum10.1.tot_l = f32[2,1024]{1,0:T(2,128)} custom-call(f32[2,1024]{1,0:T(2,128)} %get-tuple-element.165.refs_0_), custom_call_target="tpu_custom_call" | custom-call | tf_op jit(solution)/shard_map/sum10/pallas_call | solution.py:251
  226.2 13.4 %slow4.1 = (f32[4704,256]{1,0:T(8,128)}, f32[1176,256]{1,0:T(8,128)}, f32[1176,256]{1,0:T(8,128)}, f32[1176,256]{1,0:T(8,128)}, f32[1176,1024]{1,0:T(8,128)}, /*index=5*/f32[4,1024]{1,0:T(4,128)}) custom-call(s32[7]{0:T(128)} %stack.74.idx, f32[2,1024]{1,0:T(2,128)} %sum10.1.tot_l, f32[2,1280]{1,0:T(2,128)} %get-tuple-element.159.tot.tot_s.tot_f, ...), custom_call_target="tpu_custom_call" | custom-call | flops 924844032 | bytes 10235904 | tf_op jit(solution)/shard_map/slow4/pallas_call | solution.py:161
  239.8 3.1 collective-permute-done.7
  244.0 12.0 %sum11.1.back = f32[4,1024]{1,0:T(4,128)} custom-call(f32[4,1024]{1,0:T(4,128)} %get-tuple-element.174.refs_0_), custom_call_target="tpu_custom_call" | custom-call | tf_op jit(solution)/shard_map/sum11/pallas_call | solution.py:251
  256.0 38.2 %slow6.1 = (f32[1176,1280]{1,0:T(8,128)}, f32[4,1280,256]{2,1,0:T(8,128)}) custom-call(f32[2,1280]{1,0:T(2,128)} %get-tuple-element.159.tot.tot_s.tot_f, f32[4,1024]{1,0:T(4,128)} %sum11.1.back, f32[1,1024]{1,0:T(1,128)} %bitcast.223, f32[1176,1024]{1,0:T(8,128)} %get-tuple-element.175.u_ref, f32[1176,1024]{1,0:T(8,128)} %get-tuple-element.168.short, ...), custom_call_target="tpu_custom_call" | custom-call | flops 9248440320 | bytes 16819200 | tf_op jit(solution)/shard_map/slow6/pallas_call | solution.py:161
  294.3 19.2 %slow5.1 = (f32[1176,256]{1,0:T(8,128)}, f32[256,1024]{1,0:T(8,128)}, f32[7,2,7,256]{3,2,1,0:T(8,128)}, f32[7,2,7,256]{3,2,1,0:T(8,128)}, f32[2,256]{1,0:T(2,128)}) custom-call(f32[2,1024]{1,0:T(2,128)} %sum10.1.tot_l, f32[4,1024]{1,0:T(4,128)} %sum11.1.back, f32[1,1024]{1,0:T(1,128)} %bitcast.221, f32[2,256]{1,0:T(2,128)} %sum9.1.tot.tot_m, ...), custom_call_target="tpu_custom_call" | custom-call | flops 2774532096 | bytes 4233600 | tf_op jit(solution)/shard_map/slow5/pallas_call | solution.py:161
  316.7 1.5 collective-permute-start.17
  318.3 14.0 %sum12.1 = (f32[2,256]{1,0:T(2,128)}, f32[7,2,7,256]{3,2,1,0:T(8,128)}, f32[7,2,7,256]{3,2,1,0:T(8,128)}) custom-call(f32[2,256]{1,0:T(2,128)} %get-tuple-element.180.refs_0_, f32[7,2,7,256]{3,2,1,0:T(8,128)} %get-tuple-element.181.refs_1_, f32[7,2,7,256]{3,2,1,0:T(8,128)} %get-tuple-element.182.refs_2_), custom_call_target="tpu_custom_call" | custom-call | tf_op jit(solution)/shard_map/sum12/pallas_call | solution.py:251
  332.3 13.1 %slow7.1 = (f32[1176,256]{1,0:T(8,128)}, f32[256,768]{1,0:T(8,128)}, f32[2,256]{1,0:T(2,128)}) custom-call(f32[24,256]{1,0:T(8,128)} %pad_maximum_fusion.11.mp, f32[24,256]{1,0:T(8,128)} %pad_maximum_fusion.12.mn, f32[2,256]{1,0:T(2,128)} %sum9.1.tot.tot_m, f32[2,256]{1,0:T(2,128)} %get-tuple-element.183.back, f32[1,256]{1,0:T(1,128)} %reshape.536.gain.gain_m, ...), custom_call_target="tpu_custom_call" | custom-call | flops 1387266048 | bytes 3528000 | tf_op jit(solution)/shard_map/slow7/pallas_call | solution.py:161
  345.4 9.8 %sum13.1.back = f32[2,256]{1,0:T(2,128)} custom-call(f32[2,256]{1,0:T(2,128)} %get-tuple-element.189.refs_0_), custom_call_target="tpu_custom_call" | custom-call | tf_op jit(solution)/shard_map/sum13/pallas_call | solution.py:251
  355.2 19.9 %slow8.1 = (f32[4704,256]{1,0:T(8,128)}, f32[1176,256]{1,0:T(8,128)}, f32[1176,256]{1,0:T(8,128)}, f32[1176,256]{1,0:T(8,128)}, f32[1176,256]{1,0:T(8,128)}, /*i...) custom-call(s32[7]{0:T(128)} %stack.74.idx, f32[2,1280]{1,0:T(2,128)} %get-tuple-element.159.tot.tot_s.tot_f, ...), custom_call_target="tpu_custom_call" | custom-call | flops 2312110080 | bytes 11760000 | tf_op jit(solution)/shard_map/slow8/pallas_call | solution.py:161
  375.1 11.0 %sum14.1.back = f32[2,256]{1,0:T(2,128)} custom-call(f32[2,256]{1,0:T(2,128)} %get-tuple-element.191.refs_0_), custom_call_target="tpu_custom_call" | custom-call | tf_op jit(solution)/shard_map/sum14/pallas_call | solution.py:251
  386.1 8.8 %slow9.1 = f32[256,640]{1,0:T(8,128)} custom-call(s32[7]{0:T(128)} %stack.74.idx, f32[24,128]{1,0:T(8,128)} %copy-done.18, f32[2,256]{1,0:T(2,128)} %get-tuple-element.153.tot.tot_a, f32[2,256]{1,0:T(2,128)} %sum14.1.back, f32[1,256]{1,0:T(1,128)} %reshape.532.gain.gain_a, f32[1176,256]{1,0:T(8,128)} %get-tuple-element.216.us, ...), custom_call_target="tpu_custom_call" | custom-call | flops 578027520 | bytes 3528000 | tf_op jit(solution)/shard_map/slow9/pallas_call | solution.py:161
  403.9 1.8 maximum_add_fusion
  410.0 13.2 %fast5.1 = (f32[2352,128]{1,0:T(8,128)}, f32[128,512]{1,0:T(8,128)}, f32[7,2,14,128]{3,2,1,0:T(8,128)}, f32[7,2,14,128]{3,2,1,0:T(8,128)}, f32[2,128]{1,0:T(2,128)}) custom-call(f32[2,512]{1,0:T(2,128)} %get-tuple-element.150.tot, f32[2,512]{1,0:T(2,128)} %get-tuple-element.201.back, f32[1,128]{1,0:T(1,128)} %bitcast.234, f32[2,128]{1,0:T(2,128)} %sum2.1.tot.tot2, ...), custom_call_target="tpu_custom_call" | custom-call | flops 2774532096 | bytes 4233600 | tf_op jit(solution)/shard_map/fast5/pallas_call | solution.py:161
  423.2 1.9 collective-permute-done.8
  425.1 14.8 %sum5.1 = (f32[2,128]{1,0:T(2,128)}, f32[7,2,14,128]{3,2,1,0:T(8,128)}, f32[7,2,14,128]{3,2,1,0:T(8,128)}) custom-call(f32[2,128]{1,0:T(2,128)} %get-tuple-element.204.refs_0_, f32[7,2,14,128]{3,2,1,0:T(8,128)} %get-tuple-element.205.refs_1_, f32[7,2,14,128]{3,2,1,0:T(8,128)} %get-tuple-element.206.refs_2_), custom_call_target="tpu_custom_call" | custom-call | tf_op jit(solution)/shard_map/sum5/pallas_call | solution.py:251
  440.9 9.4 %fast6.1 = (f32[2352,128]{1,0:T(8,128)}, f32[256,128]{1,0:T(8,128)}, f32[2,128]{1,0:T(2,128)}) custom-call(f32[24,128]{1,0:T(8,128)} %copy-done.18, f32[24,128]{1,0:T(8,128)} %copy-done.21, f32[2,128]{1,0:T(2,128)} %sum2.1.tot.tot2, f32[2,128]{1,0:T(2,128)} %get-tuple-element.210.back2, f32[1,128]{1,0:T(1,128)} %tile.37.gain.gain2, ...), custom_call_target="tpu_custom_call" | custom-call | flops 924844032 | bytes 3612672 | tf_op jit(solution)/shard_map/fast6/pallas_call | solution.py:161
  451.5 7.9 %sum6.1.back1 = f32[2,128]{1,0:T(2,128)} custom-call(f32[2,128]{1,0:T(2,128)} %get-tuple-element.215.refs_0_), custom_call_target="tpu_custom_call" | custom-call | tf_op jit(solution)/shard_map/sum6/pallas_call | solution.py:251
  459.6 9.0 %fast7.1 = (f32[2352,128]{1,0:T(8,128)}, f32[512,128]{1,0:T(8,128)}) custom-call(s32[7]{0:T(128)} %stack.74.idx, f32[2,128]{1,0:T(2,128)} %get-tuple-element.140.tot.tot1, f32[2,128]{1,0:T(2,128)} %sum6.1.back1, f32[1,128]{1,0:T(1,128)} %tile.33.gain.gain1, f32[196,96,128]{2,1,0:T(8,128)} %bitcast.167, f32[2352,128]{1,0:T(8,128)} %get-tuple-element.218.u1, ...), custom_call_target="tpu_custom_call" | custom-call | flops 924844032 | bytes 4233600 | tf_op jit(solution)/shard_map/fast7/pallas_call | solution.py:161
  470.0 1.5 collective-permute-start.13
  472.5 57.5 %sum15.1 = (f32[88,128]{1,0:T(8,128)}, f32[8,8,2688]{2,1,0:T(8,128)}) custom-call(f32[88,128]{1,0:T(8,128)} %pad_maximum_fusion.10.x_ref, f32[8,8,2688]{2,1,0:T(8,128)} %bitcast.182), custom_call_target="tpu_custom_call" | custom-call | tf_op jit(solution)/shard_map/sum15/pallas_call | solution.py:320
  530.1 1.4 broadcast_select_fusion.1
  531.5 1.5 pad_maximum_fusion.5.us
  533.6 13.2 %last.1 = (f32[98,96,128]{2,1,0:T(8,128)}, f32[196,96,128]{2,1,0:T(8,128)}) custom-call(s32[7]{0:T(128)} %stack.74.idx, f32[24,128]{1,0:T(8,128)} %copy-done.21, f32[2,256]{1,0:T(2,128)} %get-tuple-element.153.tot.tot_a, f32[2,256]{1,0:T(2,128)} %sum14.1.back, f32[1,256]{1,0:T(1,128)} %reshape.532.gain.gain_a, f32[2352,256]{1,0:T(8,128)} %pad_maximum_fusion.5.us, ...), custom_call_target="tpu_custom_call" | custom-call | flops 1849688064 | bytes 9408000 | tf_op jit(solution)/shard_map/last/pallas_call | solution.py:161
  558.4 2.5 constant_dynamic-update-slice_fusion.5
  565.0 2.4 constant_dynamic-update-slice_fusion.1
  567.4 5.0 constant_dynamic-update-slice_fusion.4
  572.5 3.0 constant_dynamic-update-slice_fusion
  577.4 1.7 copy.180
  (303 shorter events, 65.9 us)
Async XLA Ops:
  7.2 87.9 %all-gather.13.cloned.1.call-start = ((), (), s32[]{:S(2)}) async-start(), calls=%async_computation.6 | async-start | bytes 4190208 | tf_op jit(solution)/shard_map/all_gather | solution.py:794
  10.7 215.5 %all-gather.9.cloned.1.call-start = ((), (), s32[]{:S(2)}) async-start(), calls=%async_computation.2 | async-start | bytes 3612672 | tf_op jit(solution)/shard_map/all_gather | solution.py:894
  10.7 10.0 %copy-start.3 = (f32[1280,256]{1,0:T(8,128)S(1)}, f32[1280,256]{1,0:T(8,128)}, u32[]{:S(2)}) copy-start(f32[1280,256]{1,0:T(8,128)} %param.53) | copy-start | bytes 3932164
  10.7 11.7 %copy-start.25 = (f32[3,32,32]{2,1,0:T(8,128)S(1)}, f32[3,32,32]{2,1,0:T(8,128)}, u32[]{:S(2)}) copy-start(f32[3,32,32]{2,1,0:T(8,128)} %param.35) | copy-start | bytes 36868
  10.7 11.7 %copy-start.31 = (f32[128,32]{0,1:T(8,128)S(1)}, f32[128,32]{0,1:T(8,128)}, u32[]{:S(2)}) copy-start(f32[128,32]{0,1:T(8,128)} %param.32) | copy-start | bytes 49156
  14.1 11.3 %collective-permute-start = (f32[2352,256]{1,0:T(8,128)}, f32[2352,256]{1,0:T(8,128)}, u32[]{:S(2)}, u32[]{:S(2)}) collective-permute-start(f32[2352,256]{1,0:T(8,128)} %constant_dynamic-slice_fusion.27), channel_id=1, source_target_pairs={{0,1},{1,0},{2,3},{3,2},{4,5},{5,4},{6,7},{7,6},{8,9},{9,8},{10,11... | collective-permute-start | bytes 7225352 | tf_op jit(solution)/shard_map/ppermute | solution.py:761
  16.3 91.5 %collective-permute-start.1 = (f32[98,8,128]{2,1,0:T(8,128)}, f32[98,8,128]{2,1,0:T(8,128)S(1)}, u32[]{:S(2)}, u32[]{:S(2)}) collective-permute-start(f32[98,8,128]{2,1,0:T(8,128)} %dynamic-slice_bitcast_fusion.4), channel_id=1, source_target_pairs={{0,4},{4,8},{8,12},{12,16},{16,20},{20,24},{24,28},{1,5},{5,9},{9,... | collective-permute-start | bytes 1204232 | tf_op jit(solution)/shard_map/ppermute | solution.py:830
  20.7 33.7 %collective-permute-start.3 = (f32[1280,256]{1,0:T(8,128)S(1)}, f32[1280,256]{1,0:T(8,128)S(1)}, u32[]{:S(2)}, u32[]{:S(2)}) collective-permute-start(f32[1280,256]{1,0:T(8,128)S(1)} %copy-done.3), channel_id=1, source_target_pairs={{0,2},{2,0},{1,3},{3,1},{4,6},{6,4},{5,7},{7,5},{8,10},{10,8},{9,1... | collective-permute-start | bytes 3932168 | tf_op jit(solution)/shard_map/ppermute | solution.py:771
  56.4 43.3 %collective-permute-start.4 = (f32[2,1280,256]{2,1,0:T(8,128)}, f32[2,1280,256]{2,1,0:T(8,128)}, u32[]{:S(2)}, u32[]{:S(2)}) collective-permute-start(f32[2,1280,256]{2,1,0:T(8,128)} %pad_maximum_fusion.3), channel_id=1, source_target_pairs={{0,1},{1,0},{2,3},{3,2},{4,5},{5,4},{6,7},{7,6},{8,9},{9,8},{10,11... | collective-permute-start | bytes 7864328 | tf_op jit(solution)/shard_map/ppermute | solution.py:887
  56.4 4.8 copy-start.41
  56.4 5.4 copy-start.42
  56.4 7.2 %copy-start.43 = (f32[32]{0:T(128)S(1)}, f32[32]{0:T(128)}, u32[]{:S(2)}) copy-start(f32[32]{0:T(128)} %param.36) | copy-start | bytes 388
  56.4 7.9 %copy-start.44 = (f32[32]{0:T(128)S(1)}, f32[32]{0:T(128)}, u32[]{:S(2)}) copy-start(f32[32]{0:T(128)} %param.37) | copy-start | bytes 388
  56.4 8.4 %copy-start.45 = (s32[24]{0:T(128)S(1)}, s32[24]{0:T(128)}, u32[]{:S(2)}) copy-start(s32[24]{0:T(128)} %param.31) | copy-start | bytes 292
  56.5 10.7 %copy-start.32 = (f32[32,128]{1,0:T(8,128)S(1)}, f32[32,128]{1,0:T(8,128)}, u32[]{:S(2)}) copy-start(f32[32,128]{1,0:T(8,128)} %param.38) | copy-start | bytes 49156
  59.8 34.2 %collective-permute-start.5 = (f32[2352,256]{1,0:T(8,128)}, f32[2352,256]{1,0:T(8,128)S(1)}, u32[]{:S(2)}, u32[]{:S(2)}) collective-permute-start(f32[2352,256]{1,0:T(8,128)} %constant_dynamic-slice_fusion.20), channel_id=1, source_target_pairs={{0,1},{1,0},{2,3},{3,2},{4,5},{5,4},{6,7},{7,6},{8,9},{9,8},{10,11... | collective-permute-start | bytes 7225352 | tf_op jit(solution)/shard_map/ppermute | solution.py:761
  65.1 6.7 %copy-start.18 = (f32[24,128]{1,0:T(8,128)}, f32[24,128]{1,0:T(8,128)S(1)}, u32[]{:S(2)}) copy-start(f32[24,128]{1,0:T(8,128)S(1)} %broadcast_in_dim.36.mp.mask) | copy-start | bytes 36868
  65.8 6.0 %copy-start.21 = (f32[24,128]{1,0:T(8,128)}, f32[24,128]{1,0:T(8,128)S(1)}, u32[]{:S(2)}) copy-start(f32[24,128]{1,0:T(8,128)S(1)} %broadcast_in_dim.37.mn.mask) | copy-start | bytes 36868
  70.4 76.5 %collective-permute-start.2 = (f32[2352,256]{1,0:T(8,128)}, f32[2352,256]{1,0:T(8,128)}, u32[]{:S(2)}, u32[]{:S(2)}) collective-permute-start(f32[2352,256]{1,0:T(8,128)} %pad_maximum_fusion.4), channel_id=1, source_target_pairs={{0,2},{2,0},{1,3},{3,1},{4,6},{6,4},{5,7},{7,5},{8,10},{10,8},{9,1... | collective-permute-start | bytes 7225352 | tf_op jit(solution)/shard_map/ppermute | solution.py:774
  93.9 3.6 copy-start.2
  99.7 2.5 copy-start.6
  99.7 126.5 %all-gather.11.cloned.1.call-start = ((), (), s32[]{:S(2)}) async-start(), calls=%async_computation.3 | async-start | bytes 3612672 | tf_op jit(solution)/shard_map/all_gather | solution.py:894
  140.7 172.8 %all-gather.15.cloned.1.call-start = ((), (), s32[]{:S(2)}) async-start(), calls=%async_computation.7 | async-start | bytes 3612672 | tf_op jit(solution)/shard_map/all_gather | solution.py:973
  239.6 75.2 %all-gather.17.cloned.1.call-start = ((), (), s32[]{:S(2)}) async-start(), calls=%async_computation.8 | async-start | bytes 3612672 | tf_op jit(solution)/shard_map/all_gather | solution.py:973
  239.7 3.2 collective-permute-start.7
  243.9 166.0 %reduce-scatter.5.cloned.1.call-start = ((), (), s32[]{:S(2)}) async-start(), calls=%async_computation.5 | async-start | bytes 1310720 | tf_op jit(solution)/shard_map/reduce_scatter | solution.py:1002
  314.8 95.1 %reduce-scatter.3.cloned.1.call-start = ((), (), s32[]{:S(2)}) async-start(), calls=%async_computation.4 | async-start | bytes 6553600 | tf_op jit(solution)/shard_map/reduce_scatter | solution.py:1005
  314.9 3.3 copy-start.39
  315.6 218.0 %all-reduce.4.cloned.1.call-start = ((), (), s32[]{:S(2)}) async-start(), calls=%async_computation.9 | async-start | bytes 3145728 | tf_op jit(solution)/shard_map/psum | solution.py:1025
  316.7 216.9 %collective-permute-start.17 = (f32[7,14,256]{2,1,0:T(8,128)}, f32[7,14,256]{2,1,0:T(8,128)}, u32[]{:S(2)}, u32[]{:S(2)}) collective-permute-start(f32[7,14,256]{2,1,0:T(8,128)} %get-tuple-element.240), channel_id=1, source_target_pairs={{4,0},{8,4},{12,8},{16,12},{20,16},{24,20},{28,24},{5,1},{9,5},{13... | collective-permute-start | bytes 301064 | tf_op jit(solution)/shard_map/ppermute | solution.py:903
  386.1 8.9 %copy-start.11 = (f32[256,1280]{1,0:T(8,128)S(1)}, f32[256,1280]{1,0:T(8,128)}, u32[]{:S(2)}) copy-start(f32[256,1280]{1,0:T(8,128)} %get-tuple-element.193) | copy-start | bytes 3932164
  386.1 8.8 %copy-start.14 = (f32[256,768]{1,0:T(8,128)S(1)}, f32[256,768]{1,0:T(8,128)}, u32[]{:S(2)}) copy-start(f32[256,768]{1,0:T(8,128)} %get-tuple-element.194) | copy-start | bytes 2359300
  397.3 2.3 copy-start.47
  397.3 5.5 copy-start.27
  398.5 4.3 collective-permute-start.6
  399.6 8.0 %collective-permute-start.15 = (f32[7,7,256]{2,1,0:T(8,128)S(1)}, f32[7,7,256]{2,1,0:T(8,128)S(1)}, u32[]{:S(2)}, u32[]{:S(2)}) collective-permute-start(f32[7,7,256]{2,1,0:T(8,128)S(1)} %copy-done.47), channel_id=1, source_target_pairs={{4,0},{8,4},{12,8},{16,12},{20,16},{24,20},{28,24},{5,1},{9,5},{13... | collective-permute-start | bytes 150536 | tf_op jit(solution)/shard_map/ppermute | solution.py:1027
  400.9 7.1 %collective-permute-start.16 = (f32[7,7,256]{2,1,0:T(8,128)S(1)}, f32[7,7,256]{2,1,0:T(8,128)S(1)}, u32[]{:S(2)}, u32[]{:S(2)}) collective-permute-start(f32[7,7,256]{2,1,0:T(8,128)S(1)} %copy-done.47), channel_id=1, source_target_pairs={{4,2},{6,0},{8,6},{10,4},{12,10},{14,8},{16,14},{18,12},{20,18},{2... | collective-permute-start | bytes 150536 | tf_op jit(solution)/shard_map/ppermute | solution.py:1028
  402.2 156.2 %collective-permute-start.10 = (f32[1176,256]{1,0:T(8,128)}, f32[1176,256]{1,0:T(8,128)}, u32[]{:S(2)}, u32[]{:S(2)}) collective-permute-start(f32[1176,256]{1,0:T(8,128)} %get-tuple-element.223), channel_id=1, source_target_pairs={{0,1},{1,0},{2,3},{3,2},{4,5},{5,4},{6,7},{7,6},{8,9},{9,8},{10,11... | collective-permute-start | bytes 3612680 | tf_op jit(solution)/shard_map/ppermute | solution.py:971
  403.9 4.9 copy-start.7
  406.6 18.5 %collective-permute-start.8 = (f32[64,2688]{1,0:T(8,128)}, f32[64,2688]{1,0:T(8,128)S(1)}, u32[]{:S(2)}, u32[]{:S(2)}) collective-permute-start(f32[64,2688]{1,0:T(8,128)} %slice_bitcast_fusion), channel_id=1, source_target_pairs={{0,2},{2,0},{1,3},{3,1},{4,6},{6,4},{5,7},{7,5},{8,10},{10,8},{9,1... | collective-permute-start | bytes 2064392 | tf_op jit(solution)/shard_map/ppermute | solution.py:1043
  408.8 50.7 %collective-permute-start.9 = (f32[1176,256]{1,0:T(8,128)S(1)}, f32[1176,256]{1,0:T(8,128)}, u32[]{:S(2)}, u32[]{:S(2)}) collective-permute-start(f32[1176,256]{1,0:T(8,128)S(1)} %copy-done.7), channel_id=1, source_target_pairs={{0,2},{2,0},{1,3},{3,1},{4,6},{6,4},{5,7},{7,5},{8,10},{10,8},{9,1... | collective-permute-start | bytes 3612680 | tf_op jit(solution)/shard_map/ppermute | solution.py:1044
  459.5 10.3 %copy-start.20 = (f32[128,512]{1,0:T(8,128)S(1)}, f32[128,512]{1,0:T(8,128)}, u32[]{:S(2)}) copy-start(f32[128,512]{1,0:T(8,128)} %get-tuple-element.203) | copy-start | bytes 786436
  470.0 63.1 %collective-permute-start.13 = (f32[1176,256]{1,0:T(8,128)}, f32[1176,256]{1,0:T(8,128)S(1)}, u32[]{:S(2)}, u32[]{:S(2)}) collective-permute-start(f32[1176,256]{1,0:T(8,128)} %get-tuple-element.232), channel_id=1, source_target_pairs={{0,2},{1,3},{2,0},{3,1},{4,6},{5,7},{6,4},{7,5},{8,10},{9,11},{10,... | collective-permute-start | bytes 3612680 | tf_op jit(solution)/shard_map/ppermute | solution.py:1060
  471.5 62.1 %collective-permute-start.14 = (f32[1176,256]{1,0:T(8,128)}, f32[1176,256]{1,0:T(8,128)}, u32[]{:S(2)}, u32[]{:S(2)}) collective-permute-start(f32[1176,256]{1,0:T(8,128)} %get-tuple-element.234), channel_id=1, source_target_pairs={{0,3},{1,2},{2,1},{3,0},{4,7},{5,6},{6,5},{7,4},{8,11},{9,10},{10,... | collective-permute-start | bytes 3612680 | tf_op jit(solution)/shard_map/ppermute | solution.py:1060
  530.0 37.4 %collective-permute-start.11 = (f32[98,96,128]{2,1,0:T(8,128)}, f32[98,96,128]{2,1,0:T(8,128)}, u32[]{:S(2)}, u32[]{:S(2)}) collective-permute-start(f32[98,96,128]{2,1,0:T(8,128)} %get-tuple-element.227), channel_id=1, source_target_pairs={{0,1},{1,0},{2,3},{3,2},{4,5},{5,4},{6,7},{7,6},{8,9},{9,8},{10,11... | collective-permute-start | bytes 14450696 | tf_op jit(solution)/shard_map/ppermute | solution.py:1113
  533.1 18.0 %collective-permute-start.12 = (f32[1176,256]{1,0:T(8,128)}, f32[1176,256]{1,0:T(8,128)S(1)}, u32[]{:S(2)}, u32[]{:S(2)}) collective-permute-start(f32[1176,256]{1,0:T(8,128)} %get-tuple-element.230), channel_id=1, source_target_pairs={{0,1},{1,0},{2,3},{3,2},{4,5},{5,4},{6,7},{7,6},{8,9},{9,8},{10,11... | collective-permute-start | bytes 3612680 | tf_op jit(solution)/shard_map/ppermute | solution.py:1060
  533.6 13.3 %copy-start.30 = (f32[2,256]{1,0:T(2,128)S(1)}, f32[2,256]{1,0:T(2,128)}, u32[]{:S(2)}) copy-start(f32[2,256]{1,0:T(2,128)} %sum13.1.back) | copy-start | bytes 6148
  533.6 13.9 %copy-start.37 = (f32[2,256]{1,0:T(2,128)S(1)}, f32[2,256]{1,0:T(2,128)}, u32[]{:S(2)}) copy-start(f32[2,256]{1,0:T(2,128)} %get-tuple-element.183.back) | copy-start | bytes 6148
  533.6 15.7 %copy-start.24 = (f32[4,1024]{1,0:T(4,128)S(1)}, f32[4,1024]{1,0:T(4,128)}, u32[]{:S(2)}) copy-start(f32[4,1024]{1,0:T(4,128)} %sum11.1.back) | copy-start | bytes 49156
  546.8 5.4 copy-start.26
  546.8 5.4 copy-start.15
  546.8 6.8 %copy-start.36 = (f32[2,128]{1,0:T(2,128)S(1)}, f32[2,128]{1,0:T(2,128)}, u32[]{:S(2)}) copy-start(f32[2,128]{1,0:T(2,128)} %sum6.1.back1) | copy-start | bytes 3076
  546.8 8.2 %copy-start.38 = (f32[2,128]{1,0:T(2,128)S(1)}, f32[2,128]{1,0:T(2,128)}, u32[]{:S(2)}) copy-start(f32[2,128]{1,0:T(2,128)} %get-tuple-element.210.back2) | copy-start | bytes 3076
  546.9 25.6 %collective-permute-start.18 = (f32[98,96,128]{2,1,0:T(8,128)}, f32[98,96,128]{2,1,0:T(8,128)}, u32[]{:S(2)}, u32[]{:S(2)}) collective-permute-start(f32[98,96,128]{2,1,0:T(8,128)} %get-tuple-element.242), channel_id=1, source_target_pairs={{0,1},{1,0},{2,3},{3,2},{4,5},{5,4},{6,7},{7,6},{8,9},{9,8},{10,11... | collective-permute-start | bytes 14450696 | tf_op jit(solution)/shard_map/ppermute | solution.py:1113
  549.4 26.2 %copy-start.40 = (f32[1,256]{1,0:T(1,128)}, f32[1,256]{1,0:T(1,128)S(1)}, u32[]{:S(2)}) copy-start(f32[1,256]{1,0:T(1,128)S(1)} %constant_dynamic-slice_fusion.12) | copy-start | bytes 3076
  556.7 4.3 copy-start.16
  558.4 3.6 copy-start.17
  558.4 14.0 %slice-start = ((s8[9633792]{0:T(1024)(128)(4,1)}), s8[4194304]{0:T(1024)(128)(4,1)S(1)}, s32[]{:S(2)}) async-start(s8[9633792]{0:T(1024)(128)(4,1)} %bitcast.236), calls=%async_computation.10 | async-start | bytes 8388608
  563.2 9.2 %slice-start.1 = ((s8[9633792]{0:T(1024)(128)(4,1)}), s8[4194304]{0:T(1024)(128)(4,1)S(1)}, s32[]{:S(2)}) async-start(s8[9633792]{0:T(1024)(128)(4,1)} %bitcast.236), calls=%async_computation.11 | async-start | bytes 8388608
  567.4 5.0 slice-start.2
  572.4 3.7 copy-start.19
  572.5 4.9 copy-start.10
  572.5 7.4 %copy-start.1 = (f32[5,128,64]{1,2,0:T(8,128)S(1)}, f32[5,128,64]{1,2,0:T(8,128)}, u32[]{:S(2)}) copy-start(f32[5,128,64]{1,2,0:T(8,128)} %param.41) | copy-start | bytes 491524
  575.5 4.3 copy-start.46
  (14 other events, 23.6 us)
Sparse Core Ops, SparseCore 0:
  11.5 66.9 all-gather.12
  99.8 51.0 all-gather.8
  152.4 37.7 all-gather.10
  239.8 37.5 all-gather.14
  278.7 36.0 all-gather.16
  317.2 24.9 reduce-scatter.4
  344.8 51.4 reduce-scatter.2
  410.1 114.2 all-reduce.3

commit v4 on v3

--- a/solution.py
+++ b/solution.py
@@ -265,7 +265,7 @@
     )(*xs, *rims)
 
 
-def last_sum_kernel(sizes, x_ref, v_ref, o_ref, w_ref, two_src, b1, b2, vb, s1, r1, s2, r2, s3, r3, s4, r4):
+def last_sum_kernel(sizes, x_ref, v_ref, o_ref, w_ref, two_src, b1, b2, vb, s1, r1, s2, r2, s3, r3, s4, r4, s5, r5):
     dps, ys, hs = sizes
     d = lax.axis_index("dp")
     h = lax.axis_index("hh")
@@ -294,7 +294,10 @@
     one.wait_recv()
     acc = x_ref[...] + b1[...]
     two_src[...] = acc
-    two = [send(two_src, b2.at[i - 1], s2.at[i - 1], r2.at[i - 1], {"dp": along(i)}) for i in range(1, dps)]
+    two = [
+        send(two_src.at[along(i)], b2.at[i - 1], s2.at[i - 1], r2.at[i - 1], {"dp": along(i)})
+        for i in range(1, dps)
+    ]
     piece = v_ref[d]
     for i, c in enumerate(out):
         c.wait_recv()
@@ -303,14 +306,18 @@
     back = [
         send(w_ref.at[d], w_ref.at[d], s4.at[i - 1], r4.at[i - 1], {"dp": along(i)}) for i in range(1, dps)
     ]
+    piece = two_src[d]
     for i, c in enumerate(two):
         c.wait_recv()
-        acc = acc + b2[i]
-    o_ref[...] = acc
-    for c in back:
+        piece = piece + b2[i]
+    o_ref[d] = piece
+    last = [
+        send(o_ref.at[d], o_ref.at[d], s5.at[i - 1], r5.at[i - 1], {"dp": along(i)}) for i in range(1, dps)
+    ]
+    for c in back + last:
         c.wait_recv()
     one.wait_send()
-    for c in out + two + back:
+    for c in out + two + back + last:
         c.wait_send()
 
 
@@ -326,10 +333,10 @@
         scratch_shapes=[
             pltpu.VMEM(x.shape, F32),
             pltpu.VMEM(x.shape, F32),
-            pltpu.VMEM((dps - 1,) + x.shape, F32),
+            pltpu.VMEM((dps - 1,) + x.shape[1:], F32),
             pltpu.VMEM((dps - 1,) + v.shape[1:], F32),
             dma, dma,
-        ] + [dma((dps - 1,))] * 6,
+        ] + [dma((dps - 1,))] * 8,
         compiler_params=pltpu.CompilerParams(collective_id=cid, has_side_effects=True),
     )(x, v)
 
@@ -1092,7 +1099,10 @@
     small = jnp.concatenate(
         [expand_small, reduce_small.reshape(32, 128), jnp.stack([tap0, tap1, tap2]).reshape(24, 128)], axis=0
     )
-    small, rest = last_total(small, rest.reshape(dps, -1, rest.shape[1]), 15, sizes)
+    count = small.shape[0]
+    small = jnp.pad(small, ((0, -count % dps), (0, 0)))
+    small, rest = last_total(small.reshape(dps, -1, 128), rest.reshape(dps, -1, rest.shape[1]), 15, sizes)
+    small = small.reshape(-1, 128)[:count]
     rest = rest.reshape(shard_rows, -1)
     lateral_sum = rest[:, 0:taps].reshape(shard_rows, -1, 128).transpose(1, 2, 0)
     reduce_sum = rest[:, taps : taps + joined_width].T

time: 593 us -> 590 us (level)
    unnamed x118 -> x116, local copies, waits for them, and re-layouts: 16 us -> 16 us
  transfers between devices with their start and end apart: 27 -> 27, of which waited for: 5 -> 5; matrix products, arithmetic and copies ran while one was open for 17% -> 17% of each run, Pallas kernels for 71% -> 70%
where the time goes in v4:
time: 590 us; the launch traced here: 587 us
  Pallas kernels  427 us (72%)
  local copies, waits for them, and re-layouts  75.5 us (13%)
  other arithmetic  38.2 us (6%)
  starting transfers between devices  17.4 us (3%)
  between operations  15.3 us (3%)
  waiting for transfers between devices  13.3 us (2%)
    pallas_call x18, Pallas kernels, stepped(): pl.pallas_call(body, name=name, out_shape=[o for o, _ in outs], grid_spec...  239 us
    pallas_call x12, Pallas kernels, total(): pl.pallas_call(functools.partial(sum_kernel, sizes, axes, widths, len(rim...  131 us
    pallas_call x1, Pallas kernels, last_total(): pl.pallas_call(functools.partial(last_sum_kernel, sizes), name='sum%d' %...  56.9 us
    unnamed x116, local copies, waits for them, and re-layouts  16 us
    convert_element_type x9, other arithmetic, weight_split(): return (high.astype(BF16), (w - high).astype(BF16))  15.8 us
  transfers between devices with their start and end apart: 27, of which 5 were waited for; matrix products, arithmetic and copies ran while one was open for 17% of the time, Pallas kernels for 70%

profile of v4, /device:TPU:0, one launch (start us, length us, event | category | flops | bytes accessed | tf_op | source)
XLA Modules:
  0.0 586.7 jit_solution(13015803610610592252)
XLA Ops:
  10.7 3.4 constant_dynamic-slice_fusion.27
  14.6 1.8 dynamic-slice_bitcast_fusion.4
  16.3 4.4 collective-permute-start.1
  20.7 1.6 collective-permute-start.3
  24.1 1.4 constant_dynamic-slice_fusion.28
  25.4 1.4 constant_dynamic-slice_fusion.26
  26.8 1.6 pad_maximum_fusion.4
  29.2 1.7 fusion.6
  30.9 8.0 %fast1.1 = (f32[2352,128]{1,0:T(8,128)}, f32[7,14,128]{2,1,0:T(8,128)}, f32[7,14,128]{2,1,0:T(8,128)}, f32[2,128]{1,0:T(2,128)}) custom-call(s32[7]{0:T(128)} %stack.74.idx, f32[196,96,128]{2,1,0:T(8,128)} %bitcast.158, bf16[512,128]{1,0:T(8,128)(2,1)} %get-tuple-element.346.rh, bf16[512,128]{1,0:T(8,128)(2,1)} %get-tuple-element.345.rl), custom_call_target="tpu_custom_call" | custom-call | flops 924844032 | bytes 3010560 | tf_op jit(solution)/shard_map/fast1/pallas_call | solution.py:161
  38.9 9.9 %sum1.1 = (f32[2,128]{1,0:T(2,128)}, f32[7,14,128]{2,1,0:T(8,128)}, f32[7,14,128]{2,1,0:T(8,128)}) custom-call(f32[2,128]{1,0:T(2,128)} %get-tuple-element.137.refs_0_, f32[7,14,128]{2,1,0:T(8,128)} %get-tuple-element.138.refs_1_, f32[7,14,128]{2,1,0:T(8,128)} %get-tuple-element.139.refs_2_), custom_call_target="tpu_custom_call" | custom-call | tf_op jit(solution)/shard_map/sum1/pallas_call | solution.py:251
  48.8 5.7 collective-permute-done.3
  54.5 1.8 pad_maximum_fusion.3
  56.5 3.3 constant_dynamic-slice_fusion.20
  68.0 2.4 constant_dynamic-slice_fusion.19
  70.4 1.5 collective-permute-start.2
  71.9 7.0 %fast2.1 = (f32[2352,128]{1,0:T(8,128)}, f32[2352,128]{1,0:T(8,128)}, f32[2352,128]{1,0:T(8,128)}, f32[2,128]{1,0:T(2,128)}) custom-call(f32[24,128]{1,0:T(8,128)} %copy-done.18, f32[24,128]{1,0:T(8,128)} %copy-done.21, f32[2,128]{1,0:T(2,128)} %get-tuple-element.140.tot.tot1, f32[1,128]{1,0:T(1,128)} %tile.33.gain.gain1, f32[1,128]{1,0:T(1,128)} %tile.35.bias.bias1, ...), custom_call_target="tpu_custom_call" | custom-call | flops 462422016 | bytes 2408448 | tf_op jit(solution)/shard_map/fast2/pallas_call | solution.py:161
  78.9 8.1 %sum2.1.tot.tot2 = f32[2,128]{1,0:T(2,128)} custom-call(f32[2,128]{1,0:T(2,128)} %get-tuple-element.144.refs_0_), custom_call_target="tpu_custom_call" | custom-call | tf_op jit(solution)/shard_map/sum2/pallas_call | solution.py:251
  87.0 6.9 %fast3.1 = (f32[2352,128]{1,0:T(8,128)}, f32[2,512]{1,0:T(2,128)}) custom-call(f32[2,128]{1,0:T(2,128)} %sum2.1.tot.tot2, f32[1,128]{1,0:T(1,128)} %tile.37.gain.gain2, f32[1,128]{1,0:T(1,128)} %tile.39.bias.bias2, f32[2352,128]{1,0:T(8,128)} %get-tuple-element.145.p2, bf16[128,512]{1,0:T(8,128)(2,1)} %get-tuple-element.344.eh, ...), custom_call_target="tpu_custom_call" | custom-call | flops 924844032 | bytes 1204224 | tf_op jit(solution)/shard_map/fast3/pallas_call | solution.py:161
  95.1 2.3 slice.334
  97.5 2.1 copy.121
  99.7 2.0 fusion.49
  102.8 2.8 fusion
  105.6 2.1 fusion.5
  108.5 8.9 %lateral.1 = (f32[2352,256]{1,0:T(8,128)}, f32[7,14,256]{2,1,0:T(8,128)}, f32[2,256]{1,0:T(2,128)}) custom-call(s32[7]{0:T(128)} %stack.74.idx, f32[24,128]{1,0:T(8,128)} %copy-done.18, f32[196,96,128]{2,1,0:T(8,128)} %bitcast.159, f32[98,8,128]{2,1,0:T(8,128)} %copy-done.8, bf16[256,640]{1,0:T(8,128)(2,1)} %get-tuple-element.147.wh, ...), custom_call_target="tpu_custom_call" | custom-call | flops 1387266048 | bytes 3612672 | tf_op jit(solution)/shard_map/lateral/pallas_call | solution.py:161
  117.4 9.0 %sum3.1 = (f32[2,512]{1,0:T(2,128)}, f32[2,256]{1,0:T(2,128)}) custom-call(f32[2,512]{1,0:T(2,128)} %get-tuple-element.146.refs_0_, f32[2,256]{1,0:T(2,128)} %get-tuple-element.148.refs_1_), custom_call_target="tpu_custom_call" | custom-call | tf_op jit(solution)/shard_map/sum3/pallas_call | solution.py:251
  126.4 14.2 %fast4.1 = (f32[98,96,128]{2,1,0:T(8,128)}, f32[196,96,128]{2,1,0:T(8,128)}, f32[2352,512]{1,0:T(8,128)}, f32[2,512]{1,0:T(2,128)}) custom-call(s32[7]{0:T(128)} %stack.74.idx, f32[2,512]{1,0:T(2,128)} %get-tuple-element.150.tot, f32[1,128]{1,0:T(1,128)} %bitcast.225, f32[1,128]{1,0:T(1,128)} %bitcast.224, f32[196,96,128]{2,1,0:T(8,128)} %bitcast.160, ...), custom_call_target="tpu_custom_call" | custom-call | flops 924844032 | bytes 12042240 | tf_op jit(solution)/shard_map/fast4/pallas_call | solution.py:161
  144.3 2.6 fusion.1
  146.9 21.4 %slow1.1 = (f32[1176,256]{1,0:T(8,128)}, f32[1176,1024]{1,0:T(8,128)}, bf16[7,168,1280]{2,1,0:T(8,128)(2,1)}, bf16[7,168,1280]{2,1,0:T(8,128)(2,1)}, f32[7,7,256...) custom-call(s32[7]{0:T(128)} %stack.74.idx, f32[2,256]{1,0:T(2,128)} %get-tuple-element.153.tot.tot_a, ...), custom_call_target="tpu_custom_call" | custom-call | flops 5780275200 | bytes 12531680 | tf_op jit(solution)/shard_map/slow1/pallas_call | solution.py:161
  168.3 12.8 %sum8.1 = (f32[2,1280]{1,0:T(2,128)}, f32[2,512]{1,0:T(2,128)}, f32[7,7,256]{2,1,0:T(8,128)}, f32[7,7,256]{2,1,0:T(8,128)}) custom-call(f32[2,1280]{1,0:T(2,128)} %get-tuple-element.156.refs_0_, f32[2,512]{1,0:T(2,128)} %get-tuple-element.152.refs_1_, f32[7,7,256]{2,1,0:T(8,128)} %get-tuple-element.157.refs_2_, f32[7,7,256]{2,1,0:T(8,128)} %get-tuple-element.158.refs_3_), custom_call_target="tpu_custom_call" | custom-call | tf_op jit(solution)/shard_map/sum8/pallas_call | solution.py:251
  181.0 2.1 fusion.3
  183.1 8.2 %slow2.1 = (bf16[7,168,768]{2,1,0:T(8,128)(2,1)}, bf16[7,168,768]{2,1,0:T(8,128)(2,1)}, f32[1176,256]{1,0:T(8,128)}, f32[2,256]{1,0:T(2,128)}) custom-call(f32[24,256]{1,0:T(8,128)} %pad_maximum_fusion.11.mp, f32[24,256]{1,0:T(8,128)} %pad_maximum_fusion.12.mn, f32[2,1280]{1,0:T(2,128)} %get-tuple-element.159.tot.tot_s.tot_f, ...), custom_call_target="tpu_custom_call" | custom-call | flops 693633024 | bytes 3528000 | tf_op jit(solution)/shard_map/slow2/pallas_call | solution.py:161
  191.3 11.3 %sum9.1.tot.tot_m = f32[2,256]{1,0:T(2,128)} custom-call(f32[2,256]{1,0:T(2,128)} %get-tuple-element.163.refs_0_), custom_call_target="tpu_custom_call" | custom-call | tf_op jit(solution)/shard_map/sum9/pallas_call | solution.py:251
  203.8 2.4 fusion.2
  206.3 6.9 %slow3.1 = (bf16[7,168,256]{2,1,0:T(8,128)(2,1)}, bf16[7,168,256]{2,1,0:T(8,128)(2,1)}, f32[2,1024]{1,0:T(2,128)}) custom-call(f32[2,256]{1,0:T(2,128)} %sum9.1.tot.tot_m, f32[1,256]{1,0:T(1,128)} %reshape.542.gain.gain_m, f32[1,256]{1,0:T(1,128)} %reshape.543.bias.bias_m, f32[1176,256]{1,0:T(8,128)} %get-tuple-element.164.pm, ...), custom_call_target="tpu_custom_call" | custom-call | flops 924844032 | bytes 1204224 | tf_op jit(solution)/shard_map/slow3/pallas_call | solution.py:161
  213.2 10.6 %sum10.1.tot_l = f32[2,1024]{1,0:T(2,128)} custom-call(f32[2,1024]{1,0:T(2,128)} %get-tuple-element.165.refs_0_), custom_call_target="tpu_custom_call" | custom-call | tf_op jit(solution)/shard_map/sum10/pallas_call | solution.py:251
  226.2 13.4 %slow4.1 = (f32[4704,256]{1,0:T(8,128)}, f32[1176,256]{1,0:T(8,128)}, f32[1176,256]{1,0:T(8,128)}, f32[1176,256]{1,0:T(8,128)}, f32[1176,1024]{1,0:T(8,128)}, /*index=5*/f32[4,1024]{1,0:T(4,128)}) custom-call(s32[7]{0:T(128)} %stack.74.idx, f32[2,1024]{1,0:T(2,128)} %sum10.1.tot_l, f32[2,1280]{1,0:T(2,128)} %get-tuple-element.159.tot.tot_s.tot_f, ...), custom_call_target="tpu_custom_call" | custom-call | flops 924844032 | bytes 10235904 | tf_op jit(solution)/shard_map/slow4/pallas_call | solution.py:161
  239.8 3.1 collective-permute-done.7
  244.0 12.0 %sum11.1.back = f32[4,1024]{1,0:T(4,128)} custom-call(f32[4,1024]{1,0:T(4,128)} %get-tuple-element.174.refs_0_), custom_call_target="tpu_custom_call" | custom-call | tf_op jit(solution)/shard_map/sum11/pallas_call | solution.py:251
  256.1 38.2 %slow6.1 = (f32[1176,1280]{1,0:T(8,128)}, f32[4,1280,256]{2,1,0:T(8,128)}) custom-call(f32[2,1280]{1,0:T(2,128)} %get-tuple-element.159.tot.tot_s.tot_f, f32[4,1024]{1,0:T(4,128)} %sum11.1.back, f32[1,1024]{1,0:T(1,128)} %bitcast.215, f32[1176,1024]{1,0:T(8,128)} %get-tuple-element.175.u_ref, f32[1176,1024]{1,0:T(8,128)} %get-tuple-element.168.short, ...), custom_call_target="tpu_custom_call" | custom-call | flops 9248440320 | bytes 16819200 | tf_op jit(solution)/shard_map/slow6/pallas_call | solution.py:161
  294.3 19.2 %slow5.1 = (f32[1176,256]{1,0:T(8,128)}, f32[256,1024]{1,0:T(8,128)}, f32[7,2,7,256]{3,2,1,0:T(8,128)}, f32[7,2,7,256]{3,2,1,0:T(8,128)}, f32[2,256]{1,0:T(2,128)}) custom-call(f32[2,1024]{1,0:T(2,128)} %sum10.1.tot_l, f32[4,1024]{1,0:T(4,128)} %sum11.1.back, f32[1,1024]{1,0:T(1,128)} %bitcast.213, f32[2,256]{1,0:T(2,128)} %sum9.1.tot.tot_m, ...), custom_call_target="tpu_custom_call" | custom-call | flops 2774532096 | bytes 4233600 | tf_op jit(solution)/shard_map/slow5/pallas_call | solution.py:161
  316.7 1.5 collective-permute-start.17
  318.3 14.0 %sum12.1 = (f32[2,256]{1,0:T(2,128)}, f32[7,2,7,256]{3,2,1,0:T(8,128)}, f32[7,2,7,256]{3,2,1,0:T(8,128)}) custom-call(f32[2,256]{1,0:T(2,128)} %get-tuple-element.180.refs_0_, f32[7,2,7,256]{3,2,1,0:T(8,128)} %get-tuple-element.181.refs_1_, f32[7,2,7,256]{3,2,1,0:T(8,128)} %get-tuple-element.182.refs_2_), custom_call_target="tpu_custom_call" | custom-call | tf_op jit(solution)/shard_map/sum12/pallas_call | solution.py:251
  332.3 13.1 %slow7.1 = (f32[1176,256]{1,0:T(8,128)}, f32[256,768]{1,0:T(8,128)}, f32[2,256]{1,0:T(2,128)}) custom-call(f32[24,256]{1,0:T(8,128)} %pad_maximum_fusion.11.mp, f32[24,256]{1,0:T(8,128)} %pad_maximum_fusion.12.mn, f32[2,256]{1,0:T(2,128)} %sum9.1.tot.tot_m, f32[2,256]{1,0:T(2,128)} %get-tuple-element.183.back, f32[1,256]{1,0:T(1,128)} %reshape.542.gain.gain_m, ...), custom_call_target="tpu_custom_call" | custom-call | flops 1387266048 | bytes 3528000 | tf_op jit(solution)/shard_map/slow7/pallas_call | solution.py:161
  345.4 9.8 %sum13.1.back = f32[2,256]{1,0:T(2,128)} custom-call(f32[2,256]{1,0:T(2,128)} %get-tuple-element.189.refs_0_), custom_call_target="tpu_custom_call" | custom-call | tf_op jit(solution)/shard_map/sum13/pallas_call | solution.py:251
  355.2 19.9 %slow8.1 = (f32[4704,256]{1,0:T(8,128)}, f32[1176,256]{1,0:T(8,128)}, f32[1176,256]{1,0:T(8,128)}, f32[1176,256]{1,0:T(8,128)}, f32[1176,256]{1,0:T(8,128)}, /*i...) custom-call(s32[7]{0:T(128)} %stack.74.idx, f32[2,1280]{1,0:T(2,128)} %get-tuple-element.159.tot.tot_s.tot_f, ...), custom_call_target="tpu_custom_call" | custom-call | flops 2312110080 | bytes 11760000 | tf_op jit(solution)/shard_map/slow8/pallas_call | solution.py:161
  375.2 11.0 %sum14.1.back = f32[2,256]{1,0:T(2,128)} custom-call(f32[2,256]{1,0:T(2,128)} %get-tuple-element.191.refs_0_), custom_call_target="tpu_custom_call" | custom-call | tf_op jit(solution)/shard_map/sum14/pallas_call | solution.py:251
  386.2 8.8 %slow9.1 = f32[256,640]{1,0:T(8,128)} custom-call(s32[7]{0:T(128)} %stack.74.idx, f32[24,128]{1,0:T(8,128)} %copy-done.18, f32[2,256]{1,0:T(2,128)} %get-tuple-element.153.tot.tot_a, f32[2,256]{1,0:T(2,128)} %sum14.1.back, f32[1,256]{1,0:T(1,128)} %reshape.538.gain.gain_a, f32[1176,256]{1,0:T(8,128)} %get-tuple-element.216.us, ...), custom_call_target="tpu_custom_call" | custom-call | flops 578027520 | bytes 3528000 | tf_op jit(solution)/shard_map/slow9/pallas_call | solution.py:161
  404.0 1.8 maximum_add_fusion
  410.1 13.2 %fast5.1 = (f32[2352,128]{1,0:T(8,128)}, f32[128,512]{1,0:T(8,128)}, f32[7,2,14,128]{3,2,1,0:T(8,128)}, f32[7,2,14,128]{3,2,1,0:T(8,128)}, f32[2,128]{1,0:T(2,128)}) custom-call(f32[2,512]{1,0:T(2,128)} %get-tuple-element.150.tot, f32[2,512]{1,0:T(2,128)} %get-tuple-element.201.back, f32[1,128]{1,0:T(1,128)} %bitcast.226, f32[2,128]{1,0:T(2,128)} %sum2.1.tot.tot2, ...), custom_call_target="tpu_custom_call" | custom-call | flops 2774532096 | bytes 4233600 | tf_op jit(solution)/shard_map/fast5/pallas_call | solution.py:161
  423.3 1.9 collective-permute-done.8
  425.2 14.8 %sum5.1 = (f32[2,128]{1,0:T(2,128)}, f32[7,2,14,128]{3,2,1,0:T(8,128)}, f32[7,2,14,128]{3,2,1,0:T(8,128)}) custom-call(f32[2,128]{1,0:T(2,128)} %get-tuple-element.204.refs_0_, f32[7,2,14,128]{3,2,1,0:T(8,128)} %get-tuple-element.205.refs_1_, f32[7,2,14,128]{3,2,1,0:T(8,128)} %get-tuple-element.206.refs_2_), custom_call_target="tpu_custom_call" | custom-call | tf_op jit(solution)/shard_map/sum5/pallas_call | solution.py:251
  440.9 9.4 %fast6.1 = (f32[2352,128]{1,0:T(8,128)}, f32[256,128]{1,0:T(8,128)}, f32[2,128]{1,0:T(2,128)}) custom-call(f32[24,128]{1,0:T(8,128)} %copy-done.18, f32[24,128]{1,0:T(8,128)} %copy-done.21, f32[2,128]{1,0:T(2,128)} %sum2.1.tot.tot2, f32[2,128]{1,0:T(2,128)} %get-tuple-element.210.back2, f32[1,128]{1,0:T(1,128)} %tile.37.gain.gain2, ...), custom_call_target="tpu_custom_call" | custom-call | flops 924844032 | bytes 3612672 | tf_op jit(solution)/shard_map/fast6/pallas_call | solution.py:161
  451.5 7.9 %sum6.1.back1 = f32[2,128]{1,0:T(2,128)} custom-call(f32[2,128]{1,0:T(2,128)} %get-tuple-element.215.refs_0_), custom_call_target="tpu_custom_call" | custom-call | tf_op jit(solution)/shard_map/sum6/pallas_call | solution.py:251
  459.6 9.0 %fast7.1 = (f32[2352,128]{1,0:T(8,128)}, f32[512,128]{1,0:T(8,128)}) custom-call(s32[7]{0:T(128)} %stack.74.idx, f32[2,128]{1,0:T(2,128)} %get-tuple-element.140.tot.tot1, f32[2,128]{1,0:T(2,128)} %sum6.1.back1, f32[1,128]{1,0:T(1,128)} %tile.33.gain.gain1, f32[196,96,128]{2,1,0:T(8,128)} %bitcast.162, f32[2352,128]{1,0:T(8,128)} %get-tuple-element.218.u1, ...), custom_call_target="tpu_custom_call" | custom-call | flops 924844032 | bytes 4233600 | tf_op jit(solution)/shard_map/fast7/pallas_call | solution.py:161
  470.0 1.5 collective-permute-start.13
  472.5 56.9 %sum15.1 = (f32[8,11,128]{2,1,0:T(8,128)}, f32[8,8,2688]{2,1,0:T(8,128)}) custom-call(f32[8,11,128]{2,1,0:T(8,128)} %reshape.554.x_ref, f32[8,8,2688]{2,1,0:T(8,128)} %bitcast.177), custom_call_target="tpu_custom_call" | custom-call | tf_op jit(solution)/shard_map/sum15/pallas_call | solution.py:327
  530.2 1.4 broadcast_select_fusion.1
  531.7 1.5 pad_maximum_fusion.5.us
  533.8 13.1 %last.1 = (f32[98,96,128]{2,1,0:T(8,128)}, f32[196,96,128]{2,1,0:T(8,128)}) custom-call(s32[7]{0:T(128)} %stack.74.idx, f32[24,128]{1,0:T(8,128)} %copy-done.21, f32[2,256]{1,0:T(2,128)} %get-tuple-element.153.tot.tot_a, f32[2,256]{1,0:T(2,128)} %sum14.1.back, f32[1,256]{1,0:T(1,128)} %reshape.538.gain.gain_a, f32[2352,256]{1,0:T(8,128)} %pad_maximum_fusion.5.us, ...), custom_call_target="tpu_custom_call" | custom-call | flops 1849688064 | bytes 9408000 | tf_op jit(solution)/shard_map/last/pallas_call | solution.py:161
  558.5 2.5 constant_dynamic-update-slice_fusion.5
  565.1 2.4 constant_dynamic-update-slice_fusion.1
  567.5 5.0 constant_dynamic-update-slice_fusion.4
  572.5 3.0 constant_dynamic-update-slice_fusion
  577.5 1.7 copy.163
  (302 shorter events, 66.7 us)
Async XLA Ops:
  7.2 87.9 %all-gather.13.cloned.1.call-start = ((), (), s32[]{:S(2)}) async-start(), calls=%async_computation.6 | async-start | bytes 4190208 | tf_op jit(solution)/shard_map/all_gather | solution.py:801
  10.7 215.5 %all-gather.9.cloned.1.call-start = ((), (), s32[]{:S(2)}) async-start(), calls=%async_computation.2 | async-start | bytes 3612672 | tf_op jit(solution)/shard_map/all_gather | solution.py:901
  10.7 10.0 %copy-start.3 = (f32[1280,256]{1,0:T(8,128)S(1)}, f32[1280,256]{1,0:T(8,128)}, u32[]{:S(2)}) copy-start(f32[1280,256]{1,0:T(8,128)} %param.53) | copy-start | bytes 3932164
  10.7 11.7 %copy-start.25 = (f32[3,32,32]{2,1,0:T(8,128)S(1)}, f32[3,32,32]{2,1,0:T(8,128)}, u32[]{:S(2)}) copy-start(f32[3,32,32]{2,1,0:T(8,128)} %param.35) | copy-start | bytes 36868
  10.7 11.7 %copy-start.30 = (f32[128,32]{0,1:T(8,128)S(1)}, f32[128,32]{0,1:T(8,128)}, u32[]{:S(2)}) copy-start(f32[128,32]{0,1:T(8,128)} %param.32) | copy-start | bytes 49156
  14.1 11.3 %collective-permute-start = (f32[2352,256]{1,0:T(8,128)}, f32[2352,256]{1,0:T(8,128)}, u32[]{:S(2)}, u32[]{:S(2)}) collective-permute-start(f32[2352,256]{1,0:T(8,128)} %constant_dynamic-slice_fusion.27), channel_id=1, source_target_pairs={{0,1},{1,0},{2,3},{3,2},{4,5},{5,4},{6,7},{7,6},{8,9},{9,8},{10,11... | collective-permute-start | bytes 7225352 | tf_op jit(solution)/shard_map/ppermute | solution.py:768
  16.3 91.4 %collective-permute-start.1 = (f32[98,8,128]{2,1,0:T(8,128)}, f32[98,8,128]{2,1,0:T(8,128)S(1)}, u32[]{:S(2)}, u32[]{:S(2)}) collective-permute-start(f32[98,8,128]{2,1,0:T(8,128)} %dynamic-slice_bitcast_fusion.4), channel_id=1, source_target_pairs={{0,4},{4,8},{8,12},{12,16},{16,20},{20,24},{24,28},{1,5},{5,9},{9,... | collective-permute-start | bytes 1204232 | tf_op jit(solution)/shard_map/ppermute | solution.py:837
  20.7 33.7 %collective-permute-start.3 = (f32[1280,256]{1,0:T(8,128)S(1)}, f32[1280,256]{1,0:T(8,128)S(1)}, u32[]{:S(2)}, u32[]{:S(2)}) collective-permute-start(f32[1280,256]{1,0:T(8,128)S(1)} %copy-done.3), channel_id=1, source_target_pairs={{0,2},{2,0},{1,3},{3,1},{4,6},{6,4},{5,7},{7,5},{8,10},{10,8},{9,1... | collective-permute-start | bytes 3932168 | tf_op jit(solution)/shard_map/ppermute | solution.py:778
  56.4 43.3 %collective-permute-start.4 = (f32[2,1280,256]{2,1,0:T(8,128)}, f32[2,1280,256]{2,1,0:T(8,128)}, u32[]{:S(2)}, u32[]{:S(2)}) collective-permute-start(f32[2,1280,256]{2,1,0:T(8,128)} %pad_maximum_fusion.3), channel_id=1, source_target_pairs={{0,1},{1,0},{2,3},{3,2},{4,5},{5,4},{6,7},{7,6},{8,9},{9,8},{10,11... | collective-permute-start | bytes 7864328 | tf_op jit(solution)/shard_map/ppermute | solution.py:894
  56.4 4.8 copy-start.40
  56.4 5.4 copy-start.41
  56.4 7.2 %copy-start.42 = (f32[32]{0:T(128)S(1)}, f32[32]{0:T(128)}, u32[]{:S(2)}) copy-start(f32[32]{0:T(128)} %param.36) | copy-start | bytes 388
  56.4 7.9 %copy-start.43 = (f32[32]{0:T(128)S(1)}, f32[32]{0:T(128)}, u32[]{:S(2)}) copy-start(f32[32]{0:T(128)} %param.37) | copy-start | bytes 388
  56.4 8.4 %copy-start.44 = (s32[24]{0:T(128)S(1)}, s32[24]{0:T(128)}, u32[]{:S(2)}) copy-start(s32[24]{0:T(128)} %param.31) | copy-start | bytes 292
  56.5 10.7 %copy-start.31 = (f32[32,128]{1,0:T(8,128)S(1)}, f32[32,128]{1,0:T(8,128)}, u32[]{:S(2)}) copy-start(f32[32,128]{1,0:T(8,128)} %param.38) | copy-start | bytes 49156
  59.8 34.1 %collective-permute-start.5 = (f32[2352,256]{1,0:T(8,128)}, f32[2352,256]{1,0:T(8,128)S(1)}, u32[]{:S(2)}, u32[]{:S(2)}) collective-permute-start(f32[2352,256]{1,0:T(8,128)} %constant_dynamic-slice_fusion.20), channel_id=1, source_target_pairs={{0,1},{1,0},{2,3},{3,2},{4,5},{5,4},{6,7},{7,6},{8,9},{9,8},{10,11... | collective-permute-start | bytes 7225352 | tf_op jit(solution)/shard_map/ppermute | solution.py:768
  65.1 6.7 %copy-start.18 = (f32[24,128]{1,0:T(8,128)}, f32[24,128]{1,0:T(8,128)S(1)}, u32[]{:S(2)}) copy-start(f32[24,128]{1,0:T(8,128)S(1)} %broadcast_in_dim.36.mp.mask) | copy-start | bytes 36868
  65.8 6.1 %copy-start.21 = (f32[24,128]{1,0:T(8,128)}, f32[24,128]{1,0:T(8,128)S(1)}, u32[]{:S(2)}) copy-start(f32[24,128]{1,0:T(8,128)S(1)} %broadcast_in_dim.37.mn.mask) | copy-start | bytes 36868
  70.4 76.5 %collective-permute-start.2 = (f32[2352,256]{1,0:T(8,128)}, f32[2352,256]{1,0:T(8,128)}, u32[]{:S(2)}, u32[]{:S(2)}) collective-permute-start(f32[2352,256]{1,0:T(8,128)} %pad_maximum_fusion.4), channel_id=1, source_target_pairs={{0,2},{2,0},{1,3},{3,1},{4,6},{6,4},{5,7},{7,5},{8,10},{10,8},{9,1... | collective-permute-start | bytes 7225352 | tf_op jit(solution)/shard_map/ppermute | solution.py:781
  93.9 3.6 copy-start.2
  99.6 2.5 copy-start.6
  99.6 126.5 %all-gather.11.cloned.1.call-start = ((), (), s32[]{:S(2)}) async-start(), calls=%async_computation.3 | async-start | bytes 3612672 | tf_op jit(solution)/shard_map/all_gather | solution.py:901
  140.6 172.9 %all-gather.15.cloned.1.call-start = ((), (), s32[]{:S(2)}) async-start(), calls=%async_computation.7 | async-start | bytes 3612672 | tf_op jit(solution)/shard_map/all_gather | solution.py:980
  239.7 75.2 %all-gather.17.cloned.1.call-start = ((), (), s32[]{:S(2)}) async-start(), calls=%async_computation.8 | async-start | bytes 3612672 | tf_op jit(solution)/shard_map/all_gather | solution.py:980
  239.7 3.2 collective-permute-start.7
  244.0 166.1 %reduce-scatter.5.cloned.1.call-start = ((), (), s32[]{:S(2)}) async-start(), calls=%async_computation.5 | async-start | bytes 1310720 | tf_op jit(solution)/shard_map/reduce_scatter | solution.py:1009
  314.9 95.1 %reduce-scatter.3.cloned.1.call-start = ((), (), s32[]{:S(2)}) async-start(), calls=%async_computation.4 | async-start | bytes 6553600 | tf_op jit(solution)/shard_map/reduce_scatter | solution.py:1012
  315.0 3.3 copy-start.38
  315.6 218.1 %all-reduce.4.cloned.1.call-start = ((), (), s32[]{:S(2)}) async-start(), calls=%async_computation.9 | async-start | bytes 3145728 | tf_op jit(solution)/shard_map/psum | solution.py:1032
  316.7 217.0 %collective-permute-start.17 = (f32[7,14,256]{2,1,0:T(8,128)}, f32[7,14,256]{2,1,0:T(8,128)}, u32[]{:S(2)}, u32[]{:S(2)}) collective-permute-start(f32[7,14,256]{2,1,0:T(8,128)} %get-tuple-element.240), channel_id=1, source_target_pairs={{4,0},{8,4},{12,8},{16,12},{20,16},{24,20},{28,24},{5,1},{9,5},{13... | collective-permute-start | bytes 301064 | tf_op jit(solution)/shard_map/ppermute | solution.py:910
  386.2 8.9 %copy-start.11 = (f32[256,1280]{1,0:T(8,128)S(1)}, f32[256,1280]{1,0:T(8,128)}, u32[]{:S(2)}) copy-start(f32[256,1280]{1,0:T(8,128)} %get-tuple-element.193) | copy-start | bytes 3932164
  386.2 8.8 %copy-start.14 = (f32[256,768]{1,0:T(8,128)S(1)}, f32[256,768]{1,0:T(8,128)}, u32[]{:S(2)}) copy-start(f32[256,768]{1,0:T(8,128)} %get-tuple-element.194) | copy-start | bytes 2359300
  397.3 2.3 copy-start.23
  397.3 2.3 copy-start.46
  397.4 5.5 copy-start.26
  398.5 4.3 collective-permute-start.6
  399.7 8.0 %collective-permute-start.15 = (f32[7,7,256]{2,1,0:T(8,128)S(1)}, f32[7,7,256]{2,1,0:T(8,128)S(1)}, u32[]{:S(2)}, u32[]{:S(2)}) collective-permute-start(f32[7,7,256]{2,1,0:T(8,128)S(1)} %copy-done.46), channel_id=1, source_target_pairs={{4,0},{8,4},{12,8},{16,12},{20,16},{24,20},{28,24},{5,1},{9,5},{13... | collective-permute-start | bytes 150536 | tf_op jit(solution)/shard_map/ppermute | solution.py:1034
  401.0 7.1 %collective-permute-start.16 = (f32[7,7,256]{2,1,0:T(8,128)S(1)}, f32[7,7,256]{2,1,0:T(8,128)S(1)}, u32[]{:S(2)}, u32[]{:S(2)}) collective-permute-start(f32[7,7,256]{2,1,0:T(8,128)S(1)} %copy-done.46), channel_id=1, source_target_pairs={{4,2},{6,0},{8,6},{10,4},{12,10},{14,8},{16,14},{18,12},{20,18},{2... | collective-permute-start | bytes 150536 | tf_op jit(solution)/shard_map/ppermute | solution.py:1035
  402.3 156.2 %collective-permute-start.10 = (f32[1176,256]{1,0:T(8,128)}, f32[1176,256]{1,0:T(8,128)}, u32[]{:S(2)}, u32[]{:S(2)}) collective-permute-start(f32[1176,256]{1,0:T(8,128)} %get-tuple-element.223), channel_id=1, source_target_pairs={{0,1},{1,0},{2,3},{3,2},{4,5},{5,4},{6,7},{7,6},{8,9},{9,8},{10,11... | collective-permute-start | bytes 3612680 | tf_op jit(solution)/shard_map/ppermute | solution.py:978
  403.9 4.9 copy-start.7
  406.7 18.5 %collective-permute-start.8 = (f32[64,2688]{1,0:T(8,128)}, f32[64,2688]{1,0:T(8,128)S(1)}, u32[]{:S(2)}, u32[]{:S(2)}) collective-permute-start(f32[64,2688]{1,0:T(8,128)} %slice_bitcast_fusion), channel_id=1, source_target_pairs={{0,2},{2,0},{1,3},{3,1},{4,6},{6,4},{5,7},{7,5},{8,10},{10,8},{9,1... | collective-permute-start | bytes 2064392 | tf_op jit(solution)/shard_map/ppermute | solution.py:1050
  408.8 50.7 %collective-permute-start.9 = (f32[1176,256]{1,0:T(8,128)S(1)}, f32[1176,256]{1,0:T(8,128)}, u32[]{:S(2)}, u32[]{:S(2)}) collective-permute-start(f32[1176,256]{1,0:T(8,128)S(1)} %copy-done.7), channel_id=1, source_target_pairs={{0,2},{2,0},{1,3},{3,1},{4,6},{6,4},{5,7},{7,5},{8,10},{10,8},{9,1... | collective-permute-start | bytes 3612680 | tf_op jit(solution)/shard_map/ppermute | solution.py:1051
  459.5 10.3 %copy-start.20 = (f32[128,512]{1,0:T(8,128)S(1)}, f32[128,512]{1,0:T(8,128)}, u32[]{:S(2)}) copy-start(f32[128,512]{1,0:T(8,128)} %get-tuple-element.203) | copy-start | bytes 786436
  470.0 63.2 %collective-permute-start.13 = (f32[1176,256]{1,0:T(8,128)}, f32[1176,256]{1,0:T(8,128)S(1)}, u32[]{:S(2)}, u32[]{:S(2)}) collective-permute-start(f32[1176,256]{1,0:T(8,128)} %get-tuple-element.232), channel_id=1, source_target_pairs={{0,2},{1,3},{2,0},{3,1},{4,6},{5,7},{6,4},{7,5},{8,10},{9,11},{10,... | collective-permute-start | bytes 3612680 | tf_op jit(solution)/shard_map/ppermute | solution.py:1067
  471.5 62.2 %collective-permute-start.14 = (f32[1176,256]{1,0:T(8,128)}, f32[1176,256]{1,0:T(8,128)}, u32[]{:S(2)}, u32[]{:S(2)}) collective-permute-start(f32[1176,256]{1,0:T(8,128)} %get-tuple-element.234), channel_id=1, source_target_pairs={{0,3},{1,2},{2,1},{3,0},{4,7},{5,6},{6,5},{7,4},{8,11},{9,10},{10,... | collective-permute-start | bytes 3612680 | tf_op jit(solution)/shard_map/ppermute | solution.py:1067
  530.2 37.2 %collective-permute-start.11 = (f32[98,96,128]{2,1,0:T(8,128)}, f32[98,96,128]{2,1,0:T(8,128)}, u32[]{:S(2)}, u32[]{:S(2)}) collective-permute-start(f32[98,96,128]{2,1,0:T(8,128)} %get-tuple-element.227), channel_id=1, source_target_pairs={{0,1},{1,0},{2,3},{3,2},{4,5},{5,4},{6,7},{7,6},{8,9},{9,8},{10,11... | collective-permute-start | bytes 14450696 | tf_op jit(solution)/shard_map/ppermute | solution.py:1123
  533.2 18.0 %collective-permute-start.12 = (f32[1176,256]{1,0:T(8,128)}, f32[1176,256]{1,0:T(8,128)S(1)}, u32[]{:S(2)}, u32[]{:S(2)}) collective-permute-start(f32[1176,256]{1,0:T(8,128)} %get-tuple-element.230), channel_id=1, source_target_pairs={{0,1},{1,0},{2,3},{3,2},{4,5},{5,4},{6,7},{7,6},{8,9},{9,8},{10,11... | collective-permute-start | bytes 3612680 | tf_op jit(solution)/shard_map/ppermute | solution.py:1067
  533.7 13.3 %copy-start.29 = (f32[2,256]{1,0:T(2,128)S(1)}, f32[2,256]{1,0:T(2,128)}, u32[]{:S(2)}) copy-start(f32[2,256]{1,0:T(2,128)} %sum13.1.back) | copy-start | bytes 6148
  533.7 13.9 %copy-start.36 = (f32[2,256]{1,0:T(2,128)S(1)}, f32[2,256]{1,0:T(2,128)}, u32[]{:S(2)}) copy-start(f32[2,256]{1,0:T(2,128)} %get-tuple-element.183.back) | copy-start | bytes 6148
  533.7 15.6 %copy-start.24 = (f32[4,1024]{1,0:T(4,128)S(1)}, f32[4,1024]{1,0:T(4,128)}, u32[]{:S(2)}) copy-start(f32[4,1024]{1,0:T(4,128)} %sum11.1.back) | copy-start | bytes 49156
  546.9 5.4 copy-start.15
  546.9 6.8 %copy-start.35 = (f32[2,128]{1,0:T(2,128)S(1)}, f32[2,128]{1,0:T(2,128)}, u32[]{:S(2)}) copy-start(f32[2,128]{1,0:T(2,128)} %sum6.1.back1) | copy-start | bytes 3076
  546.9 8.2 %copy-start.37 = (f32[2,128]{1,0:T(2,128)S(1)}, f32[2,128]{1,0:T(2,128)}, u32[]{:S(2)}) copy-start(f32[2,128]{1,0:T(2,128)} %get-tuple-element.210.back2) | copy-start | bytes 3076
  546.9 25.6 %collective-permute-start.18 = (f32[98,96,128]{2,1,0:T(8,128)}, f32[98,96,128]{2,1,0:T(8,128)}, u32[]{:S(2)}, u32[]{:S(2)}) collective-permute-start(f32[98,96,128]{2,1,0:T(8,128)} %get-tuple-element.242), channel_id=1, source_target_pairs={{0,1},{1,0},{2,3},{3,2},{4,5},{5,4},{6,7},{7,6},{8,9},{9,8},{10,11... | collective-permute-start | bytes 14450696 | tf_op jit(solution)/shard_map/ppermute | solution.py:1123
  549.4 26.2 %copy-start.39 = (f32[1,256]{1,0:T(1,128)}, f32[1,256]{1,0:T(1,128)S(1)}, u32[]{:S(2)}) copy-start(f32[1,256]{1,0:T(1,128)S(1)} %constant_dynamic-slice_fusion.12) | copy-start | bytes 3076
  556.7 4.3 copy-start.16
  558.5 3.6 copy-start.17
  558.5 14.0 %slice-start = ((s8[9633792]{0:T(1024)(128)(4,1)}), s8[4194304]{0:T(1024)(128)(4,1)S(1)}, s32[]{:S(2)}) async-start(s8[9633792]{0:T(1024)(128)(4,1)} %bitcast.228), calls=%async_computation.10 | async-start | bytes 8388608
  563.2 9.2 %slice-start.1 = ((s8[9633792]{0:T(1024)(128)(4,1)}), s8[4194304]{0:T(1024)(128)(4,1)S(1)}, s32[]{:S(2)}) async-start(s8[9633792]{0:T(1024)(128)(4,1)} %bitcast.228), calls=%async_computation.11 | async-start | bytes 8388608
  567.5 5.0 slice-start.2
  572.5 3.7 copy-start.19
  572.5 4.9 copy-start.10
  572.5 7.4 %copy-start.1 = (f32[5,128,64]{1,2,0:T(8,128)S(1)}, f32[5,128,64]{1,2,0:T(8,128)}, u32[]{:S(2)}) copy-start(f32[5,128,64]{1,2,0:T(8,128)} %param.41) | copy-start | bytes 491524
  575.6 4.3 copy-start.45
  (13 other events, 21.3 us)
Sparse Core Ops, SparseCore 0:
  11.5 66.9 all-gather.12
  99.7 51.0 all-gather.8
  152.4 37.7 all-gather.10
  239.8 37.5 all-gather.14
  278.8 36.0 all-gather.16
  317.2 24.9 reduce-scatter.4
  344.9 51.4 reduce-scatter.2
  410.2 111.4 all-reduce.3
